TPU v7x, 1024 devices: a whole 8x8x8 slice. The times are simulated.
1024 devices in a mesh: section: 8 (over y_hi, core), tensor: 128 (over y_lo, x, z).
Axes of the slice: x: 8, y: 8 (y_hi: 4, y_lo: 2; y = y_hi * 2 + y_lo), z: 8, core: 2. Of those that a mesh axis runs over, the one named last changes fastest.
Arguments:
- acts: bfloat16 [8, 512, 4096], P('section', 'tensor'), may hold values from -6 to 6
- norm_gain: float32 [8, 4096], P('section'), may hold values from 0.1 to 1.9
- gate_w: bfloat16 [8, 128, 1024, 512], P('section', 'tensor'), may hold values from -0.09375 to 0.09375
- up_w: bfloat16 [8, 128, 1024, 512], P('section', 'tensor'), may hold values from -0.09375 to 0.09375
- down_w: bfloat16 [8, 128, 512, 1024], P('section', 'tensor'), may hold values from -0.046875 to 0.046875
Outputs:
- received: bfloat16 [8, 512, 4096], P('section', 'tensor')
All inputs are finite; a program needn't handle non-finite values.
Results may differ from a plain program's by a relative error of at most 0.0051.
Values may be sent and summed in bfloat16 or wider, within the bound.
No kernel may reach another device: no remote copies, remote signals or barrier semaphores. Data moves between devices by JAX's collectives and lax.ppermute only.
A program may use at most 32 MiB of HBM per device.

v0:
```python
import jax
import jax.numpy as jnp
from jax import lax
from jax.sharding import PartitionSpec as P


def swapped(block, axis, distance):
    count = lax.axis_size(axis)
    route = []
    for low in range(count):
        high = low | 1 << distance
        if high != low and high < count:
            route += [(low, high), (high, low)]
    return lax.ppermute(block, axis, route)


def passed_along(value, axis, steps):
    count = lax.axis_size(axis)
    first, last = (max(0, -steps), min(count, count - steps))
    return lax.ppermute(value, axis, [(source, source + steps) for source in range(first, last)])


def bit_of(position, level):
    return position // 2**level % 2


def ordered(own_part, partner, upper_bit, dimension):
    leading = jnp.where(upper_bit == 0, own_part, partner)
    trailing = jnp.where(upper_bit == 0, partner, own_part)
    return jnp.concatenate([leading, trailing], axis=dimension)


def halves(values, upper_bit, dimension):
    middle = values.shape[dimension] // 2
    lower = lax.slice_in_dim(values, 0, middle, axis=dimension)
    higher = lax.slice_in_dim(values, middle, 2 * middle, axis=dimension)
    return (jnp.where(upper_bit == 0, lower, higher), jnp.where(upper_bit == 0, higher, lower))


def unreverse(values, depth, dimension):
    extent = values.shape
    inner = extent[dimension] // 2**depth
    pieces_shape = extent[:dimension] + (2,) * depth + (inner,) + extent[dimension + 1 :]
    permutation = (
        list(range(dimension))
        + [dimension + depth - 1 - level for level in range(depth)]
        + list(range(dimension + depth, len(pieces_shape)))
    )
    return jnp.transpose(values.reshape(pieces_shape), permutation).reshape(extent)


def trade_values(values, level):
    return swapped(values, "tensor", level)


def trade_sums(values, level):
    return swapped(values, "tensor", level)


def per_device(acts, norm_gain, gate_w, up_w, down_w):
    inputs = acts[0].astype(jnp.float32)
    scale = lax.rsqrt(jnp.mean(inputs * inputs, axis=-1, keepdims=True) + 1e-05)
    normed = (inputs * scale * norm_gain[0][None, :]).astype(jnp.bfloat16)
    gate_local = gate_w[0, 0]
    up_local = up_w[0, 0]
    down_local = down_w[0, 0]
    groups_a = normed.shape[1] // gate_local.shape[0]
    bits_a = groups_a.bit_length() - 1
    bits_b = (lax.axis_size("tensor") // groups_a).bit_length() - 1
    position = lax.axis_index("tensor")
    columns = normed
    for level in reversed(range(bits_a)):
        upper_bit = bit_of(position, level)
        kept, sent = halves(columns, upper_bit, 1)
        columns = ordered(kept, trade_values(sent, level), upper_bit, 0)
    columns = unreverse(columns, bits_a, 0)
    for level in range(bits_a, bits_a + bits_b):
        columns = ordered(columns, trade_values(columns, level), bit_of(position, level), 0)
    gate = jnp.dot(columns, gate_local, preferred_element_type=jnp.float32)
    up_part = jnp.dot(columns, up_local, preferred_element_type=jnp.float32)
    both = jnp.stack([gate, up_part])
    for level in range(bits_a):
        both = both + trade_sums(both, level)
    hidden = (jax.nn.silu(both[0]) * both[1]).astype(jnp.bfloat16)
    partial_rows = jnp.dot(hidden, down_local, preferred_element_type=jnp.float32)
    for level in reversed(range(bits_a, bits_a + bits_b)):
        upper_bit = bit_of(position, level)
        kept, sent = halves(partial_rows, upper_bit, 0)
        partial_rows = kept + trade_sums(sent, level)
    for level in reversed(range(bits_a)):
        upper_bit = bit_of(position, level)
        kept, sent = halves(partial_rows, upper_bit, 0)
        partial_rows = ordered(kept, trade_sums(sent, level), upper_bit, 1)
    summed = unreverse(partial_rows, bits_a, 1)
    block = (inputs + summed).astype(jnp.bfloat16)
    arrived = passed_along(block, "section", 1)
    return arrived[None]


def solution(mesh):
    in_specs = (
        P("section", "tensor", None),
        P("section", None),
        P("section", "tensor", None, None),
        P("section", "tensor", None, None),
        P("section", "tensor", None, None),
    )
    out_specs = P("section", "tensor", None)
    return jax.shard_map(
        per_device, mesh=mesh, in_specs=in_specs, out_specs=out_specs, check_vma=False
    )
```

profile of v0, /device:TPU:1, one launch (start us, length us, event | category | flops | bytes accessed | tf_op | source)
XLA Modules:
  0.0 309.5 jit_solution(7007595477928341160)
XLA Ops:
  1.9 8.5 %collective-permute-start = (bf16[4,2048]{1,0:T(4,128)(2,1)S(1)}, bf16[4,2048]{1,0:T(4,128)(2,1)S(1)}, u32[]{:S(2)}, u32[]{:S(2)}) collective-permute-start(bf16[4,2048]{1,0:T(4,128)(2,1)S(1)} %broadcast_select_fusion.12), channel_id=1, source_target_pairs={{0,2},{2,0},{1,3},{3,1},{4,6},{6,4},{5,7},{7,5},{8,10},{10,8},{9,1... | collective-permute-start | bytes 49160 | tf_op jit(solution)/shard_map/ppermute | solution.py:14
  11.5 4.9 %collective-permute-start.1 = (bf16[8,1024]{1,0:T(8,128)(2,1)S(1)}, bf16[8,1024]{1,0:T(8,128)(2,1)S(1)}, u32[]{:S(2)}, u32[]{:S(2)}) collective-permute-start(bf16[8,1024]{1,0:T(8,128)(2,1)S(1)} %broadcast_select_fusion.16), channel_id=1, source_target_pairs={{0,1},{1,0},{2,3},{3,2},{4,5},{5,4},{6,7},{7,6},{8,9},{9,8},{10,11... | collective-permute-start | bytes 49160 | tf_op jit(solution)/shard_map/ppermute | solution.py:14
  16.4 1.1 collective-permute-done.1
  17.7 11.6 %collective-permute-start.2 = (bf16[16,1024]{1,0:T(8,128)(2,1)S(1)}, bf16[16,1024]{1,0:T(8,128)(2,1)S(1)}, u32[]{:S(2)}, u32[]{:S(2)}) collective-permute-start(bf16[16,1024]{1,0:T(8,128)(2,1)S(1)} %reshape.24), channel_id=1, source_target_pairs={{0,4},{4,0},{1,5},{5,1},{2,6},{6,2},{3,7},{7,3},{8,12},{12,8},{9,1... | collective-permute-start | bytes 98312 | tf_op jit(solution)/shard_map/ppermute | solution.py:14
  29.3 1.3 collective-permute-done.2
  30.6 3.1 %collective-permute-start.3 = (bf16[32,1024]{1,0:T(8,128)(2,1)S(1)}, bf16[32,1024]{1,0:T(8,128)(2,1)S(1)}, u32[]{:S(2)}, u32[]{:S(2)}) collective-permute-start(bf16[32,1024]{1,0:T(8,128)(2,1)S(1)} %pad_maximum_fusion.7), channel_id=1, source_target_pairs={{0,8},{8,0},{1,9},{9,1},{2,10},{10,2},{3,11},{11,3},{4,12},{12,4},... | collective-permute-start | bytes 196616 | tf_op jit(solution)/shard_map/ppermute | solution.py:14
  33.7 2.1 collective-permute-done.3
  35.9 3.8 %collective-permute-start.4 = (bf16[64,1024]{1,0:T(8,128)(2,1)S(1)}, bf16[64,1024]{1,0:T(8,128)(2,1)S(1)}, u32[]{:S(2)}, u32[]{:S(2)}) collective-permute-start(bf16[64,1024]{1,0:T(8,128)(2,1)S(1)} %pad_maximum_fusion.6), channel_id=1, source_target_pairs={{0,16},{16,0},{1,17},{17,1},{2,18},{18,2},{3,19},{19,3},{4,20},{20... | collective-permute-start | bytes 393224 | tf_op jit(solution)/shard_map/ppermute | solution.py:14
  39.7 4.3 %collective-permute-done.4 = bf16[64,1024]{1,0:T(8,128)(2,1)S(1)} collective-permute-done((bf16[64,1024]{1,0:T(8,128)(2,1)S(1)}, bf16[64,1024]{1,0:T(8,128)(2,1)S(1)}, u32[]{:S(2)}, u32[]{:S(2)}) %collective-permute-start.4) | collective-permute-done | bytes 131104 | tf_op jit(solution)/shard_map/ppermute | solution.py:14
  44.1 6.7 %collective-permute-start.5 = (bf16[128,1024]{1,0:T(8,128)(2,1)S(1)}, bf16[128,1024]{1,0:T(8,128)(2,1)S(1)}, u32[]{:S(2)}, u32[]{:S(2)}) collective-permute-start(bf16[128,1024]{1,0:T(8,128)(2,1)S(1)} %pad_maximum_fusion.5), channel_id=1, source_target_pairs={{0,32},{32,0},{1,33},{33,1},{2,34},{34,2},{3,35},{35,3},{4,36},{36... | collective-permute-start | bytes 786440 | tf_op jit(solution)/shard_map/ppermute | solution.py:14
  50.9 7.1 %collective-permute-done.5 = bf16[128,1024]{1,0:T(8,128)(2,1)S(1)} collective-permute-done((bf16[128,1024]{1,0:T(8,128)(2,1)S(1)}, bf16[128,1024]{1,0:T(8,128)(2,1)S(1)}, u32[]{:S(2)}, u32[]{:S(2)}) %collective-permute-start.5) | collective-permute-done | bytes 262176 | tf_op jit(solution)/shard_map/ppermute | solution.py:14
  58.2 2.8 collective-permute-start.6
  61.0 7.3 %collective-permute-done.6 = bf16[256,1024]{1,0:T(8,128)(2,1)S(1)} collective-permute-done((bf16[256,1024]{1,0:T(8,128)(2,1)S(1)}, bf16[256,1024]{1,0:T(8,128)(2,1)S(1)}, u32[]{:S(2)}, u32[]{:S(2)}) %collective-permute-start.6) | collective-permute-done | bytes 524320 | tf_op jit(solution)/shard_map/ppermute | solution.py:14
  70.8 3.0 collective-permute-start.7
  73.8 32.5 %collective-permute-done.7 = f32[2,512,512]{2,1,0:T(8,128)S(1)} collective-permute-done((f32[2,512,512]{2,1,0:T(8,128)S(1)}, f32[2,512,512]{2,1,0:T(8,128)S(1)}, u32[]{:S(2)}, u32[]{:S(2)}) %collective-permute-start.7) | collective-permute-done | bytes 2097184 | tf_op jit(solution)/shard_map/ppermute | solution.py:14
  106.7 8.0 %collective-permute-start.8 = (f32[2,512,512]{2,1,0:T(8,128)S(1)}, f32[2,512,512]{2,1,0:T(8,128)S(1)}, u32[]{:S(2)}, u32[]{:S(2)}) collective-permute-start(f32[2,512,512]{2,1,0:T(8,128)S(1)} %fusion.16), channel_id=1, source_target_pairs={{0,2},{2,0},{1,3},{3,1},{4,6},{6,4},{5,7},{7,5},{8,10},{10,8},{9,1... | collective-permute-start | bytes 6291464 | tf_op jit(solution)/shard_map/ppermute | solution.py:14
  114.8 85.3 %collective-permute-done.8 = f32[2,512,512]{2,1,0:T(8,128)S(1)} collective-permute-done((f32[2,512,512]{2,1,0:T(8,128)S(1)}, f32[2,512,512]{2,1,0:T(8,128)S(1)}, u32[]{:S(2)}, u32[]{:S(2)}) %collective-permute-start.8) | collective-permute-done | bytes 2097184 | tf_op jit(solution)/shard_map/ppermute | solution.py:14
  201.7 5.1 %collective-permute-start.9 = (f32[256,1024]{1,0:T(8,128)S(1)}, f32[256,1024]{1,0:T(8,128)S(1)}, u32[]{:S(2)}, u32[]{:S(2)}) collective-permute-start(f32[256,1024]{1,0:T(8,128)S(1)} %slice_select_fusion), channel_id=1, source_target_pairs={{0,64},{64,0},{1,65},{65,1},{2,66},{66,2},{3,67},{67,3},{4,68},{68... | collective-permute-start | bytes 3145736 | tf_op jit(solution)/shard_map/ppermute | solution.py:14
  206.8 18.1 %collective-permute-done.9 = f32[256,1024]{1,0:T(8,128)S(1)} collective-permute-done((f32[256,1024]{1,0:T(8,128)S(1)}, f32[256,1024]{1,0:T(8,128)S(1)}, u32[]{:S(2)}, u32[]{:S(2)}) %collective-permute-start.9) | collective-permute-done | bytes 1048608 | tf_op jit(solution)/shard_map/ppermute | solution.py:14
  225.3 7.0 %collective-permute-start.10 = (f32[128,1024]{1,0:T(8,128)S(1)}, f32[128,1024]{1,0:T(8,128)S(1)}, u32[]{:S(2)}, u32[]{:S(2)}) collective-permute-start(f32[128,1024]{1,0:T(8,128)S(1)} %slice_select_fusion.1), channel_id=1, source_target_pairs={{0,32},{32,0},{1,33},{33,1},{2,34},{34,2},{3,35},{35,3},{4,36},{36... | collective-permute-start | bytes 1572872 | tf_op jit(solution)/shard_map/ppermute | solution.py:14
  232.3 6.9 %collective-permute-done.10 = f32[128,1024]{1,0:T(8,128)S(1)} collective-permute-done((f32[128,1024]{1,0:T(8,128)S(1)}, f32[128,1024]{1,0:T(8,128)S(1)}, u32[]{:S(2)}, u32[]{:S(2)}) %collective-permute-start.10) | collective-permute-done | bytes 524320 | tf_op jit(solution)/shard_map/ppermute | solution.py:14
  239.4 20.3 %collective-permute-start.11 = (f32[64,1024]{1,0:T(8,128)S(1)}, f32[64,1024]{1,0:T(8,128)S(1)}, u32[]{:S(2)}, u32[]{:S(2)}) collective-permute-start(f32[64,1024]{1,0:T(8,128)S(1)} %slice_select_fusion.2), channel_id=1, source_target_pairs={{0,16},{16,0},{1,17},{17,1},{2,18},{18,2},{3,19},{19,3},{4,20},{20... | collective-permute-start | bytes 786440 | tf_op jit(solution)/shard_map/ppermute | solution.py:14
  259.8 11.0 %collective-permute-done.11 = f32[64,1024]{1,0:T(8,128)S(1)} collective-permute-done((f32[64,1024]{1,0:T(8,128)S(1)}, f32[64,1024]{1,0:T(8,128)S(1)}, u32[]{:S(2)}, u32[]{:S(2)}) %collective-permute-start.11) | collective-permute-done | bytes 262176 | tf_op jit(solution)/shard_map/ppermute | solution.py:14
  270.9 2.9 collective-permute-start.12
  273.7 2.8 collective-permute-done.12
  276.6 10.1 %collective-permute-start.13 = (f32[16,1024]{1,0:T(8,128)S(1)}, f32[16,1024]{1,0:T(8,128)S(1)}, u32[]{:S(2)}, u32[]{:S(2)}) collective-permute-start(f32[16,1024]{1,0:T(8,128)S(1)} %slice_select_fusion.4), channel_id=1, source_target_pairs={{0,4},{4,0},{1,5},{5,1},{2,6},{6,2},{3,7},{7,3},{8,12},{12,8},{9,1... | collective-permute-start | bytes 196616 | tf_op jit(solution)/shard_map/ppermute | solution.py:14
  286.7 1.6 collective-permute-done.13
  288.4 1.9 collective-permute-start.14
  290.3 3.6 %collective-permute-done.14 = f32[8,1024]{1,0:T(8,128)S(1)} collective-permute-done((f32[8,1024]{1,0:T(8,128)S(1)}, f32[8,1024]{1,0:T(8,128)S(1)}, u32[]{:S(2)}, u32[]{:S(2)}) %collective-permute-start.14) | collective-permute-done | bytes 32800 | tf_op jit(solution)/shard_map/ppermute | solution.py:14
  294.0 1.9 collective-permute-start.15
  295.9 2.7 collective-permute-done.15
  298.9 9.0 %collective-permute-start.16 = (bf16[4,4096]{1,0:T(4,128)(2,1)S(1)}, bf16[4,4096]{1,0:T(4,128)(2,1)S(1)}, u32[]{:S(2)}, u32[]{:S(2)}) collective-permute-start(bf16[4,4096]{1,0:T(4,128)(2,1)S(1)} %fusion.10), channel_id=1, source_target_pairs={{0,128},{128,256},{256,384},{384,512},{512,640},{640,768},{768,896... | collective-permute-start | bytes 98312 | tf_op jit(solution)/shard_map/ppermute | solution.py:20
  (56 shorter events, 10.4 us)
Async XLA Ops:
  0.0 200.8 %copy-start = (bf16[1,1,512,1024]{3,2,1,0:T(8,128)(2,1)S(1)}, bf16[1,1,512,1024]{3,2,1,0:T(8,128)(2,1)}, u32[]{:S(2)}) copy-start(bf16[1,1,512,1024]{3,2,1,0:T(8,128)(2,1)} %param.9) | copy-start | bytes 3145732
  1.9 9.6 %collective-permute-start = (bf16[4,2048]{1,0:T(4,128)(2,1)S(1)}, bf16[4,2048]{1,0:T(4,128)(2,1)S(1)}, u32[]{:S(2)}, u32[]{:S(2)}) collective-permute-start(bf16[4,2048]{1,0:T(4,128)(2,1)S(1)} %broadcast_select_fusion.12), channel_id=1, source_target_pairs={{0,2},{2,0},{1,3},{3,1},{4,6},{6,4},{5,7},{7,5},{8,10},{10,8},{9,1... | collective-permute-start | bytes 49160 | tf_op jit(solution)/shard_map/ppermute | solution.py:14
  11.5 6.0 %collective-permute-start.1 = (bf16[8,1024]{1,0:T(8,128)(2,1)S(1)}, bf16[8,1024]{1,0:T(8,128)(2,1)S(1)}, u32[]{:S(2)}, u32[]{:S(2)}) collective-permute-start(bf16[8,1024]{1,0:T(8,128)(2,1)S(1)} %broadcast_select_fusion.16), channel_id=1, source_target_pairs={{0,1},{1,0},{2,3},{3,2},{4,5},{5,4},{6,7},{7,6},{8,9},{9,8},{10,11... | collective-permute-start | bytes 49160 | tf_op jit(solution)/shard_map/ppermute | solution.py:14
  17.7 12.9 %collective-permute-start.2 = (bf16[16,1024]{1,0:T(8,128)(2,1)S(1)}, bf16[16,1024]{1,0:T(8,128)(2,1)S(1)}, u32[]{:S(2)}, u32[]{:S(2)}) collective-permute-start(bf16[16,1024]{1,0:T(8,128)(2,1)S(1)} %reshape.24), channel_id=1, source_target_pairs={{0,4},{4,0},{1,5},{5,1},{2,6},{6,2},{3,7},{7,3},{8,12},{12,8},{9,1... | collective-permute-start | bytes 98312 | tf_op jit(solution)/shard_map/ppermute | solution.py:14
  30.6 5.3 %collective-permute-start.3 = (bf16[32,1024]{1,0:T(8,128)(2,1)S(1)}, bf16[32,1024]{1,0:T(8,128)(2,1)S(1)}, u32[]{:S(2)}, u32[]{:S(2)}) collective-permute-start(bf16[32,1024]{1,0:T(8,128)(2,1)S(1)} %pad_maximum_fusion.7), channel_id=1, source_target_pairs={{0,8},{8,0},{1,9},{9,1},{2,10},{10,2},{3,11},{11,3},{4,12},{12,4},... | collective-permute-start | bytes 196616 | tf_op jit(solution)/shard_map/ppermute | solution.py:14
  35.9 8.1 %collective-permute-start.4 = (bf16[64,1024]{1,0:T(8,128)(2,1)S(1)}, bf16[64,1024]{1,0:T(8,128)(2,1)S(1)}, u32[]{:S(2)}, u32[]{:S(2)}) collective-permute-start(bf16[64,1024]{1,0:T(8,128)(2,1)S(1)} %pad_maximum_fusion.6), channel_id=1, source_target_pairs={{0,16},{16,0},{1,17},{17,1},{2,18},{18,2},{3,19},{19,3},{4,20},{20... | collective-permute-start | bytes 393224 | tf_op jit(solution)/shard_map/ppermute | solution.py:14
  44.1 13.9 %collective-permute-start.5 = (bf16[128,1024]{1,0:T(8,128)(2,1)S(1)}, bf16[128,1024]{1,0:T(8,128)(2,1)S(1)}, u32[]{:S(2)}, u32[]{:S(2)}) collective-permute-start(bf16[128,1024]{1,0:T(8,128)(2,1)S(1)} %pad_maximum_fusion.5), channel_id=1, source_target_pairs={{0,32},{32,0},{1,33},{33,1},{2,34},{34,2},{3,35},{35,3},{4,36},{36... | collective-permute-start | bytes 786440 | tf_op jit(solution)/shard_map/ppermute | solution.py:14
  58.2 10.2 %collective-permute-start.6 = (bf16[256,1024]{1,0:T(8,128)(2,1)S(1)}, bf16[256,1024]{1,0:T(8,128)(2,1)S(1)}, u32[]{:S(2)}, u32[]{:S(2)}) collective-permute-start(bf16[256,1024]{1,0:T(8,128)(2,1)S(1)} %pad_maximum_fusion.4), channel_id=1, source_target_pairs={{0,64},{64,0},{1,65},{65,1},{2,66},{66,2},{3,67},{67,3},{4,68},{68... | collective-permute-start | bytes 1572872 | tf_op jit(solution)/shard_map/ppermute | solution.py:14
  61.0 7.6 %copy-start.2 = (bf16[1,1,1024,512]{3,2,1,0:T(8,128)(2,1)S(1)}, bf16[1,1,1024,512]{3,2,1,0:T(8,128)(2,1)}, u32[]{:S(2)}) copy-start(bf16[1,1,1024,512]{3,2,1,0:T(8,128)(2,1)} %param.8) | copy-start | bytes 3145732
  68.7 1.2 copy-start.3
  70.8 35.5 %collective-permute-start.7 = (f32[2,512,512]{2,1,0:T(8,128)S(1)}, f32[2,512,512]{2,1,0:T(8,128)S(1)}, u32[]{:S(2)}, u32[]{:S(2)}) collective-permute-start(f32[2,512,512]{2,1,0:T(8,128)S(1)} %pad_maximum_fusion), channel_id=1, source_target_pairs={{0,1},{1,0},{2,3},{3,2},{4,5},{5,4},{6,7},{7,6},{8,9},{9,8},{10,11... | collective-permute-start | bytes 6291464 | tf_op jit(solution)/shard_map/ppermute | solution.py:14
  106.7 93.3 %collective-permute-start.8 = (f32[2,512,512]{2,1,0:T(8,128)S(1)}, f32[2,512,512]{2,1,0:T(8,128)S(1)}, u32[]{:S(2)}, u32[]{:S(2)}) collective-permute-start(f32[2,512,512]{2,1,0:T(8,128)S(1)} %fusion.16), channel_id=1, source_target_pairs={{0,2},{2,0},{1,3},{3,1},{4,6},{6,4},{5,7},{7,5},{8,10},{10,8},{9,1... | collective-permute-start | bytes 6291464 | tf_op jit(solution)/shard_map/ppermute | solution.py:14
  201.7 23.2 %collective-permute-start.9 = (f32[256,1024]{1,0:T(8,128)S(1)}, f32[256,1024]{1,0:T(8,128)S(1)}, u32[]{:S(2)}, u32[]{:S(2)}) collective-permute-start(f32[256,1024]{1,0:T(8,128)S(1)} %slice_select_fusion), channel_id=1, source_target_pairs={{0,64},{64,0},{1,65},{65,1},{2,66},{66,2},{3,67},{67,3},{4,68},{68... | collective-permute-start | bytes 3145736 | tf_op jit(solution)/shard_map/ppermute | solution.py:14
  225.3 13.9 %collective-permute-start.10 = (f32[128,1024]{1,0:T(8,128)S(1)}, f32[128,1024]{1,0:T(8,128)S(1)}, u32[]{:S(2)}, u32[]{:S(2)}) collective-permute-start(f32[128,1024]{1,0:T(8,128)S(1)} %slice_select_fusion.1), channel_id=1, source_target_pairs={{0,32},{32,0},{1,33},{33,1},{2,34},{34,2},{3,35},{35,3},{4,36},{36... | collective-permute-start | bytes 1572872 | tf_op jit(solution)/shard_map/ppermute | solution.py:14
  239.3 59.5 %copy-start.1 = (bf16[1,4,4096]{2,1,0:T(4,128)(2,1)S(1)}, bf16[1,4,4096]{2,1,0:T(4,128)(2,1)}, u32[]{:S(2)}) copy-start(bf16[1,4,4096]{2,1,0:T(4,128)(2,1)} %param.5) | copy-start | bytes 98308
  239.4 31.4 %collective-permute-start.11 = (f32[64,1024]{1,0:T(8,128)S(1)}, f32[64,1024]{1,0:T(8,128)S(1)}, u32[]{:S(2)}, u32[]{:S(2)}) collective-permute-start(f32[64,1024]{1,0:T(8,128)S(1)} %slice_select_fusion.2), channel_id=1, source_target_pairs={{0,16},{16,0},{1,17},{17,1},{2,18},{18,2},{3,19},{19,3},{4,20},{20... | collective-permute-start | bytes 786440 | tf_op jit(solution)/shard_map/ppermute | solution.py:14
  270.9 5.7 %collective-permute-start.12 = (f32[32,1024]{1,0:T(8,128)S(1)}, f32[32,1024]{1,0:T(8,128)S(1)}, u32[]{:S(2)}, u32[]{:S(2)}) collective-permute-start(f32[32,1024]{1,0:T(8,128)S(1)} %slice_select_fusion.3), channel_id=1, source_target_pairs={{0,8},{8,0},{1,9},{9,1},{2,10},{10,2},{3,11},{11,3},{4,12},{12,4},... | collective-permute-start | bytes 393224 | tf_op jit(solution)/shard_map/ppermute | solution.py:14
  276.6 11.7 %collective-permute-start.13 = (f32[16,1024]{1,0:T(8,128)S(1)}, f32[16,1024]{1,0:T(8,128)S(1)}, u32[]{:S(2)}, u32[]{:S(2)}) collective-permute-start(f32[16,1024]{1,0:T(8,128)S(1)} %slice_select_fusion.4), channel_id=1, source_target_pairs={{0,4},{4,0},{1,5},{5,1},{2,6},{6,2},{3,7},{7,3},{8,12},{12,8},{9,1... | collective-permute-start | bytes 196616 | tf_op jit(solution)/shard_map/ppermute | solution.py:14
  288.4 5.6 %collective-permute-start.14 = (f32[8,1024]{1,0:T(8,128)S(1)}, f32[8,1024]{1,0:T(8,128)S(1)}, u32[]{:S(2)}, u32[]{:S(2)}) collective-permute-start(f32[8,1024]{1,0:T(8,128)S(1)} %slice_select_fusion.5), channel_id=1, source_target_pairs={{0,2},{2,0},{1,3},{3,1},{4,6},{6,4},{5,7},{7,5},{8,10},{10,8},{9,1... | collective-permute-start | bytes 98312 | tf_op jit(solution)/shard_map/ppermute | solution.py:14
  294.0 4.7 %collective-permute-start.15 = (f32[4,2048]{1,0:T(4,128)S(1)}, f32[4,2048]{1,0:T(4,128)S(1)}, u32[]{:S(2)}, u32[]{:S(2)}) collective-permute-start(f32[4,2048]{1,0:T(4,128)S(1)} %broadcast_select_fusion.22), channel_id=1, source_target_pairs={{0,1},{1,0},{2,3},{3,2},{4,5},{5,4},{6,7},{7,6},{8,9},{9,8},{10,11... | collective-permute-start | bytes 98312 | tf_op jit(solution)/shard_map/ppermute | solution.py:14
  298.9 10.0 %collective-permute-start.16 = (bf16[4,4096]{1,0:T(4,128)(2,1)S(1)}, bf16[4,4096]{1,0:T(4,128)(2,1)S(1)}, u32[]{:S(2)}, u32[]{:S(2)}) collective-permute-start(bf16[4,4096]{1,0:T(4,128)(2,1)S(1)} %fusion.10), channel_id=1, source_target_pairs={{0,128},{128,256},{256,384},{384,512},{512,640},{640,768},{768,896... | collective-permute-start | bytes 98312 | tf_op jit(solution)/shard_map/ppermute | solution.py:20
where the time goes:
time: 312 us; the launch traced here: 310 us
  waiting for transfers between devices  190 us (61%)
  starting transfers between devices  111 us (36%)
  other arithmetic  4.77 us (2%)
    ppermute x16, waiting for transfers between devices, swapped(): return lax.ppermute(block, axis, route)  189 us
    ppermute x16, starting transfers between devices, swapped(): return lax.ppermute(block, axis, route)  102 us
    ppermute x1, starting transfers between devices, passed_along(): lax.ppermute(value, axis, [(source, source + steps) for source in range(f...  8.99 us
  transfers between devices with their start and end apart: 17, of which 17 were waited for; matrix products, arithmetic and copies ran while one was open for 0% of the time, Pallas kernels for 0%

commit v1 on v0

v1 whole, which is shorter than its diff:
```python
import jax
import jax.numpy as jnp
from jax import lax
from jax.sharding import PartitionSpec as P


def quads(groups_a):
    count = lax.axis_size("tensor")
    return [list(range(low, low + groups_a)) for low in range(0, count, groups_a)]


def passed_along(value, axis, steps):
    count = lax.axis_size(axis)
    first, last = (max(0, -steps), min(count, count - steps))
    return lax.ppermute(value, axis, [(source, source + steps) for source in range(first, last)])


def per_device(acts, norm_gain, gate_w, up_w, down_w):
    inputs = acts[0].astype(jnp.float32)
    tokens, features = inputs.shape
    scale = lax.rsqrt(jnp.mean(inputs * inputs, axis=-1, keepdims=True) + 1e-05)
    normed = (inputs * scale * norm_gain[0][None, :]).astype(jnp.bfloat16)
    gate_local = gate_w[0, 0]
    up_local = up_w[0, 0]
    down_local = down_w[0, 0]
    depth, width = gate_local.shape
    devices = lax.axis_size("tensor")
    groups_a = features // depth
    groups_b = devices // groups_a
    total = devices * tokens

    by_block = jnp.transpose(normed.reshape(tokens, groups_a, depth), (1, 0, 2))
    sent = jnp.tile(by_block, (groups_b, 1, 1))
    columns = lax.all_to_all(sent, "tensor", 0, 0, tiled=True).reshape(total, depth)

    gate = jnp.dot(columns, gate_local, preferred_element_type=jnp.float32)
    up_part = jnp.dot(columns, up_local, preferred_element_type=jnp.float32)
    both = jnp.concatenate([gate.astype(jnp.bfloat16), up_part.astype(jnp.bfloat16)], axis=1)
    shares = both.reshape(groups_a, total // groups_a, 2 * width)
    shares = lax.all_to_all(shares, "tensor", 0, 0, axis_index_groups=quads(groups_a), tiled=True)
    summed = jnp.sum(shares.astype(jnp.float32), axis=0)
    hidden = (jax.nn.silu(summed[:, :width]) * summed[:, width:]).astype(jnp.bfloat16)
    hidden = jnp.tile(hidden[None], (groups_a, 1, 1))
    hidden = lax.all_to_all(hidden, "tensor", 0, 0, axis_index_groups=quads(groups_a), tiled=True)
    hidden = hidden.reshape(total, width)

    partial_rows = jnp.dot(hidden, down_local, preferred_element_type=jnp.float32)
    sent = partial_rows.astype(jnp.bfloat16).reshape(devices, tokens, depth)
    parts = lax.all_to_all(sent, "tensor", 0, 0, tiled=True)
    parts = parts.reshape(groups_b, groups_a, tokens, depth).astype(jnp.float32)
    rows = jnp.transpose(jnp.sum(parts, axis=0), (1, 0, 2)).reshape(tokens, features)
    block = (inputs + rows).astype(jnp.bfloat16)
    return passed_along(block, "section", 1)[None]


def solution(mesh):
    in_specs = (
        P("section", "tensor", None),
        P("section", None),
        P("section", "tensor", None, None),
        P("section", "tensor", None, None),
        P("section", "tensor", None, None),
    )
    out_specs = P("section", "tensor", None)
    return jax.shard_map(
        per_device, mesh=mesh, in_specs=in_specs, out_specs=out_specs, check_vma=False
    )
```

time: 312 us -> 157 us (0.50)
  waiting for transfers between devices: 190 us -> 1 us
  blocking collectives: 0 us -> 135 us
  starting transfers between devices: 111 us -> 9.36 us
    ppermute x16 -> x0, waiting for transfers between devices: 189 us -> none  [swapped(): return lax.ppermute(block, axis, route)]
    all_to_all x0 -> x4, blocking collectives: none -> 135 us  [the longest x1 54.6 us: per_device(): lax.all_to_all(sent, 'tensor', 0, 0, tiled=True).reshape(total, depth)]
    ppermute x16 -> x0, starting transfers between devices: 102 us -> none  [swapped(): return lax.ppermute(block, axis, route)]
  transfers between devices with their start and end apart: 17 -> 1, of which waited for: 17 -> 1; matrix products, arithmetic and copies ran while one was open for 0% -> 0% of each run, Pallas kernels for 0% -> 0%
where the time goes in v1:
time: 157 us; the launch traced here: 156 us
  blocking collectives  135 us (86%)
  starting transfers between devices  9.36 us (6%)
  local copies, waits for them, and re-layouts  3.59 us (2%)
  matrix products  3.54 us (2%)
  other arithmetic  3.35 us (2%)
    all_to_all x1, blocking collectives, per_device(): lax.all_to_all(sent, 'tensor', 0, 0, tiled=True).reshape(total, depth)  54.6 us
    all_to_all x1, blocking collectives, per_device(): parts = lax.all_to_all(sent, 'tensor', 0, 0, tiled=True)  36.9 us
    all_to_all x1, blocking collectives, per_device(): lax.all_to_all(shares, 'tensor', 0, 0, axis_index_groups=quads(groups_a),...  27.2 us
    all_to_all x1, blocking collectives, per_device(): lax.all_to_all(hidden, 'tensor', 0, 0, axis_index_groups=quads(groups_a),...  16.5 us
    ppermute x1, starting transfers between devices, passed_along(): lax.ppermute(value, axis, [(source, source + steps) for source in range(f...  9.36 us
  transfers between devices with their start and end apart: 1, of which 1 were waited for; matrix products, arithmetic and copies ran while one was open for 0% of the time, Pallas kernels for 0%

profile of v1, /device:TPU:1, one launch (start us, length us, event | category | flops | bytes accessed | tf_op | source)
XLA Modules:
  0.0 156.0 jit_solution(12850795786181220172)
XLA Ops:
  0.0 0.0 copy-start
  0.0 1.0 fusion.4
  1.0 0.8 reshape.55
  1.8 0.5 broadcast.38
  2.3 1.4 reduce.3
  3.7 0.1 fusion.6
  3.9 0.5 tile.6
  4.3 54.6 %all_to_all.20 = bf16[128,4,1024]{2,1,0:T(4,128)(2,1)S(1)} all-to-all(bf16[128,4,1024]{2,1,0:T(4,128)(2,1)S(1)} %bitcast.34), channel_id=1, replica_groups=mesh['section'=8,'tensor'=128] {'tensor'}, dimensions={0} | all-to-all | bytes 2097152 | tf_op jit(solution)/shard_map/all_to_all | solution.py:34
  58.9 0.3 reshape.49
  59.2 0.0 copy-start.2
  59.2 2.1 %convolution_convert_fusion.1 = bf16[512,512]{0,1:T(8,128)(2,1)S(1)} fusion(bf16[512,1024]{1,0:T(8,128)(2,1)S(1)} %reshape.49, bf16[1,1,1024,512]{3,2,1,0:T(8,128)(2,1)} %param.8), kind=kOutput, calls=%fused_computation.3 | convolution fusion | flops 537133056 | bytes 2621440 | tf_op jit(solution)/shard_map/dot_general | solution.py:37
  61.3 0.0 copy-done.2
  61.3 0.8 convolution_convert_fusion.2
  62.0 0.2 copy_bitcast_fusion
  62.2 27.2 %all_to_all.21 = bf16[4,128,1024]{1,2,0:T(8,128)(2,1)S(1)} all-to-all(bf16[4,128,1024]{1,2,0:T(8,128)(2,1)S(1)} %copy_bitcast_fusion), channel_id=1, replica_groups={{0,1,2,3},{4,5,6,7},{8,9,10,11},{12,13,14,15},{16,17,18,19},{20,21,22,2..., dimensions={0} | all-to-all | bytes 2097152 | tf_op jit(solution)/shard_map/all_to_all | solution.py:40
  89.4 0.1 convert_reduce_fusion.1
  89.5 0.1 fusion.3
  89.6 0.1 copy.10
  89.8 16.5 %all_to_all.22 = bf16[4,128,512]{2,1,0:T(8,128)(2,1)S(1)} all-to-all(bf16[4,128,512]{2,1,0:T(8,128)(2,1)S(1)} %tile.8), channel_id=1, replica_groups={{0,1,2,3},{4,5,6,7},{8,9,10,11},{12,13,14,15},{16,17,18,19},{20,21,22,2..., dimensions={0} | all-to-all | bytes 1048576 | tf_op jit(solution)/shard_map/all_to_all | solution.py:44
  106.3 0.0 copy-done
  106.3 0.7 convolution_convert_fusion
  107.0 0.4 reshape.52
  107.4 36.9 %all_to_all.23 = bf16[128,4,1024]{2,1,0:T(4,128)(2,1)S(1)} all-to-all(bf16[128,4,1024]{2,1,0:T(4,128)(2,1)S(1)} %reshape.52), channel_id=1, replica_groups=mesh['section'=8,'tensor'=128] {'tensor'}, dimensions={0} | all-to-all | bytes 2097152 | tf_op jit(solution)/shard_map/all_to_all | solution.py:49
  144.3 0.0 copy-start.1
  144.3 0.4 convert_reduce_fusion
  144.7 0.3 copy-done.1
  145.1 9.4 %collective-permute-start = (bf16[4,4096]{1,0:T(4,128)(2,1)S(1)}, bf16[4,4096]{1,0:T(4,128)(2,1)S(1)}, u32[]{:S(2)}, u32[]{:S(2)}) collective-permute-start(bf16[4,4096]{1,0:T(4,128)(2,1)S(1)} %fusion.5), channel_id=1, source_target_pairs={{0,128},{128,256},{256,384},{384,512},{512,640},{640,768},{768,896... | collective-permute-start | bytes 98312 | tf_op jit(solution)/shard_map/ppermute | solution.py:15
  154.4 1.0 collective-permute-done
  155.4 0.6 copy.17
  (5 shorter events, 0.1 us)
Async XLA Ops:
  0.0 106.3 %copy-start = (bf16[1,1,512,1024]{3,2,1,0:T(8,128)(2,1)S(1)}, bf16[1,1,512,1024]{3,2,1,0:T(8,128)(2,1)}, u32[]{:S(2)}) copy-start(bf16[1,1,512,1024]{3,2,1,0:T(8,128)(2,1)} %param.9) | copy-start | bytes 3145732
  59.2 2.1 %copy-start.2 = (bf16[1,1,1024,512]{3,2,1,0:T(8,128)(2,1)S(1)}, bf16[1,1,1024,512]{3,2,1,0:T(8,128)(2,1)}, u32[]{:S(2)}) copy-start(bf16[1,1,1024,512]{3,2,1,0:T(8,128)(2,1)} %param.7) | copy-start | bytes 3145732
  144.3 0.8 copy-start.1
  145.1 10.4 %collective-permute-start = (bf16[4,4096]{1,0:T(4,128)(2,1)S(1)}, bf16[4,4096]{1,0:T(4,128)(2,1)S(1)}, u32[]{:S(2)}, u32[]{:S(2)}) collective-permute-start(bf16[4,4096]{1,0:T(4,128)(2,1)S(1)} %fusion.5), channel_id=1, source_target_pairs={{0,128},{128,256},{256,384},{384,512},{512,640},{640,768},{768,896... | collective-permute-start | bytes 98312 | tf_op jit(solution)/shard_map/ppermute | solution.py:15

commit v2 on v1

v2 whole, which is shorter than its diff:
```python
import jax
import jax.numpy as jnp
from jax import lax
from jax.sharding import PartitionSpec as P


def runs(size):
    count = lax.axis_size("tensor")
    return [list(range(low, low + size)) for low in range(0, count, size)]


def traded(blocks, size):
    return lax.all_to_all(blocks, "tensor", 0, 0, axis_index_groups=runs(size), tiled=True)


def mirrored(values):
    count = lax.axis_size("tensor")
    half = count // 2
    return lax.ppermute(values, "tensor", [(i, (i + half) % count) for i in range(count)])


def passed_along(value, axis, steps):
    count = lax.axis_size(axis)
    first, last = (max(0, -steps), min(count, count - steps))
    return lax.ppermute(value, axis, [(source, source + steps) for source in range(first, last)])


def per_device(acts, norm_gain, gate_w, up_w, down_w):
    inputs = acts[0].astype(jnp.float32)
    tokens, features = inputs.shape
    scale = lax.rsqrt(jnp.mean(inputs * inputs, axis=-1, keepdims=True) + 1e-05)
    normed = (inputs * scale * norm_gain[0][None, :]).astype(jnp.bfloat16)
    gate_local = gate_w[0, 0]
    up_local = up_w[0, 0]
    down_local = down_w[0, 0]
    depth, width = gate_local.shape
    groups_a = features // depth
    near = lax.axis_size("tensor") // 2
    groups_b = near // groups_a
    total = near * tokens

    def hidden_share(columns):
        gate = jnp.dot(columns, gate_local, preferred_element_type=jnp.float32)
        up_part = jnp.dot(columns, up_local, preferred_element_type=jnp.float32)
        both = jnp.concatenate([gate.astype(jnp.bfloat16), up_part.astype(jnp.bfloat16)], axis=1)
        shares = traded(both.reshape(groups_a, total // groups_a, 2 * width), groups_a)
        summed = jnp.sum(shares.astype(jnp.float32), axis=0)
        return (jax.nn.silu(summed[:, :width]) * summed[:, width:]).astype(jnp.bfloat16)

    def down_rows(share):
        hidden = traded(jnp.tile(share[None], (groups_a, 1, 1)), groups_a).reshape(total, width)
        return jnp.dot(hidden, down_local, preferred_element_type=jnp.float32)

    by_block = jnp.transpose(normed.reshape(tokens, groups_a, depth), (1, 0, 2))
    near_columns = traded(jnp.tile(by_block, (groups_b, 1, 1)), near).reshape(total, depth)
    far_columns = mirrored(near_columns)
    near_share = hidden_share(near_columns)
    far_share = hidden_share(far_columns)

    far_rows = mirrored(down_rows(far_share).astype(jnp.bfloat16))
    rows = down_rows(near_share) + far_rows.astype(jnp.float32)
    parts = traded(rows.astype(jnp.bfloat16).reshape(near, tokens, depth), near)
    parts = parts.reshape(groups_b, groups_a, tokens, depth).astype(jnp.float32)
    summed = jnp.transpose(jnp.sum(parts, axis=0), (1, 0, 2)).reshape(tokens, features)
    block = (inputs + summed).astype(jnp.bfloat16)
    return passed_along(block, "section", 1)[None]


def solution(mesh):
    in_specs = (
        P("section", "tensor", None),
        P("section", None),
        P("section", "tensor", None, None),
        P("section", "tensor", None, None),
        P("section", "tensor", None, None),
    )
    out_specs = P("section", "tensor", None)
    return jax.shard_map(
        per_device, mesh=mesh, in_specs=in_specs, out_specs=out_specs, check_vma=False
    )
```

time: 157 us -> 155 us (0.987)
  blocking collectives: 135 us -> 79.9 us
  waiting for transfers between devices: 1 us -> 33.6 us
  starting transfers between devices: 9.36 us -> 30.9 us
    all_to_all x4 -> x3, blocking collectives: 135 us -> 79.9 us  [traded(): lax.all_to_all(blocks, 'tensor', 0, 0, axis_index_groups=runs(size), tile...]
    all_to_all x0 -> x3, waiting for transfers between devices: none -> 24.5 us  [traded(): lax.all_to_all(blocks, 'tensor', 0, 0, axis_index_groups=runs(size), tile...]
    all_to_all x0 -> x3, starting transfers between devices: none -> 14.7 us  [traded(): lax.all_to_all(blocks, 'tensor', 0, 0, axis_index_groups=runs(size), tile...]
    ppermute x0 -> x2, waiting for transfers between devices: none -> 8.1 us  [mirrored(): lax.ppermute(values, 'tensor', [(i, (i + half) % count) for i in range(co...]
    ppermute x0 -> x2, starting transfers between devices: none -> 6.77 us  [mirrored(): lax.ppermute(values, 'tensor', [(i, (i + half) % count) for i in range(co...]
    concatenate x0 -> x2, other arithmetic: none -> 1.73 us  [hidden_share(): jnp.concatenate([gate.astype(jnp.bfloat16), up_part.astype(jnp.bfloat16)]...]
    dot_general x3 -> x6, matrix products: 3.54 us -> 2.63 us  [the longest x2 0.88 us: down_rows(): return jnp.dot(hidden, down_local, preferred_element_type=jnp.float32)]
  transfers between devices with their start and end apart: 1 -> 6, of which waited for: 1 -> 5; matrix products, arithmetic and copies ran while one was open for 0% -> 1% of each run, Pallas kernels for 0% -> 0%
where the time goes in v2:
time: 155 us
  blocking collectives  79.9 us (52%)
  waiting for transfers between devices  33.6 us (22%)
  starting transfers between devices  30.9 us (20%)
  other arithmetic  4.01 us (3%)
  local copies, waits for them, and re-layouts  3.39 us (2%)
  matrix products  2.63 us (2%)
    all_to_all x3, blocking collectives, traded(): lax.all_to_all(blocks, 'tensor', 0, 0, axis_index_groups=runs(size), tile...  79.9 us
    all_to_all x3, waiting for transfers between devices, traded(): lax.all_to_all(blocks, 'tensor', 0, 0, axis_index_groups=runs(size), tile...  24.5 us
    all_to_all x3, starting transfers between devices, traded(): lax.all_to_all(blocks, 'tensor', 0, 0, axis_index_groups=runs(size), tile...  14.7 us
    ppermute x1, starting transfers between devices, passed_along(): lax.ppermute(value, axis, [(source, source + steps) for source in range(f...  9.42 us
    ppermute x2, waiting for transfers between devices, mirrored(): lax.ppermute(values, 'tensor', [(i, (i + half) % count) for i in range(co...  8.1 us
    ppermute x2, starting transfers between devices, mirrored(): lax.ppermute(values, 'tensor', [(i, (i + half) % count) for i in range(co...  6.77 us
  transfers between devices with their start and end apart: 6, of which 5 were waited for; matrix products, arithmetic and copies ran while one was open for 1% of the time, Pallas kernels for 0%

profile of v2, /device:TPU:1, one launch (start us, length us, event | category | flops | bytes accessed | tf_op | source)
XLA Modules:
  0.0 154.7 jit_solution(9161133382995911793)
XLA Ops:
  0.0 1.0 fusion.9
  1.1 0.5 broadcast.42
  1.6 0.1 copy-done.5
  1.7 0.7 reduce.3
  2.6 0.2 tile.8
  2.8 39.4 %all_to_all.30 = bf16[64,4,1024]{2,1,0:T(4,128)(2,1)S(1)} all-to-all(bf16[64,4,1024]{2,1,0:T(4,128)(2,1)S(1)} %bitcast.44), channel_id=1, replica_groups={{0,1,2,3,4,5,6,7,8,9,10,11,12,13,14,15,16,17,18,19,20,21,22,23,24,25,26..., dimensions={0} | all-to-all | bytes 1048576 | tf_op jit(solution)/shard_map/all_to_all | solution.py:13
  42.4 3.5 %collective-permute-start = (bf16[256,1024]{1,0:T(8,128)(2,1)S(1)}, bf16[256,1024]{1,0:T(8,128)(2,1)S(1)}, u32[]{:S(2)}, u32[]{:S(2)}) collective-permute-start(bf16[256,1024]{1,0:T(8,128)(2,1)S(1)} %reshape.58), channel_id=1, source_target_pairs={{0,64},{1,65},{2,66},{3,67},{4,68},{5,69},{6,70},{7,71},{8,72},{9,... | collective-permute-start | bytes 1572872 | tf_op jit(solution)/shard_map/ppermute | solution.py:19
  45.8 8.1 %collective-permute-done = bf16[256,1024]{1,0:T(8,128)(2,1)S(1)} collective-permute-done((bf16[256,1024]{1,0:T(8,128)(2,1)S(1)}, bf16[256,1024]{1,0:T(8,128)(2,1)S(1)}, u32[]{:S(2)}, u32[]{:S(2)}) %collective-permute-start) | collective-permute-done | bytes 524320 | tf_op jit(solution)/shard_map/ppermute | solution.py:19
  53.9 0.4 convolution_convert_fusion.1
  54.4 0.4 convolution_convert_fusion.2
  54.8 0.9 pad_maximum_fusion.1
  55.7 5.3 %all-to-all-start.3 = ((bf16[4,64,1024]{2,1,0:T(8,128)(2,1)}), bf16[4,64,1024]{2,1,0:T(8,128)(2,1)S(1)}, u32[]{:S(2)}, u32[]{:S(2)}) async-start(bf16[4,64,1024]{2,1,0:T(8,128)(2,1)} %bitcast.43), calls=%async_computation.3 | async-start | bytes 1048576 | tf_op jit(solution)/shard_map/all_to_all | solution.py:13
  61.0 0.4 convolution_convert_fusion.3
  61.4 0.8 copy-done.3
  62.2 0.4 convolution_convert_fusion.4
  62.6 0.9 pad_maximum_fusion
  63.5 8.3 %all-to-all-done.3 = bf16[4,64,1024]{2,1,0:T(8,128)(2,1)S(1)} async-done(((bf16[4,64,1024]{2,1,0:T(8,128)(2,1)}), bf16[4,64,1024]{2,1,0:T(8,128)(2,1)S(1)}, u32[]{:S(2)}, u32[]{:S(2)}) %all-to-all-start.3) | async-done | bytes 524320 | tf_op jit(solution)/shard_map/all_to_all | solution.py:13
  71.8 4.5 %all-to-all-start.1 = ((bf16[4,64,1024]{2,1,0:T(8,128)(2,1)}), bf16[4,64,1024]{2,1,0:T(8,128)(2,1)S(1)}, u32[]{:S(2)}, u32[]{:S(2)}) async-start(bf16[4,64,1024]{2,1,0:T(8,128)(2,1)} %bitcast.5), calls=%async_computation.1 | async-start | bytes 1048576 | tf_op jit(solution)/shard_map/all_to_all | solution.py:13
  76.5 10.7 %all-to-all-done.1 = bf16[4,64,1024]{2,1,0:T(8,128)(2,1)S(1)} async-done(((bf16[4,64,1024]{2,1,0:T(8,128)(2,1)}), bf16[4,64,1024]{2,1,0:T(8,128)(2,1)S(1)}, u32[]{:S(2)}, u32[]{:S(2)}) %all-to-all-start.1) | async-done | bytes 524320 | tf_op jit(solution)/shard_map/all_to_all | solution.py:13
  87.2 0.7 tile.11
  87.9 4.9 %all-to-all-start.4 = ((bf16[4,64,512]{2,1,0:T(8,128)(2,1)}), bf16[4,64,512]{2,1,0:T(8,128)(2,1)S(1)}, u32[]{:S(2)}, u32[]{:S(2)}) async-start(bf16[4,64,512]{2,1,0:T(8,128)(2,1)} %tile.11), calls=%async_computation.4 | async-start | bytes 524288 | tf_op jit(solution)/shard_map/all_to_all | solution.py:13
  92.9 5.5 %all-to-all-done.4 = bf16[4,64,512]{2,1,0:T(8,128)(2,1)S(1)} async-done(((bf16[4,64,512]{2,1,0:T(8,128)(2,1)}), bf16[4,64,512]{2,1,0:T(8,128)(2,1)S(1)}, u32[]{:S(2)}, u32[]{:S(2)}) %all-to-all-start.4) | async-done | bytes 262176 | tf_op jit(solution)/shard_map/all_to_all | solution.py:13
  98.4 0.4 convolution_convert_fusion
  98.9 3.3 %collective-permute-start.1 = (bf16[256,1024]{1,0:T(8,128)(2,1)S(1)}, bf16[256,1024]{1,0:T(8,128)(2,1)S(1)}, u32[]{:S(2)}, u32[]{:S(2)}) collective-permute-start(bf16[256,1024]{1,0:T(8,128)(2,1)S(1)} %convolution_convert_fusion), channel_id=1, source_target_pairs={{0,64},{1,65},{2,66},{3,67},{4,68},{5,69},{6,70},{7,71},{8,72},{9,... | collective-permute-start | bytes 1572872 | tf_op jit(solution)/shard_map/ppermute | solution.py:19
  102.3 8.9 %all_to_all.31 = bf16[4,64,512]{2,1,0:T(8,128)(2,1)S(1)} all-to-all(bf16[4,64,512]{2,1,0:T(8,128)(2,1)S(1)} %tile.10), channel_id=1, replica_groups={{0,1,2,3},{4,5,6,7},{8,9,10,11},{12,13,14,15},{16,17,18,19},{20,21,22,2..., dimensions={0} | all-to-all | bytes 524288 | tf_op jit(solution)/shard_map/all_to_all | solution.py:13
  111.2 0.4 add_convert_fusion
  111.7 0.2 reshape.63
  111.9 31.5 %all_to_all.32 = bf16[64,4,1024]{2,1,0:T(4,128)(2,1)S(1)} all-to-all(bf16[64,4,1024]{2,1,0:T(4,128)(2,1)S(1)} %reshape.63), channel_id=1, replica_groups={{0,1,2,3,4,5,6,7,8,9,10,11,12,13,14,15,16,17,18,19,20,21,22,23,24,25,26..., dimensions={0} | all-to-all | bytes 1048576 | tf_op jit(solution)/shard_map/all_to_all | solution.py:13
  143.4 0.2 convert_reduce_fusion
  143.6 9.4 %collective-permute-start.2 = (bf16[4,4096]{1,0:T(4,128)(2,1)S(1)}, bf16[4,4096]{1,0:T(4,128)(2,1)S(1)}, u32[]{:S(2)}, u32[]{:S(2)}) collective-permute-start(bf16[4,4096]{1,0:T(4,128)(2,1)S(1)} %fusion.10), channel_id=1, source_target_pairs={{0,128},{128,256},{256,384},{384,512},{512,640},{640,768},{768,896... | collective-permute-start | bytes 98312 | tf_op jit(solution)/shard_map/ppermute | solution.py:25
  153.0 1.0 collective-permute-done.2
  154.0 0.6 copy.9
  (23 shorter events, 0.6 us)
Async XLA Ops:
  0.0 98.4 %copy-start = (bf16[1,1,512,1024]{3,2,1,0:T(8,128)(2,1)S(1)}, bf16[1,1,512,1024]{3,2,1,0:T(8,128)(2,1)}, u32[]{:S(2)}) copy-start(bf16[1,1,512,1024]{3,2,1,0:T(8,128)(2,1)} %param.9) | copy-start | bytes 3145732
  0.0 1.0 copy-start.4
  1.0 0.7 copy-start.5
  2.8 51.2 %copy-start.1 = (bf16[1,1,1024,512]{3,2,1,0:T(8,128)(2,1)S(1)}, bf16[1,1,1024,512]{3,2,1,0:T(8,128)(2,1)}, u32[]{:S(2)}) copy-start(bf16[1,1,1024,512]{3,2,1,0:T(8,128)(2,1)} %param.8) | copy-start | bytes 3145732
  42.3 12.0 %copy-start.2 = (bf16[1,1,1024,512]{3,2,1,0:T(8,128)(2,1)S(1)}, bf16[1,1,1024,512]{3,2,1,0:T(8,128)(2,1)}, u32[]{:S(2)}) copy-start(bf16[1,1,1024,512]{3,2,1,0:T(8,128)(2,1)} %param.7) | copy-start | bytes 3145732
  42.4 11.6 %collective-permute-start = (bf16[256,1024]{1,0:T(8,128)(2,1)S(1)}, bf16[256,1024]{1,0:T(8,128)(2,1)S(1)}, u32[]{:S(2)}, u32[]{:S(2)}) collective-permute-start(bf16[256,1024]{1,0:T(8,128)(2,1)S(1)} %reshape.58), channel_id=1, source_target_pairs={{0,64},{1,65},{2,66},{3,67},{4,68},{5,69},{6,70},{7,71},{8,72},{9,... | collective-permute-start | bytes 1572872 | tf_op jit(solution)/shard_map/ppermute | solution.py:19
  55.7 16.1 %all-to-all-start.3 = ((bf16[4,64,1024]{2,1,0:T(8,128)(2,1)}), bf16[4,64,1024]{2,1,0:T(8,128)(2,1)S(1)}, u32[]{:S(2)}, u32[]{:S(2)}) async-start(bf16[4,64,1024]{2,1,0:T(8,128)(2,1)} %bitcast.43), calls=%async_computation.3 | async-start | bytes 1048576 | tf_op jit(solution)/shard_map/all_to_all | solution.py:13
  61.0 1.2 copy-start.3
  71.8 15.4 %all-to-all-start.1 = ((bf16[4,64,1024]{2,1,0:T(8,128)(2,1)}), bf16[4,64,1024]{2,1,0:T(8,128)(2,1)S(1)}, u32[]{:S(2)}, u32[]{:S(2)}) async-start(bf16[4,64,1024]{2,1,0:T(8,128)(2,1)} %bitcast.5), calls=%async_computation.1 | async-start | bytes 1048576 | tf_op jit(solution)/shard_map/all_to_all | solution.py:13
  87.9 10.5 %all-to-all-start.4 = ((bf16[4,64,512]{2,1,0:T(8,128)(2,1)}), bf16[4,64,512]{2,1,0:T(8,128)(2,1)S(1)}, u32[]{:S(2)}, u32[]{:S(2)}) async-start(bf16[4,64,512]{2,1,0:T(8,128)(2,1)} %tile.11), calls=%async_computation.4 | async-start | bytes 524288 | tf_op jit(solution)/shard_map/all_to_all | solution.py:13
  98.9 12.3 %collective-permute-start.1 = (bf16[256,1024]{1,0:T(8,128)(2,1)S(1)}, bf16[256,1024]{1,0:T(8,128)(2,1)S(1)}, u32[]{:S(2)}, u32[]{:S(2)}) collective-permute-start(bf16[256,1024]{1,0:T(8,128)(2,1)S(1)} %convolution_convert_fusion), channel_id=1, source_target_pairs={{0,64},{1,65},{2,66},{3,67},{4,68},{5,69},{6,70},{7,71},{8,72},{9,... | collective-permute-start | bytes 1572872 | tf_op jit(solution)/shard_map/ppermute | solution.py:19
  143.6 10.4 %collective-permute-start.2 = (bf16[4,4096]{1,0:T(4,128)(2,1)S(1)}, bf16[4,4096]{1,0:T(4,128)(2,1)S(1)}, u32[]{:S(2)}, u32[]{:S(2)}) collective-permute-start(bf16[4,4096]{1,0:T(4,128)(2,1)S(1)} %fusion.10), channel_id=1, source_target_pairs={{0,128},{128,256},{256,384},{384,512},{512,640},{640,768},{768,896... | collective-permute-start | bytes 98312 | tf_op jit(solution)/shard_map/ppermute | solution.py:25

commit v3 on v2

v3 whole, which is shorter than its diff:
```python
import jax
import jax.numpy as jnp
from jax import lax
from jax.experimental import pallas as pl
from jax.experimental.pallas import tpu as pltpu
from jax.sharding import PartitionSpec as P

f32, bf16 = jnp.float32, jnp.bfloat16


def runs(size):
    count = lax.axis_size("tensor")
    return [list(range(low, low + size)) for low in range(0, count, size)]


def traded(blocks, size):
    return lax.all_to_all(blocks, "tensor", 0, 0, axis_index_groups=runs(size), tiled=True)


def mirrored(values):
    count = lax.axis_size("tensor")
    half = count // 2
    return lax.ppermute(values, "tensor", [(i, (i + half) % count) for i in range(count)])


def passed_along(value, axis, steps):
    count = lax.axis_size(axis)
    first, last = (max(0, -steps), min(count, count - steps))
    return lax.ppermute(value, axis, [(source, source + steps) for source in range(first, last)])


def dot(left, right):
    return jnp.dot(left, right, preferred_element_type=f32)


def local(body, outs, flops, moved, *operands):
    spec = pl.BlockSpec(memory_space=pltpu.VMEM)
    return pl.pallas_call(
        body,
        out_shape=[jax.ShapeDtypeStruct(shape, bf16) for shape in outs],
        in_specs=[spec] * len(operands),
        out_specs=[spec] * len(outs),
        compiler_params=pltpu.CompilerParams(vmem_limit_bytes=24 * 2**20),
        cost_estimate=pl.CostEstimate(flops=flops, bytes_accessed=moved, transcendentals=0),
    )(*operands)


def norm_kernel(acts_ref, gain_ref, out_ref):
    count, _, depth = out_ref.shape
    inputs = acts_ref[...].astype(f32)
    groups = inputs.shape[1] // depth
    scale = lax.rsqrt(jnp.mean(inputs * inputs, axis=-1, keepdims=True) + 1e-05)
    normed = (inputs * scale * gain_ref[...]).astype(bf16)
    for block in range(count):
        low = block % groups * depth
        out_ref[block] = normed[:, low : low + depth]


def gate_up(columns_ref, gate_ref, up_ref, both_ref):
    width = gate_ref.shape[1]
    both_ref[:, :width] = dot(columns_ref[...], gate_ref[...]).astype(bf16)
    both_ref[:, width:] = dot(columns_ref[...], up_ref[...]).astype(bf16)


def gated(shares_ref):
    width = shares_ref.shape[2] // 2
    total = shares_ref[0].astype(f32)
    for part in range(1, shares_ref.shape[0]):
        total = total + shares_ref[part].astype(f32)
    gate = total[:, :width]
    return (gate / (1.0 + jnp.exp(-gate)) * total[:, width:]).astype(bf16)


def gate_up_and_gated(shares_ref, columns_ref, gate_ref, up_ref, both_ref, share_ref):
    gate_up(columns_ref, gate_ref, up_ref, both_ref)
    share_ref[...] = gated(shares_ref)


def copies(share, out_ref):
    for block in range(out_ref.shape[0]):
        out_ref[block] = share


def gated_copies(shares_ref, out_ref):
    copies(gated(shares_ref), out_ref)


def down_far(hidden_ref, down_ref, share_ref, rows_ref, out_ref):
    rows_ref[...] = dot(hidden_ref[...], down_ref[...]).astype(bf16)
    copies(share_ref[...], out_ref)


def down_near(hidden_ref, down_ref, far_ref, rows_ref):
    own = dot(hidden_ref[...], down_ref[...])
    rows_ref[...] = (own + far_ref[...].astype(f32)).astype(bf16)


def per_device(acts, norm_gain, gate_w, up_w, down_w):
    gate_local, up_local, down_local = gate_w[0, 0], up_w[0, 0], down_w[0, 0]
    tokens, features = acts.shape[1:]
    depth, width = gate_local.shape
    groups_a = features // depth
    near = lax.axis_size("tensor") // 2
    groups_b = near // groups_a
    total = near * tokens
    piece = total // groups_a
    cost = 2 * total * depth * width
    weight = 2 * depth * width

    (sent,) = local(norm_kernel, [(near, tokens, depth)], 0, 2 * total * depth, acts[0], norm_gain)
    near_columns = traded(sent, near).reshape(total, depth)
    far_columns = mirrored(near_columns)

    (both,) = local(
        gate_up, [(total, 2 * width)], 2 * cost, 2 * weight, near_columns, gate_local, up_local
    )
    shares = traded(both.reshape(groups_a, piece, 2 * width), groups_a)
    both, near_share = local(
        gate_up_and_gated,
        [(total, 2 * width), (piece, width)],
        2 * cost,
        2 * weight,
        shares,
        far_columns,
        gate_local,
        up_local,
    )
    shares = traded(both.reshape(groups_a, piece, 2 * width), groups_a)
    (spread,) = local(gated_copies, [(groups_a, piece, width)], 0, 2 * total * width, shares)
    hidden = traded(spread, groups_a).reshape(total, width)
    far_rows, spread = local(
        down_far,
        [(total, depth), (groups_a, piece, width)],
        cost,
        weight,
        hidden,
        down_local,
        near_share,
    )
    far_rows = mirrored(far_rows)
    hidden = traded(spread, groups_a).reshape(total, width)
    (rows,) = local(down_near, [(total, depth)], cost, weight, hidden, down_local, far_rows)

    parts = traded(rows.reshape(near, tokens, depth), near)
    parts = parts.reshape(groups_b, groups_a, tokens, depth).astype(f32)
    summed = jnp.transpose(jnp.sum(parts, axis=0), (1, 0, 2)).reshape(tokens, features)
    block = (acts[0].astype(f32) + summed).astype(bf16)
    return passed_along(block, "section", 1)[None]


def solution(mesh):
    in_specs = (
        P("section", "tensor", None),
        P("section", None),
        P("section", "tensor", None, None),
        P("section", "tensor", None, None),
        P("section", "tensor", None, None),
    )
    out_specs = P("section", "tensor", None)
    return jax.shard_map(
        per_device, mesh=mesh, in_specs=in_specs, out_specs=out_specs, check_vma=False
    )
```

time: 155 us -> 141 us (0.910)
  waiting for transfers between devices: 33.6 us -> 9.8 us
  blocking collectives: 79.9 us -> 101 us
  starting transfers between devices: 30.9 us -> 21.2 us
  other arithmetic: 4.01 us -> 0.25 us
  Pallas kernels: 0 us -> 3.4 us
  matrix products: 2.63 us -> 0 us
    all_to_all x3 -> x1, waiting for transfers between devices: 24.5 us -> 0.01 us  [traded(): lax.all_to_all(blocks, 'tensor', 0, 0, axis_index_groups=runs(size), tile...]
    all_to_all x3 -> x5, blocking collectives: 79.9 us -> 101 us  [traded(): lax.all_to_all(blocks, 'tensor', 0, 0, axis_index_groups=runs(size), tile...]
    all_to_all x3 -> x1, starting transfers between devices: 14.7 us -> 4.33 us  [traded(): lax.all_to_all(blocks, 'tensor', 0, 0, axis_index_groups=runs(size), tile...]
    pallas_call x0 -> x6, Pallas kernels: none -> 3.4 us  [local(): pl.pallas_call(body, out_shape=[jax.ShapeDtypeStruct(shape, bf16) for sha...]
    dot_general x6 -> x0, matrix products: 2.63 us -> none  [the longest x2 0.88 us: down_rows(): return jnp.dot(hidden, down_local, preferred_element_type=jnp.float32)]
    unnamed x14 -> x17, local copies, waits for them, and re-layouts: 2.08 us -> 4.48 us
    concatenate x2 -> x0, other arithmetic: 1.73 us -> none  [hidden_share(): jnp.concatenate([gate.astype(jnp.bfloat16), up_part.astype(jnp.bfloat16)]...]
  transfers between devices with their start and end apart: 6 -> 4, of which waited for: 5 -> 2; matrix products, arithmetic and copies ran while one was open for 1% -> 0% of each run, Pallas kernels for 0% -> 0%
where the time goes in v3:
time: 141 us; the launch traced here: 140 us
  blocking collectives  101 us (72%)
  starting transfers between devices  21.2 us (15%)
  waiting for transfers between devices  9.8 us (7%)
  local copies, waits for them, and re-layouts  4.79 us (3%)
  Pallas kernels  3.4 us (2%)
    all_to_all x5, blocking collectives, traded(): lax.all_to_all(blocks, 'tensor', 0, 0, axis_index_groups=runs(size), tile...  101 us
    ppermute x1, starting transfers between devices, passed_along(): lax.ppermute(value, axis, [(source, source + steps) for source in range(f...  10.2 us
    ppermute x2, waiting for transfers between devices, mirrored(): lax.ppermute(values, 'tensor', [(i, (i + half) % count) for i in range(co...  8.79 us
    ppermute x2, starting transfers between devices, mirrored(): lax.ppermute(values, 'tensor', [(i, (i + half) % count) for i in range(co...  6.62 us
    unnamed x17, local copies, waits for them, and re-layouts  4.48 us
    all_to_all x1, starting transfers between devices, traded(): lax.all_to_all(blocks, 'tensor', 0, 0, axis_index_groups=runs(size), tile...  4.33 us
    pallas_call x6, Pallas kernels, local(): pl.pallas_call(body, out_shape=[jax.ShapeDtypeStruct(shape, bf16) for sha...  3.4 us
  transfers between devices with their start and end apart: 4, of which 2 were waited for; matrix products, arithmetic and copies ran while one was open for 0% of the time, Pallas kernels for 0%

profile of v3, /device:TPU:1, one launch (start us, length us, event | category | flops | bytes accessed | tf_op | source)
XLA Modules:
  0.0 140.3 jit_solution(14634590391141875832)
XLA Ops:
  0.0 0.8 copy-done.5
  0.8 0.7 copy-done.7
  1.5 0.2 shard_map.55
  1.6 0.0 copy-start
  1.7 0.0 copy-start.1
  1.7 39.4 %all_to_all.30 = bf16[64,4,1024]{2,1,0:T(4,128)(2,1)S(1)} all-to-all(bf16[64,4,1024]{2,1,0:T(4,128)(2,1)S(1)} %shard_map.55), channel_id=1, replica_groups={{0,1,2,3,4,5,6,7,8,9,10,11,12,13,14,15,16,17,18,19,20,21,22,23,24,25,26..., dimensions={0} | all-to-all | bytes 1048576 | tf_op jit(solution)/shard_map/all_to_all | solution.py:17
  41.1 0.1 reshape.24.columns_ref
  41.3 1.5 %shard_map.56 = bf16[256,1024]{1,0:T(8,128)(2,1)} custom-call(bf16[256,1024]{1,0:T(8,128)(2,1)S(1)} %reshape.24.columns_ref, bf16[1024,512]{1,0:T(8,128)(2,1)S(1)} %bitcast.15, bf16[1024,512]{1,0:T(8,128)(2,1)S(1)} %bitcast.17), custom_call_target="tpu_custom_call" | custom-call | flops 536870912 | bytes 2097152 | tf_op jit(solution)/shard_map/pallas_call | solution.py:38
  42.8 4.3 %all-to-all-start.1 = ((bf16[4,64,1024]{2,1,0:T(8,128)(2,1)}), bf16[4,64,1024]{2,1,0:T(8,128)(2,1)S(1)}, u32[]{:S(2)}, u32[]{:S(2)}) async-start(bf16[4,64,1024]{2,1,0:T(8,128)(2,1)} %bitcast.3), calls=%async_computation.1 | async-start | bytes 1048576 | tf_op jit(solution)/shard_map/all_to_all | solution.py:17
  47.1 3.3 %collective-permute-start = (bf16[256,1024]{1,0:T(8,128)(2,1)S(1)}, bf16[256,1024]{1,0:T(8,128)(2,1)S(1)}, u32[]{:S(2)}, u32[]{:S(2)}) collective-permute-start(bf16[256,1024]{1,0:T(8,128)(2,1)S(1)} %reshape.24.columns_ref), channel_id=1, source_target_pairs={{0,64},{1,65},{2,66},{3,67},{4,68},{5,69},{6,70},{7,71},{8,72},{9,... | collective-permute-start | bytes 1572872 | tf_op jit(solution)/shard_map/ppermute | solution.py:23
  50.4 8.8 %collective-permute-done.columns_ref = bf16[256,1024]{1,0:T(8,128)(2,1)S(1)} collective-permute-done((bf16[256,1024]{1,0:T(8,128)(2,1)S(1)}, bf16[256,1024]{1,0:T(8,128)(2,1)S(1)}, u32[]{:S(2)}, u32[]{:S(2)}) %collective-permute-start) | collective-permute-done | bytes 524320 | tf_op jit(solution)/shard_map/ppermute | solution.py:23
  59.2 0.8 copy-done.3
  60.0 0.0 all-to-all-done.1.shares_ref
  60.0 1.0 copy-done.4
  61.1 0.7 shard_map.57
  61.8 0.0 copy-start.2
  61.8 14.0 %all_to_all.31.shares_ref = bf16[4,64,1024]{2,1,0:T(8,128)(2,1)S(1)} all-to-all(bf16[4,64,1024]{2,1,0:T(8,128)(2,1)S(1)} %bitcast.23), channel_id=1, replica_groups={{0,1,2,3},{4,5,6,7},{8,9,10,11},{12,13,14,15},{16,17,18,19},{20,21,22,2..., dimensions={0} | all-to-all | bytes 1048576 | tf_op jit(solution)/shard_map/all_to_all | solution.py:17
  75.8 0.1 shard_map.58
  75.9 11.2 %all_to_all.32 = bf16[4,64,512]{2,1,0:T(8,128)(2,1)S(1)} all-to-all(bf16[4,64,512]{2,1,0:T(8,128)(2,1)S(1)} %shard_map.58), channel_id=1, replica_groups={{0,1,2,3},{4,5,6,7},{8,9,10,11},{12,13,14,15},{16,17,18,19},{20,21,22,2..., dimensions={0} | all-to-all | bytes 524288 | tf_op jit(solution)/shard_map/all_to_all | solution.py:17
  87.1 0.0 copy-done.2
  87.1 0.4 shard_map.59
  87.5 3.3 %collective-permute-start.1 = (bf16[256,1024]{1,0:T(8,128)(2,1)S(1)}, bf16[256,1024]{1,0:T(8,128)(2,1)S(1)}, u32[]{:S(2)}, u32[]{:S(2)}) collective-permute-start(bf16[256,1024]{1,0:T(8,128)(2,1)S(1)} %get-tuple-element.12), channel_id=1, source_target_pairs={{0,64},{1,65},{2,66},{3,67},{4,68},{5,69},{6,70},{7,71},{8,72},{9,... | collective-permute-start | bytes 1572872 | tf_op jit(solution)/shard_map/ppermute | solution.py:23
  90.9 8.6 %all_to_all.33 = bf16[4,64,512]{2,1,0:T(8,128)(2,1)S(1)} all-to-all(bf16[4,64,512]{2,1,0:T(8,128)(2,1)S(1)} %get-tuple-element.11), channel_id=1, replica_groups={{0,1,2,3},{4,5,6,7},{8,9,10,11},{12,13,14,15},{16,17,18,19},{20,21,22,2..., dimensions={0} | all-to-all | bytes 524288 | tf_op jit(solution)/shard_map/all_to_all | solution.py:17
  99.5 0.0 collective-permute-done.1.far_ref
  99.5 0.4 shard_map.60
  99.9 0.2 reshape.29
  100.1 27.5 %all_to_all.34 = bf16[64,4,1024]{2,1,0:T(4,128)(2,1)S(1)} all-to-all(bf16[64,4,1024]{2,1,0:T(4,128)(2,1)S(1)} %reshape.29), channel_id=1, replica_groups={{0,1,2,3,4,5,6,7,8,9,10,11,12,13,14,15,16,17,18,19,20,21,22,23,24,25,26..., dimensions={0} | all-to-all | bytes 1048576 | tf_op jit(solution)/shard_map/all_to_all | solution.py:17
  127.6 0.2 convert_reduce_fusion
  127.8 0.5 copy-done.6
  128.4 10.2 %collective-permute-start.2 = (bf16[4,4096]{1,0:T(4,128)(2,1)S(1)}, bf16[4,4096]{1,0:T(4,128)(2,1)S(1)}, u32[]{:S(2)}, u32[]{:S(2)}) collective-permute-start(bf16[4,4096]{1,0:T(4,128)(2,1)S(1)} %add_convert_fusion), channel_id=1, source_target_pairs={{0,128},{128,256},{256,384},{384,512},{512,640},{640,768},{768,896... | collective-permute-start | bytes 98312 | tf_op jit(solution)/shard_map/ppermute | solution.py:29
  138.7 1.0 collective-permute-done.2
  139.7 0.6 copy.7
  (8 shorter events, 0.0 us)
Async XLA Ops:
  0.0 0.8 copy-start.5
  0.8 0.7 copy-start.7
  1.6 39.6 %copy-start = (bf16[1,1,1024,512]{3,2,1,0:T(8,128)(2,1)S(1)}, bf16[1,1,1024,512]{3,2,1,0:T(8,128)(2,1)}, u32[]{:S(2)}) copy-start(bf16[1,1,1024,512]{3,2,1,0:T(8,128)(2,1)} %param.7) | copy-start | bytes 3145732
  1.7 39.6 %copy-start.1 = (bf16[1,1,1024,512]{3,2,1,0:T(8,128)(2,1)S(1)}, bf16[1,1,1024,512]{3,2,1,0:T(8,128)(2,1)}, u32[]{:S(2)}) copy-start(bf16[1,1,1024,512]{3,2,1,0:T(8,128)(2,1)} %param.8) | copy-start | bytes 3145732
  42.8 17.2 %all-to-all-start.1 = ((bf16[4,64,1024]{2,1,0:T(8,128)(2,1)}), bf16[4,64,1024]{2,1,0:T(8,128)(2,1)S(1)}, u32[]{:S(2)}, u32[]{:S(2)}) async-start(bf16[4,64,1024]{2,1,0:T(8,128)(2,1)} %bitcast.3), calls=%async_computation.1 | async-start | bytes 1048576 | tf_op jit(solution)/shard_map/all_to_all | solution.py:17
  47.1 12.1 %collective-permute-start = (bf16[256,1024]{1,0:T(8,128)(2,1)S(1)}, bf16[256,1024]{1,0:T(8,128)(2,1)S(1)}, u32[]{:S(2)}, u32[]{:S(2)}) collective-permute-start(bf16[256,1024]{1,0:T(8,128)(2,1)S(1)} %reshape.24.columns_ref), channel_id=1, source_target_pairs={{0,64},{1,65},{2,66},{3,67},{4,68},{5,69},{6,70},{7,71},{8,72},{9,... | collective-permute-start | bytes 1572872 | tf_op jit(solution)/shard_map/ppermute | solution.py:23
  59.2 0.8 copy-start.3
  60.0 1.0 copy-start.4
  61.8 25.3 %copy-start.2 = (bf16[1,1,512,1024]{3,2,1,0:T(8,128)(2,1)S(1)}, bf16[1,1,512,1024]{3,2,1,0:T(8,128)(2,1)}, u32[]{:S(2)}) copy-start(bf16[1,1,512,1024]{3,2,1,0:T(8,128)(2,1)} %param.9) | copy-start | bytes 3145732
  87.5 11.9 %collective-permute-start.1 = (bf16[256,1024]{1,0:T(8,128)(2,1)S(1)}, bf16[256,1024]{1,0:T(8,128)(2,1)S(1)}, u32[]{:S(2)}, u32[]{:S(2)}) collective-permute-start(bf16[256,1024]{1,0:T(8,128)(2,1)S(1)} %get-tuple-element.12), channel_id=1, source_target_pairs={{0,64},{1,65},{2,66},{3,67},{4,68},{5,69},{6,70},{7,71},{8,72},{9,... | collective-permute-start | bytes 1572872 | tf_op jit(solution)/shard_map/ppermute | solution.py:23
  127.6 0.8 copy-start.6
  128.4 11.3 %collective-permute-start.2 = (bf16[4,4096]{1,0:T(4,128)(2,1)S(1)}, bf16[4,4096]{1,0:T(4,128)(2,1)S(1)}, u32[]{:S(2)}, u32[]{:S(2)}) collective-permute-start(bf16[4,4096]{1,0:T(4,128)(2,1)S(1)} %add_convert_fusion), channel_id=1, source_target_pairs={{0,128},{128,256},{256,384},{384,512},{512,640},{640,768},{768,896... | collective-permute-start | bytes 98312 | tf_op jit(solution)/shard_map/ppermute | solution.py:29

commit v4 on v2

v4 whole, which is shorter than its diff:
```python
import jax
import jax.numpy as jnp
from jax import lax
from jax.experimental import pallas as pl
from jax.experimental.pallas import tpu as pltpu
from jax.sharding import PartitionSpec as P

f32, bf16 = jnp.float32, jnp.bfloat16


def runs(size):
    count = lax.axis_size("tensor")
    return [list(range(low, low + size)) for low in range(0, count, size)]


def traded(blocks, size):
    return lax.all_to_all(blocks, "tensor", 0, 0, axis_index_groups=runs(size), tiled=True)


def flipped(values, mask):
    count = lax.axis_size("tensor")
    return lax.ppermute(values, "tensor", [(i, i ^ mask) for i in range(count)])


def passed_along(value, mask):
    sections, count = lax.axis_size("section"), lax.axis_size("tensor")
    route = [
        (section * count + place, (section + 1) * count + (place ^ mask))
        for section in range(sections - 1)
        for place in range(count)
    ]
    return lax.ppermute(value, ("section", "tensor"), route)


def dot(left, right):
    return jnp.dot(left, right, preferred_element_type=f32)


def local(body, outs, flops, moved, *operands, scratch=(), after=()):
    spec = pl.BlockSpec(memory_space=pltpu.VMEM)

    def kernel(*refs):
        body(*refs[len(after) :])

    return pl.pallas_call(
        kernel,
        out_shape=[jax.ShapeDtypeStruct(shape, kind) for shape, kind in outs],
        in_specs=[pl.BlockSpec(memory_space=pl.ANY)] * len(after) + [spec] * len(operands),
        out_specs=[spec] * len(outs),
        scratch_shapes=[pltpu.VMEM(shape, kind) for shape, kind in scratch],
        compiler_params=pltpu.CompilerParams(vmem_limit_bytes=24 * 2**20),
        cost_estimate=pl.CostEstimate(flops=flops, bytes_accessed=moved, transcendentals=0),
    )(*after, *operands)


def norm_kernel(acts_ref, gain_ref, out_ref):
    count, _, depth = out_ref.shape
    inputs = acts_ref[...].astype(f32)
    groups = inputs.shape[1] // depth
    scale = lax.rsqrt(jnp.mean(inputs * inputs, axis=-1, keepdims=True) + 1e-05)
    normed = (inputs * scale * gain_ref[...]).astype(bf16)
    for block in range(count):
        low = block % groups * depth
        out_ref[block] = normed[:, low : low + depth]


def rows_of(step, groups, piece):
    member = lax.rem(lax.axis_index("tensor"), groups) ^ step
    return pl.ds(pl.multiple_of(member * piece, piece), piece)


def gate_up_kernel(columns_ref, gate_ref, up_ref, own_ref, *rest):
    *sent_refs, sums_ref = rest
    width = gate_ref.shape[1]
    piece, groups = own_ref.shape[0], len(sent_refs) + 1
    sums_ref[:, :width] = dot(columns_ref[...], gate_ref[...])
    sums_ref[:, width:] = dot(columns_ref[...], up_ref[...])
    own_ref[...] = sums_ref[rows_of(0, groups, piece)]
    for step in range(1, groups):
        sent_refs[step - 1][...] = sums_ref[rows_of(step, groups, piece)].astype(bf16)


def gated_kernel(own_ref, *rest):
    *got_refs, share_ref = rest
    width = share_ref.shape[1]
    total = own_ref[...]
    for got_ref in got_refs:
        total = total + got_ref[...].astype(f32)
    gate = total[:, :width]
    share_ref[...] = (gate / (1.0 + jnp.exp(-gate)) * total[:, width:]).astype(bf16)


def gathered(share_refs, hidden_ref):
    piece, groups = share_refs[0].shape[0], len(share_refs)
    for step in range(groups):
        hidden_ref[rows_of(step, groups, piece)] = share_refs[step][...]
    return hidden_ref[...]


def down_kernel(down_ref, *rest):
    *share_refs, rows_ref, hidden_ref = rest
    rows_ref[...] = dot(gathered(share_refs, hidden_ref), down_ref[...]).astype(bf16)


def down_add_kernel(down_ref, other_ref, *rest):
    *share_refs, rows_ref, hidden_ref = rest
    own = dot(gathered(share_refs, hidden_ref), down_ref[...])
    rows_ref[...] = (own + other_ref[...].astype(f32)).astype(bf16)


def per_device(acts, norm_gain, gate_w, up_w, down_w):
    gate_local, up_local, down_local = gate_w[0, 0], up_w[0, 0], down_w[0, 0]
    tokens, features = acts.shape[1:]
    depth, width = gate_local.shape
    groups_a = features // depth
    near = lax.axis_size("tensor") // 2
    groups_b = near // groups_a
    total = near * tokens
    piece = total // groups_a
    cost = 2 * total * depth * width
    weight = 2 * depth * width

    def partial_sums(columns):
        own, *sent = local(
            gate_up_kernel,
            [((piece, 2 * width), f32)] + [((piece, 2 * width), bf16)] * (groups_a - 1),
            2 * cost,
            2 * weight,
            columns,
            gate_local,
            up_local,
            scratch=[((total, 2 * width), f32)],
        )
        return [own] + [flipped(part, step + 1) for step, part in enumerate(sent)]

    def hidden_shares(parts, after=()):
        shape = (piece, width)
        (share,) = local(gated_kernel, [(shape, bf16)], 0, 2 * total * width, *parts, after=after)
        return [share] + [flipped(share, step) for step in range(1, groups_a)]

    def down(kernel, *operands, after=()):
        (rows,) = local(
            kernel,
            [((total, depth), bf16)],
            cost,
            weight,
            down_local,
            *operands,
            scratch=[((total, width), bf16)],
            after=after,
        )
        return rows

    mirror_acts = flipped(acts[0], near)
    (sent,) = local(
        norm_kernel, [((near, tokens, depth), bf16)], 0, 2 * total * depth, acts[0], norm_gain
    )
    near_columns = traded(sent, near).reshape(total, depth)
    far_columns = flipped(near_columns, near)
    near_parts = partial_sums(near_columns)
    far_parts = partial_sums(far_columns)
    near_hidden = hidden_shares(near_parts, after=far_parts[:1])
    far_hidden = hidden_shares(far_parts)

    mirror_rows = flipped(down(down_kernel, *near_hidden, after=far_parts[1:]), near)
    rows = down(down_add_kernel, mirror_rows, *far_hidden)
    parts = traded(rows.reshape(near, tokens, depth), near)
    parts = parts.reshape(groups_b, groups_a, tokens, depth).astype(f32)
    summed = jnp.transpose(jnp.sum(parts, axis=0), (1, 0, 2)).reshape(tokens, features)
    block = (mirror_acts.astype(f32) + summed).astype(bf16)
    return passed_along(block, near)[None]


def solution(mesh):
    in_specs = (
        P("section", "tensor", None),
        P("section", None),
        P("section", "tensor", None, None),
        P("section", "tensor", None, None),
        P("section", "tensor", None, None),
    )
    out_specs = P("section", "tensor", None)
    return jax.shard_map(
        per_device, mesh=mesh, in_specs=in_specs, out_specs=out_specs, check_vma=False
    )
```

time: 155 us -> 141 us (0.910)
  blocking collectives: 79.9 us -> 39.4 us
  starting transfers between devices: 30.9 us -> 69.3 us
  waiting for transfers between devices: 33.6 us -> 24.3 us
  other arithmetic: 4.01 us -> 0.25 us
  Pallas kernels: 0 us -> 2.76 us
  matrix products: 2.63 us -> 0 us
    all_to_all x3 -> x1, blocking collectives: 79.9 us -> 39.4 us  [traded(): lax.all_to_all(blocks, 'tensor', 0, 0, axis_index_groups=runs(size), tile...]
    ppermute x3 -> x16, starting transfers between devices: 16.2 us -> 56 us  [the longest x15 44.5 us: flipped(): return lax.ppermute(values, 'tensor', [(i, i ^ mask) for i in range(count)])]
    all_to_all x3 -> x1, waiting for transfers between devices: 24.5 us -> 11.1 us  [traded(): lax.all_to_all(blocks, 'tensor', 0, 0, axis_index_groups=runs(size), tile...]
    ppermute x3 -> x16, waiting for transfers between devices: 9.11 us -> 13.2 us  [the longest x15 12.2 us: flipped(): return lax.ppermute(values, 'tensor', [(i, i ^ mask) for i in range(count)])]
    pallas_call x0 -> x7, Pallas kernels: none -> 2.76 us  [local(): pl.pallas_call(kernel, out_shape=[jax.ShapeDtypeStruct(shape, kind) for s...]
    dot_general x6 -> x0, matrix products: 2.63 us -> none  [the longest x2 0.88 us: down_rows(): return jnp.dot(hidden, down_local, preferred_element_type=jnp.float32)]
    concatenate x2 -> x0, other arithmetic: 1.73 us -> none  [hidden_share(): jnp.concatenate([gate.astype(jnp.bfloat16), up_part.astype(jnp.bfloat16)]...]
    all_to_all x3 -> x1, starting transfers between devices: 14.7 us -> 13.2 us  [traded(): lax.all_to_all(blocks, 'tensor', 0, 0, axis_index_groups=runs(size), tile...]
  transfers between devices with their start and end apart: 6 -> 17, of which waited for: 5 -> 6; matrix products, arithmetic and copies ran while one was open for 1% -> 0% of each run, Pallas kernels for 0% -> 1%
where the time goes in v4:
time: 141 us; the launch traced here: 140 us
  starting transfers between devices  69.3 us (49%)
  blocking collectives  39.4 us (28%)
  waiting for transfers between devices  24.3 us (17%)
  local copies, waits for them, and re-layouts  3.23 us (2%)
  Pallas kernels  2.76 us (2%)
    ppermute x15, starting transfers between devices, flipped(): return lax.ppermute(values, 'tensor', [(i, i ^ mask) for i in range(count)])  44.5 us
    all_to_all x1, blocking collectives, traded(): lax.all_to_all(blocks, 'tensor', 0, 0, axis_index_groups=runs(size), tile...  39.4 us
    all_to_all x1, starting transfers between devices, traded(): lax.all_to_all(blocks, 'tensor', 0, 0, axis_index_groups=runs(size), tile...  13.2 us
    ppermute x15, waiting for transfers between devices, flipped(): return lax.ppermute(values, 'tensor', [(i, i ^ mask) for i in range(count)])  12.2 us
    ppermute x1, starting transfers between devices, passed_along(): return lax.ppermute(value, ('section', 'tensor'), route)  11.6 us
    all_to_all x1, waiting for transfers between devices, traded(): lax.all_to_all(blocks, 'tensor', 0, 0, axis_index_groups=runs(size), tile...  11.1 us
  transfers between devices with their start and end apart: 17, of which 6 were waited for; matrix products, arithmetic and copies ran while one was open for 0% of the time, Pallas kernels for 1%

profile of v4, /device:TPU:1, one launch (start us, length us, event | category | flops | bytes accessed | tf_op | source)
XLA Modules:
  0.0 139.6 jit_solution(11360104406593857849)
XLA Ops:
  0.0 0.8 copy-done.3
  0.8 0.7 copy-done.5
  1.7 39.4 %all_to_all.10 = bf16[64,4,1024]{2,1,0:T(4,128)(2,1)S(1)} all-to-all(bf16[64,4,1024]{2,1,0:T(4,128)(2,1)S(1)} %shard_map.55), channel_id=1, replica_groups={{0,1,2,3,4,5,6,7,8,9,10,11,12,13,14,15,16,17,18,19,20,21,22,23,24,25,26..., dimensions={0} | all-to-all | bytes 1048576 | tf_op jit(solution)/shard_map/all_to_all | solution.py:17
  41.2 3.3 %collective-permute-start.1 = (bf16[256,1024]{1,0:T(8,128)(2,1)S(1)}, bf16[256,1024]{1,0:T(8,128)(2,1)S(1)}, u32[]{:S(2)}, u32[]{:S(2)}) collective-permute-start(bf16[256,1024]{1,0:T(8,128)(2,1)S(1)} %reshape.12.refs_0_), channel_id=1, source_target_pairs={{0,64},{1,65},{2,66},{3,67},{4,68},{5,69},{6,70},{7,71},{8,72},{9,... | collective-permute-start | bytes 1572872 | tf_op jit(solution)/shard_map/ppermute | solution.py:22
  44.6 0.8 shard_map.57
  45.4 3.0 %collective-permute-start.5 = (bf16[64,1024]{1,0:T(8,128)(2,1)S(1)}, bf16[64,1024]{1,0:T(8,128)(2,1)S(1)}, u32[]{:S(2)}, u32[]{:S(2)}) collective-permute-start(bf16[64,1024]{1,0:T(8,128)(2,1)S(1)} %get-tuple-element.18), channel_id=1, source_target_pairs={{0,1},{1,0},{2,3},{3,2},{4,5},{5,4},{6,7},{7,6},{8,9},{9,8},{10,11... | collective-permute-start | bytes 393224 | tf_op jit(solution)/shard_map/ppermute | solution.py:22
  48.4 4.2 %collective-permute-start.6 = (bf16[64,1024]{1,0:T(8,128)(2,1)S(1)}, bf16[64,1024]{1,0:T(8,128)(2,1)S(1)}, u32[]{:S(2)}, u32[]{:S(2)}) collective-permute-start(bf16[64,1024]{1,0:T(8,128)(2,1)S(1)} %get-tuple-element.19), channel_id=1, source_target_pairs={{0,2},{1,3},{2,0},{3,1},{4,6},{5,7},{6,4},{7,5},{8,10},{9,11},{10,... | collective-permute-start | bytes 393224 | tf_op jit(solution)/shard_map/ppermute | solution.py:22
  52.5 2.1 %collective-permute-start.7 = (bf16[64,1024]{1,0:T(8,128)(2,1)S(1)}, bf16[64,1024]{1,0:T(8,128)(2,1)S(1)}, u32[]{:S(2)}, u32[]{:S(2)}) collective-permute-start(bf16[64,1024]{1,0:T(8,128)(2,1)S(1)} %get-tuple-element.20), channel_id=1, source_target_pairs={{0,3},{1,2},{2,1},{3,0},{4,7},{5,6},{6,5},{7,4},{8,11},{9,10},{10,... | collective-permute-start | bytes 393224 | tf_op jit(solution)/shard_map/ppermute | solution.py:22
  54.7 0.8 shard_map.56
  55.4 2.1 %collective-permute-start.2 = (bf16[64,1024]{1,0:T(8,128)(2,1)S(1)}, bf16[64,1024]{1,0:T(8,128)(2,1)S(1)}, u32[]{:S(2)}, u32[]{:S(2)}) collective-permute-start(bf16[64,1024]{1,0:T(8,128)(2,1)S(1)} %get-tuple-element.13), channel_id=1, source_target_pairs={{0,1},{1,0},{2,3},{3,2},{4,5},{5,4},{6,7},{7,6},{8,9},{9,8},{10,11... | collective-permute-start | bytes 393224 | tf_op jit(solution)/shard_map/ppermute | solution.py:22
  57.6 4.0 %collective-permute-done.7.refs_4_ = bf16[64,1024]{1,0:T(8,128)(2,1)S(1)} collective-permute-done((bf16[64,1024]{1,0:T(8,128)(2,1)S(1)}, bf16[64,1024]{1,0:T(8,128)(2,1)S(1)}, u32[]{:S(2)}, u32[]{:S(2)}) %collective-permute-start.7) | collective-permute-done | bytes 131104 | tf_op jit(solution)/shard_map/ppermute | solution.py:22
  61.7 1.9 %collective-permute-start.8 = (bf16[64,512]{1,0:T(8,128)(2,1)S(1)}, bf16[64,512]{1,0:T(8,128)(2,1)S(1)}, u32[]{:S(2)}, u32[]{:S(2)}) collective-permute-start(bf16[64,512]{1,0:T(8,128)(2,1)S(1)} %shard_map.58.refs_4_), channel_id=1, source_target_pairs={{0,1},{1,0},{2,3},{3,2},{4,5},{5,4},{6,7},{7,6},{8,9},{9,8},{10,11... | collective-permute-start | bytes 196616 | tf_op jit(solution)/shard_map/ppermute | solution.py:22
  63.6 2.8 %collective-permute-start.3 = (bf16[64,1024]{1,0:T(8,128)(2,1)S(1)}, bf16[64,1024]{1,0:T(8,128)(2,1)S(1)}, u32[]{:S(2)}, u32[]{:S(2)}) collective-permute-start(bf16[64,1024]{1,0:T(8,128)(2,1)S(1)} %get-tuple-element.14), channel_id=1, source_target_pairs={{0,2},{1,3},{2,0},{3,1},{4,6},{5,7},{6,4},{7,5},{8,10},{9,11},{10,... | collective-permute-start | bytes 393224 | tf_op jit(solution)/shard_map/ppermute | solution.py:22
  66.4 4.6 %collective-permute-start.4 = (bf16[64,1024]{1,0:T(8,128)(2,1)S(1)}, bf16[64,1024]{1,0:T(8,128)(2,1)S(1)}, u32[]{:S(2)}, u32[]{:S(2)}) collective-permute-start(bf16[64,1024]{1,0:T(8,128)(2,1)S(1)} %get-tuple-element.15), channel_id=1, source_target_pairs={{0,3},{1,2},{2,1},{3,0},{4,7},{5,6},{6,5},{7,4},{8,11},{9,10},{10,... | collective-permute-start | bytes 393224 | tf_op jit(solution)/shard_map/ppermute | solution.py:22
  71.0 1.9 %collective-permute-start.9 = (bf16[64,512]{1,0:T(8,128)(2,1)S(1)}, bf16[64,512]{1,0:T(8,128)(2,1)S(1)}, u32[]{:S(2)}, u32[]{:S(2)}) collective-permute-start(bf16[64,512]{1,0:T(8,128)(2,1)S(1)} %shard_map.58.refs_4_), channel_id=1, source_target_pairs={{0,2},{1,3},{2,0},{3,1},{4,6},{5,7},{6,4},{7,5},{8,10},{9,11},{10,... | collective-permute-start | bytes 196616 | tf_op jit(solution)/shard_map/ppermute | solution.py:22
  72.9 3.1 %collective-permute-start.10 = (bf16[64,512]{1,0:T(8,128)(2,1)S(1)}, bf16[64,512]{1,0:T(8,128)(2,1)S(1)}, u32[]{:S(2)}, u32[]{:S(2)}) collective-permute-start(bf16[64,512]{1,0:T(8,128)(2,1)S(1)} %shard_map.58.refs_4_), channel_id=1, source_target_pairs={{0,3},{1,2},{2,1},{3,0},{4,7},{5,6},{6,5},{7,4},{8,11},{9,10},{10,... | collective-permute-start | bytes 196616 | tf_op jit(solution)/shard_map/ppermute | solution.py:22
  76.0 5.0 %collective-permute-done.9.refs_6_ = bf16[64,512]{1,0:T(8,128)(2,1)S(1)} collective-permute-done((bf16[64,512]{1,0:T(8,128)(2,1)S(1)}, bf16[64,512]{1,0:T(8,128)(2,1)S(1)}, u32[]{:S(2)}, u32[]{:S(2)}) %collective-permute-start.9) | collective-permute-done | bytes 65568 | tf_op jit(solution)/shard_map/ppermute | solution.py:22
  81.0 0.4 shard_map.59
  81.4 2.0 %collective-permute-start.11 = (bf16[256,1024]{1,0:T(8,128)(2,1)S(1)}, bf16[256,1024]{1,0:T(8,128)(2,1)S(1)}, u32[]{:S(2)}, u32[]{:S(2)}) collective-permute-start(bf16[256,1024]{1,0:T(8,128)(2,1)S(1)} %shard_map.59), channel_id=1, source_target_pairs={{0,64},{1,65},{2,66},{3,67},{4,68},{5,69},{6,70},{7,71},{8,72},{9,... | collective-permute-start | bytes 1572872 | tf_op jit(solution)/shard_map/ppermute | solution.py:22
  83.5 4.3 %collective-permute-start.12 = (bf16[64,512]{1,0:T(8,128)(2,1)S(1)}, bf16[64,512]{1,0:T(8,128)(2,1)S(1)}, u32[]{:S(2)}, u32[]{:S(2)}) collective-permute-start(bf16[64,512]{1,0:T(8,128)(2,1)S(1)} %shard_map.60.refs_2_), channel_id=1, source_target_pairs={{0,1},{1,0},{2,3},{3,2},{4,5},{5,4},{6,7},{7,6},{8,9},{9,8},{10,11... | collective-permute-start | bytes 196616 | tf_op jit(solution)/shard_map/ppermute | solution.py:22
  87.8 2.3 %collective-permute-start.13 = (bf16[64,512]{1,0:T(8,128)(2,1)S(1)}, bf16[64,512]{1,0:T(8,128)(2,1)S(1)}, u32[]{:S(2)}, u32[]{:S(2)}) collective-permute-start(bf16[64,512]{1,0:T(8,128)(2,1)S(1)} %shard_map.60.refs_2_), channel_id=1, source_target_pairs={{0,2},{1,3},{2,0},{3,1},{4,6},{5,7},{6,4},{7,5},{8,10},{9,11},{10,... | collective-permute-start | bytes 196616 | tf_op jit(solution)/shard_map/ppermute | solution.py:22
  90.1 3.6 %collective-permute-start.14 = (bf16[64,512]{1,0:T(8,128)(2,1)S(1)}, bf16[64,512]{1,0:T(8,128)(2,1)S(1)}, u32[]{:S(2)}, u32[]{:S(2)}) collective-permute-start(bf16[64,512]{1,0:T(8,128)(2,1)S(1)} %shard_map.60.refs_2_), channel_id=1, source_target_pairs={{0,3},{1,2},{2,1},{3,0},{4,7},{5,6},{6,5},{7,4},{8,11},{9,10},{10,... | collective-permute-start | bytes 196616 | tf_op jit(solution)/shard_map/ppermute | solution.py:22
  93.7 0.4 collective-permute-done.13.refs_4_
  94.1 2.9 %collective-permute-done.14.refs_5_ = bf16[64,512]{1,0:T(8,128)(2,1)S(1)} collective-permute-done((bf16[64,512]{1,0:T(8,128)(2,1)S(1)}, bf16[64,512]{1,0:T(8,128)(2,1)S(1)}, u32[]{:S(2)}, u32[]{:S(2)}) %collective-permute-start.14) | collective-permute-done | bytes 65568 | tf_op jit(solution)/shard_map/ppermute | solution.py:22
  97.0 0.4 shard_map.61
  97.5 1.0 reshape.13
  98.5 13.2 %all-to-all-start.1 = ((bf16[64,4,1024]{2,1,0:T(4,128)(2,1)}), bf16[64,4,1024]{2,1,0:T(4,128)(2,1)S(1)}, u32[]{:S(2)}, u32[]{:S(2)}) async-start(bf16[64,4,1024]{2,1,0:T(4,128)(2,1)} %reshape.13), calls=%async_computation.1 | async-start | bytes 1048576 | tf_op jit(solution)/shard_map/all_to_all | solution.py:17
  111.7 3.3 %collective-permute-start = (bf16[4,4096]{1,0:T(4,128)(2,1)S(1)}, bf16[4,4096]{1,0:T(4,128)(2,1)S(1)}, u32[]{:S(2)}, u32[]{:S(2)}) collective-permute-start(bf16[4,4096]{1,0:T(4,128)(2,1)S(1)} %bitcast.17), channel_id=1, source_target_pairs={{0,64},{1,65},{2,66},{3,67},{4,68},{5,69},{6,70},{7,71},{8,72},{9,... | collective-permute-start | bytes 98312 | tf_op jit(solution)/shard_map/ppermute | solution.py:22
  115.0 11.1 %all-to-all-done.1 = bf16[64,4,1024]{2,1,0:T(4,128)(2,1)S(1)} async-done(((bf16[64,4,1024]{2,1,0:T(4,128)(2,1)}), bf16[64,4,1024]{2,1,0:T(4,128)(2,1)S(1)}, u32[]{:S(2)}, u32[]{:S(2)}) %all-to-all-start.1) | async-done | bytes 524320 | tf_op jit(solution)/shard_map/all_to_all | solution.py:17
  126.4 11.6 %collective-permute-start.15 = (bf16[4,4096]{1,0:T(4,128)(2,1)S(1)}, bf16[4,4096]{1,0:T(4,128)(2,1)S(1)}, u32[]{:S(2)}, u32[]{:S(2)}) collective-permute-start(bf16[4,4096]{1,0:T(4,128)(2,1)S(1)} %add_convert_fusion), channel_id=1, source_target_pairs={{0,192},{1,193},{2,194},{3,195},{4,196},{5,197},{6,198},{7,199},{8... | collective-permute-start | bytes 98312 | tf_op jit(solution)/shard_map/ppermute | solution.py:32
  138.0 1.0 collective-permute-done.15
  139.0 0.6 copy.7
  (27 shorter events, 0.8 us)
Async XLA Ops:
  0.0 0.8 copy-start.3
  0.8 0.7 copy-start.5
  1.6 42.9 %copy-start = (bf16[1,1,1024,512]{3,2,1,0:T(8,128)(2,1)S(1)}, bf16[1,1,1024,512]{3,2,1,0:T(8,128)(2,1)}, u32[]{:S(2)}) copy-start(bf16[1,1,1024,512]{3,2,1,0:T(8,128)(2,1)} %param.7) | copy-start | bytes 3145732
  1.7 42.9 %copy-start.1 = (bf16[1,1,1024,512]{3,2,1,0:T(8,128)(2,1)S(1)}, bf16[1,1,1024,512]{3,2,1,0:T(8,128)(2,1)}, u32[]{:S(2)}) copy-start(bf16[1,1,1024,512]{3,2,1,0:T(8,128)(2,1)} %param.8) | copy-start | bytes 3145732
  41.2 13.4 %collective-permute-start.1 = (bf16[256,1024]{1,0:T(8,128)(2,1)S(1)}, bf16[256,1024]{1,0:T(8,128)(2,1)S(1)}, u32[]{:S(2)}, u32[]{:S(2)}) collective-permute-start(bf16[256,1024]{1,0:T(8,128)(2,1)S(1)} %reshape.12.refs_0_), channel_id=1, source_target_pairs={{0,64},{1,65},{2,66},{3,67},{4,68},{5,69},{6,70},{7,71},{8,72},{9,... | collective-permute-start | bytes 1572872 | tf_op jit(solution)/shard_map/ppermute | solution.py:22
  45.4 12.2 %collective-permute-start.5 = (bf16[64,1024]{1,0:T(8,128)(2,1)S(1)}, bf16[64,1024]{1,0:T(8,128)(2,1)S(1)}, u32[]{:S(2)}, u32[]{:S(2)}) collective-permute-start(bf16[64,1024]{1,0:T(8,128)(2,1)S(1)} %get-tuple-element.18), channel_id=1, source_target_pairs={{0,1},{1,0},{2,3},{3,2},{4,5},{5,4},{6,7},{7,6},{8,9},{9,8},{10,11... | collective-permute-start | bytes 393224 | tf_op jit(solution)/shard_map/ppermute | solution.py:22
  48.4 9.2 %collective-permute-start.6 = (bf16[64,1024]{1,0:T(8,128)(2,1)S(1)}, bf16[64,1024]{1,0:T(8,128)(2,1)S(1)}, u32[]{:S(2)}, u32[]{:S(2)}) collective-permute-start(bf16[64,1024]{1,0:T(8,128)(2,1)S(1)} %get-tuple-element.19), channel_id=1, source_target_pairs={{0,2},{1,3},{2,0},{3,1},{4,6},{5,7},{6,4},{7,5},{8,10},{9,11},{10,... | collective-permute-start | bytes 393224 | tf_op jit(solution)/shard_map/ppermute | solution.py:22
  52.5 9.0 %collective-permute-start.7 = (bf16[64,1024]{1,0:T(8,128)(2,1)S(1)}, bf16[64,1024]{1,0:T(8,128)(2,1)S(1)}, u32[]{:S(2)}, u32[]{:S(2)}) collective-permute-start(bf16[64,1024]{1,0:T(8,128)(2,1)S(1)} %get-tuple-element.20), channel_id=1, source_target_pairs={{0,3},{1,2},{2,1},{3,0},{4,7},{5,6},{6,5},{7,4},{8,11},{9,10},{10,... | collective-permute-start | bytes 393224 | tf_op jit(solution)/shard_map/ppermute | solution.py:22
  54.7 26.3 %copy-start.2 = (bf16[1,1,512,1024]{3,2,1,0:T(8,128)(2,1)S(1)}, bf16[1,1,512,1024]{3,2,1,0:T(8,128)(2,1)}, u32[]{:S(2)}) copy-start(bf16[1,1,512,1024]{3,2,1,0:T(8,128)(2,1)} %param.9) | copy-start | bytes 3145732
  55.4 25.5 %collective-permute-start.2 = (bf16[64,1024]{1,0:T(8,128)(2,1)S(1)}, bf16[64,1024]{1,0:T(8,128)(2,1)S(1)}, u32[]{:S(2)}, u32[]{:S(2)}) collective-permute-start(bf16[64,1024]{1,0:T(8,128)(2,1)S(1)} %get-tuple-element.13), channel_id=1, source_target_pairs={{0,1},{1,0},{2,3},{3,2},{4,5},{5,4},{6,7},{7,6},{8,9},{9,8},{10,11... | collective-permute-start | bytes 393224 | tf_op jit(solution)/shard_map/ppermute | solution.py:22
  61.7 11.2 %collective-permute-start.8 = (bf16[64,512]{1,0:T(8,128)(2,1)S(1)}, bf16[64,512]{1,0:T(8,128)(2,1)S(1)}, u32[]{:S(2)}, u32[]{:S(2)}) collective-permute-start(bf16[64,512]{1,0:T(8,128)(2,1)S(1)} %shard_map.58.refs_4_), channel_id=1, source_target_pairs={{0,1},{1,0},{2,3},{3,2},{4,5},{5,4},{6,7},{7,6},{8,9},{9,8},{10,11... | collective-permute-start | bytes 196616 | tf_op jit(solution)/shard_map/ppermute | solution.py:22
  63.6 17.4 %collective-permute-start.3 = (bf16[64,1024]{1,0:T(8,128)(2,1)S(1)}, bf16[64,1024]{1,0:T(8,128)(2,1)S(1)}, u32[]{:S(2)}, u32[]{:S(2)}) collective-permute-start(bf16[64,1024]{1,0:T(8,128)(2,1)S(1)} %get-tuple-element.14), channel_id=1, source_target_pairs={{0,2},{1,3},{2,0},{3,1},{4,6},{5,7},{6,4},{7,5},{8,10},{9,11},{10,... | collective-permute-start | bytes 393224 | tf_op jit(solution)/shard_map/ppermute | solution.py:22
  66.4 14.6 %collective-permute-start.4 = (bf16[64,1024]{1,0:T(8,128)(2,1)S(1)}, bf16[64,1024]{1,0:T(8,128)(2,1)S(1)}, u32[]{:S(2)}, u32[]{:S(2)}) collective-permute-start(bf16[64,1024]{1,0:T(8,128)(2,1)S(1)} %get-tuple-element.15), channel_id=1, source_target_pairs={{0,3},{1,2},{2,1},{3,0},{4,7},{5,6},{6,5},{7,4},{8,11},{9,10},{10,... | collective-permute-start | bytes 393224 | tf_op jit(solution)/shard_map/ppermute | solution.py:22
  71.0 10.0 %collective-permute-start.9 = (bf16[64,512]{1,0:T(8,128)(2,1)S(1)}, bf16[64,512]{1,0:T(8,128)(2,1)S(1)}, u32[]{:S(2)}, u32[]{:S(2)}) collective-permute-start(bf16[64,512]{1,0:T(8,128)(2,1)S(1)} %shard_map.58.refs_4_), channel_id=1, source_target_pairs={{0,2},{1,3},{2,0},{3,1},{4,6},{5,7},{6,4},{7,5},{8,10},{9,11},{10,... | collective-permute-start | bytes 196616 | tf_op jit(solution)/shard_map/ppermute | solution.py:22
  72.9 8.1 %collective-permute-start.10 = (bf16[64,512]{1,0:T(8,128)(2,1)S(1)}, bf16[64,512]{1,0:T(8,128)(2,1)S(1)}, u32[]{:S(2)}, u32[]{:S(2)}) collective-permute-start(bf16[64,512]{1,0:T(8,128)(2,1)S(1)} %shard_map.58.refs_4_), channel_id=1, source_target_pairs={{0,3},{1,2},{2,1},{3,0},{4,7},{5,6},{6,5},{7,4},{8,11},{9,10},{10,... | collective-permute-start | bytes 196616 | tf_op jit(solution)/shard_map/ppermute | solution.py:22
  81.4 15.6 %collective-permute-start.11 = (bf16[256,1024]{1,0:T(8,128)(2,1)S(1)}, bf16[256,1024]{1,0:T(8,128)(2,1)S(1)}, u32[]{:S(2)}, u32[]{:S(2)}) collective-permute-start(bf16[256,1024]{1,0:T(8,128)(2,1)S(1)} %shard_map.59), channel_id=1, source_target_pairs={{0,64},{1,65},{2,66},{3,67},{4,68},{5,69},{6,70},{7,71},{8,72},{9,... | collective-permute-start | bytes 1572872 | tf_op jit(solution)/shard_map/ppermute | solution.py:22
  83.5 10.2 %collective-permute-start.12 = (bf16[64,512]{1,0:T(8,128)(2,1)S(1)}, bf16[64,512]{1,0:T(8,128)(2,1)S(1)}, u32[]{:S(2)}, u32[]{:S(2)}) collective-permute-start(bf16[64,512]{1,0:T(8,128)(2,1)S(1)} %shard_map.60.refs_2_), channel_id=1, source_target_pairs={{0,1},{1,0},{2,3},{3,2},{4,5},{5,4},{6,7},{7,6},{8,9},{9,8},{10,11... | collective-permute-start | bytes 196616 | tf_op jit(solution)/shard_map/ppermute | solution.py:22
  87.8 6.3 %collective-permute-start.13 = (bf16[64,512]{1,0:T(8,128)(2,1)S(1)}, bf16[64,512]{1,0:T(8,128)(2,1)S(1)}, u32[]{:S(2)}, u32[]{:S(2)}) collective-permute-start(bf16[64,512]{1,0:T(8,128)(2,1)S(1)} %shard_map.60.refs_2_), channel_id=1, source_target_pairs={{0,2},{1,3},{2,0},{3,1},{4,6},{5,7},{6,4},{7,5},{8,10},{9,11},{10,... | collective-permute-start | bytes 196616 | tf_op jit(solution)/shard_map/ppermute | solution.py:22
  90.1 6.9 %collective-permute-start.14 = (bf16[64,512]{1,0:T(8,128)(2,1)S(1)}, bf16[64,512]{1,0:T(8,128)(2,1)S(1)}, u32[]{:S(2)}, u32[]{:S(2)}) collective-permute-start(bf16[64,512]{1,0:T(8,128)(2,1)S(1)} %shard_map.60.refs_2_), channel_id=1, source_target_pairs={{0,3},{1,2},{2,1},{3,0},{4,7},{5,6},{6,5},{7,4},{8,11},{9,10},{10,... | collective-permute-start | bytes 196616 | tf_op jit(solution)/shard_map/ppermute | solution.py:22
  98.5 13.2 %copy-start.4 = (bf16[1,4,4096]{2,1,0:T(4,128)(2,1)S(1)}, bf16[1,4,4096]{2,1,0:T(4,128)(2,1)}, u32[]{:S(2)}) copy-start(bf16[1,4,4096]{2,1,0:T(4,128)(2,1)} %param.5) | copy-start | bytes 98308
  98.5 27.7 %all-to-all-start.1 = ((bf16[64,4,1024]{2,1,0:T(4,128)(2,1)}), bf16[64,4,1024]{2,1,0:T(4,128)(2,1)S(1)}, u32[]{:S(2)}, u32[]{:S(2)}) async-start(bf16[64,4,1024]{2,1,0:T(4,128)(2,1)} %reshape.13), calls=%async_computation.1 | async-start | bytes 1048576 | tf_op jit(solution)/shard_map/all_to_all | solution.py:17
  111.7 14.7 %collective-permute-start = (bf16[4,4096]{1,0:T(4,128)(2,1)S(1)}, bf16[4,4096]{1,0:T(4,128)(2,1)S(1)}, u32[]{:S(2)}, u32[]{:S(2)}) collective-permute-start(bf16[4,4096]{1,0:T(4,128)(2,1)S(1)} %bitcast.17), channel_id=1, source_target_pairs={{0,64},{1,65},{2,66},{3,67},{4,68},{5,69},{6,70},{7,71},{8,72},{9,... | collective-permute-start | bytes 98312 | tf_op jit(solution)/shard_map/ppermute | solution.py:22
  126.4 12.6 %collective-permute-start.15 = (bf16[4,4096]{1,0:T(4,128)(2,1)S(1)}, bf16[4,4096]{1,0:T(4,128)(2,1)S(1)}, u32[]{:S(2)}, u32[]{:S(2)}) collective-permute-start(bf16[4,4096]{1,0:T(4,128)(2,1)S(1)} %add_convert_fusion), channel_id=1, source_target_pairs={{0,192},{1,193},{2,194},{3,195},{4,196},{5,197},{6,198},{7,199},{8... | collective-permute-start | bytes 98312 | tf_op jit(solution)/shard_map/ppermute | solution.py:32

commit v5 on v3

v5 whole, which is shorter than its diff:
```python
import jax
import jax.numpy as jnp
from jax import lax
from jax.experimental import pallas as pl
from jax.experimental.pallas import tpu as pltpu
from jax.sharding import PartitionSpec as P

f32, bf16 = jnp.float32, jnp.bfloat16


def runs(size):
    count = lax.axis_size("tensor")
    return [list(range(low, low + size)) for low in range(0, count, size)]


def traded(blocks, size):
    return lax.all_to_all(blocks, "tensor", 0, 0, axis_index_groups=runs(size), tiled=True)


def flipped(values, mask):
    count = lax.axis_size("tensor")
    return lax.ppermute(values, "tensor", [(i, i ^ mask) for i in range(count)])


def passed_along(value, mask):
    sections, count = lax.axis_size("section"), lax.axis_size("tensor")
    route = [
        (section * count + place, (section + 1) * count + (place ^ mask))
        for section in range(sections - 1)
        for place in range(count)
    ]
    return lax.ppermute(value, ("section", "tensor"), route)


def dot(left, right):
    return jnp.dot(left, right, preferred_element_type=f32)


def local(body, outs, flops, moved, *operands):
    spec = pl.BlockSpec(memory_space=pltpu.VMEM)
    return pl.pallas_call(
        body,
        out_shape=[jax.ShapeDtypeStruct(shape, bf16) for shape in outs],
        in_specs=[spec] * len(operands),
        out_specs=[spec] * len(outs),
        compiler_params=pltpu.CompilerParams(vmem_limit_bytes=24 * 2**20),
        cost_estimate=pl.CostEstimate(flops=flops, bytes_accessed=moved, transcendentals=0),
    )(*operands)


def norm_kernel(acts_ref, gain_ref, out_ref):
    count, _, depth = out_ref.shape
    inputs = acts_ref[...].astype(f32)
    groups = inputs.shape[1] // depth
    scale = lax.rsqrt(jnp.mean(inputs * inputs, axis=-1, keepdims=True) + 1e-05)
    normed = (inputs * scale * gain_ref[...]).astype(bf16)
    for block in range(count):
        low = block % groups * depth
        out_ref[block] = normed[:, low : low + depth]


def gate_up(columns_ref, gate_ref, up_ref, out_ref):
    width = gate_ref.shape[1]
    out_ref[:, :width] = dot(columns_ref[...], gate_ref[...]).astype(bf16)
    out_ref[:, width : 2 * width] = dot(columns_ref[...], up_ref[...]).astype(bf16)


def gated(shares_ref, width):
    total = shares_ref[0, :, : 2 * width].astype(f32)
    for part in range(1, shares_ref.shape[0]):
        total = total + shares_ref[part, :, : 2 * width].astype(f32)
    gate = total[:, :width]
    return (gate / (1.0 + jnp.exp(-gate)) * total[:, width:]).astype(bf16)


def near_share_kernel(shares_ref, share_ref):
    share_ref[...] = gated(shares_ref, share_ref.shape[1])


def far_sums_near_share(columns_ref, share_ref, gate_ref, up_ref, out_ref):
    piece, width = share_ref.shape
    gate_up(columns_ref, gate_ref, up_ref, out_ref)
    for low in range(0, out_ref.shape[0], piece):
        out_ref[low : low + piece, 2 * width :] = share_ref[...]


def near_down_far_share(got_ref, down_ref, rows_ref, spread_ref):
    groups, piece, _ = got_ref.shape
    width = down_ref.shape[0]
    hidden = got_ref[:, :, 2 * width :].reshape(groups * piece, width)
    rows_ref[...] = dot(hidden, down_ref[...]).astype(bf16)
    share = gated(got_ref, width)
    for part in range(groups):
        spread_ref[part] = share


def far_down(hidden_ref, down_ref, other_ref, rows_ref):
    own = dot(hidden_ref[...], down_ref[...])
    rows_ref[...] = (own + other_ref[...].astype(f32)).astype(bf16)


def per_device(acts, norm_gain, gate_w, up_w, down_w):
    gate_local, up_local, down_local = gate_w[0, 0], up_w[0, 0], down_w[0, 0]
    tokens, features = acts.shape[1:]
    depth, width = gate_local.shape
    groups_a = features // depth
    near = lax.axis_size("tensor") // 2
    groups_b = near // groups_a
    total = near * tokens
    piece = total // groups_a
    cost = 2 * total * depth * width
    weight = 2 * depth * width

    mirror_acts = flipped(acts[0], near)
    (sent,) = local(norm_kernel, [(near, tokens, depth)], 0, 2 * total * depth, acts[0], norm_gain)
    near_columns = traded(sent, near).reshape(total, depth)
    far_columns = flipped(near_columns, near)

    (sums,) = local(
        gate_up, [(total, 2 * width)], 2 * cost, 2 * weight, near_columns, gate_local, up_local
    )
    shares = traded(sums.reshape(groups_a, piece, 2 * width), groups_a)
    (near_share,) = local(near_share_kernel, [(piece, width)], 0, 2 * total * width, shares)
    (sums,) = local(
        far_sums_near_share,
        [(total, 3 * width)],
        2 * cost,
        2 * weight,
        far_columns,
        near_share,
        gate_local,
        up_local,
    )
    got = traded(sums.reshape(groups_a, piece, 3 * width), groups_a)
    near_rows, spread = local(
        near_down_far_share,
        [(total, depth), (groups_a, piece, width)],
        cost,
        weight,
        got,
        down_local,
    )

    mirror_rows = flipped(near_rows, near)
    hidden = traded(spread, groups_a).reshape(total, width)
    (rows,) = local(far_down, [(total, depth)], cost, weight, hidden, down_local, mirror_rows)
    parts = traded(rows.reshape(near, tokens, depth), near)
    parts = parts.reshape(groups_b, groups_a, tokens, depth).astype(f32)
    summed = jnp.transpose(jnp.sum(parts, axis=0), (1, 0, 2)).reshape(tokens, features)
    block = (mirror_acts.astype(f32) + summed).astype(bf16)
    return passed_along(block, near)[None]


def solution(mesh):
    in_specs = (
        P("section", "tensor", None),
        P("section", None),
        P("section", "tensor", None, None),
        P("section", "tensor", None, None),
        P("section", "tensor", None, None),
    )
    out_specs = P("section", "tensor", None)
    return jax.shard_map(
        per_device, mesh=mesh, in_specs=in_specs, out_specs=out_specs, check_vma=False
    )
```

time: 141 us -> 137 us (0.972)
  blocking collectives: 101 us -> 70.4 us
  starting transfers between devices: 21.2 us -> 36.3 us
  waiting for transfers between devices: 9.8 us -> 21.7 us
    all_to_all x5 -> x3, blocking collectives: 101 us -> 70.4 us  [traded(): lax.all_to_all(blocks, 'tensor', 0, 0, axis_index_groups=runs(size), tile...]
    all_to_all x1 -> x2, waiting for transfers between devices: 0.01 us -> 19 us  [traded(): lax.all_to_all(blocks, 'tensor', 0, 0, axis_index_groups=runs(size), tile...]
    all_to_all x1 -> x2, starting transfers between devices: 4.33 us -> 15 us  [traded(): lax.all_to_all(blocks, 'tensor', 0, 0, axis_index_groups=runs(size), tile...]
    ppermute x3 -> x4, waiting for transfers between devices: 9.8 us -> 2.72 us  [the longest x3 1.71 us: flipped(): return lax.ppermute(values, 'tensor', [(i, i ^ mask) for i in range(count)])]
    ppermute x3 -> x4, starting transfers between devices: 16.9 us -> 21.3 us  [the longest x1 11.4 us: passed_along(): return lax.ppermute(value, ('section', 'tensor'), route)]
    unnamed x17 -> x15, local copies, waits for them, and re-layouts: 4.48 us -> 2.89 us
  transfers between devices with their start and end apart: 4 -> 6, of which waited for: 2 -> 5; matrix products, arithmetic and copies ran while one was open for 0% -> 0% of each run, Pallas kernels for 0% -> 0%
where the time goes in v5:
time: 137 us
  blocking collectives  70.4 us (51%)
  starting transfers between devices  36.3 us (26%)
  waiting for transfers between devices  21.7 us (16%)
  local copies, waits for them, and re-layouts  4.01 us (3%)
  Pallas kernels  3.63 us (3%)
    all_to_all x3, blocking collectives, traded(): lax.all_to_all(blocks, 'tensor', 0, 0, axis_index_groups=runs(size), tile...  70.4 us
    all_to_all x2, waiting for transfers between devices, traded(): lax.all_to_all(blocks, 'tensor', 0, 0, axis_index_groups=runs(size), tile...  19 us
    all_to_all x2, starting transfers between devices, traded(): lax.all_to_all(blocks, 'tensor', 0, 0, axis_index_groups=runs(size), tile...  15 us
    ppermute x1, starting transfers between devices, passed_along(): return lax.ppermute(value, ('section', 'tensor'), route)  11.4 us
    ppermute x3, starting transfers between devices, flipped(): return lax.ppermute(values, 'tensor', [(i, i ^ mask) for i in range(count)])  9.95 us
    pallas_call x6, Pallas kernels, local(): pl.pallas_call(body, out_shape=[jax.ShapeDtypeStruct(shape, bf16) for sha...  3.63 us
    unnamed x15, local copies, waits for them, and re-layouts  2.89 us
  transfers between devices with their start and end apart: 6, of which 5 were waited for; matrix products, arithmetic and copies ran while one was open for 0% of the time, Pallas kernels for 0%

profile of v5, /device:TPU:1, one launch (start us, length us, event | category | flops | bytes accessed | tf_op | source)
XLA Modules:
  0.0 136.5 jit_solution(17118054698840445764)
XLA Ops:
  0.0 0.8 copy-done.4
  0.8 0.7 copy-done.6
  1.5 0.2 shard_map.55
  1.6 0.0 copy-start
  1.7 0.0 copy-start.1
  1.7 39.4 %all_to_all.25 = bf16[64,4,1024]{2,1,0:T(4,128)(2,1)S(1)} all-to-all(bf16[64,4,1024]{2,1,0:T(4,128)(2,1)S(1)} %shard_map.55), channel_id=1, replica_groups={{0,1,2,3,4,5,6,7,8,9,10,11,12,13,14,15,16,17,18,19,20,21,22,23,24,25,26..., dimensions={0} | all-to-all | bytes 1048576 | tf_op jit(solution)/shard_map/all_to_all | solution.py:17
  41.1 0.1 reshape.21.columns_ref
  41.3 0.7 shard_map.56
  42.0 0.0 copy-start.3
  42.0 0.8 copy-done.3
  42.8 4.3 %all-to-all-start.1 = ((bf16[4,64,1024]{2,1,0:T(8,128)(2,1)}), bf16[4,64,1024]{2,1,0:T(8,128)(2,1)S(1)}, u32[]{:S(2)}, u32[]{:S(2)}) async-start(bf16[4,64,1024]{2,1,0:T(8,128)(2,1)} %bitcast.20), calls=%async_computation.1 | async-start | bytes 1048576 | tf_op jit(solution)/shard_map/all_to_all | solution.py:17
  47.1 3.3 %collective-permute-start.1 = (bf16[256,1024]{1,0:T(8,128)(2,1)S(1)}, bf16[256,1024]{1,0:T(8,128)(2,1)}, u32[]{:S(2)}, u32[]{:S(2)}) collective-permute-start(bf16[256,1024]{1,0:T(8,128)(2,1)S(1)} %reshape.21.columns_ref), channel_id=1, source_target_pairs={{0,64},{1,65},{2,66},{3,67},{4,68},{5,69},{6,70},{7,71},{8,72},{9,... | collective-permute-start | bytes 1572872 | tf_op jit(solution)/shard_map/ppermute | solution.py:22
  50.4 7.7 %all-to-all-done.1.shares_ref = bf16[4,64,1024]{2,1,0:T(8,128)(2,1)S(1)} async-done(((bf16[4,64,1024]{2,1,0:T(8,128)(2,1)}), bf16[4,64,1024]{2,1,0:T(8,128)(2,1)S(1)}, u32[]{:S(2)}, u32[]{:S(2)}) %all-to-all-start.1) | async-done | bytes 524320 | tf_op jit(solution)/shard_map/all_to_all | solution.py:17
  58.1 0.1 shard_map.57.share_ref
  58.2 1.1 collective-permute-done.1.columns_ref
  59.3 1.8 %shard_map.58 = bf16[256,1536]{1,0:T(8,128)(2,1)S(1)} custom-call(bf16[256,1024]{1,0:T(8,128)(2,1)} %collective-permute-done.1.columns_ref, bf16[64,512]{1,0:T(8,128)(2,1)S(1)} %shard_map.57.share_ref, bf16[1024,512]{1,0:T(8,128)(2,1)S(1)} %bitcast.14, bf16[1024,512]{1,0:T(8,128)(2,1)S(1)} %bitcast.16), custom_call_target="tpu_custom_call" | custom-call | flops 536870912 | bytes 2097152 | tf_op jit(solution)/shard_map/pallas_call | solution.py:41
  61.1 0.0 copy-start.2
  61.1 22.4 %all_to_all.26.got_ref = bf16[4,64,1536]{2,1,0:T(8,128)(2,1)S(1)} all-to-all(bf16[4,64,1536]{2,1,0:T(8,128)(2,1)S(1)} %bitcast.19), channel_id=1, replica_groups={{0,1,2,3},{4,5,6,7},{8,9,10,11},{12,13,14,15},{16,17,18,19},{20,21,22,2..., dimensions={0} | all-to-all | bytes 1572864 | tf_op jit(solution)/shard_map/all_to_all | solution.py:17
  83.5 0.5 shard_map.59
  84.0 3.3 %collective-permute-start.2 = (bf16[256,1024]{1,0:T(8,128)(2,1)S(1)}, bf16[256,1024]{1,0:T(8,128)(2,1)S(1)}, u32[]{:S(2)}, u32[]{:S(2)}) collective-permute-start(bf16[256,1024]{1,0:T(8,128)(2,1)S(1)} %get-tuple-element.8), channel_id=1, source_target_pairs={{0,64},{1,65},{2,66},{3,67},{4,68},{5,69},{6,70},{7,71},{8,72},{9,... | collective-permute-start | bytes 1572872 | tf_op jit(solution)/shard_map/ppermute | solution.py:22
  87.3 8.5 %all_to_all.27 = bf16[4,64,512]{2,1,0:T(8,128)(2,1)S(1)} all-to-all(bf16[4,64,512]{2,1,0:T(8,128)(2,1)S(1)} %get-tuple-element.7), channel_id=1, replica_groups={{0,1,2,3},{4,5,6,7},{8,9,10,11},{12,13,14,15},{16,17,18,19},{20,21,22,2..., dimensions={0} | all-to-all | bytes 524288 | tf_op jit(solution)/shard_map/all_to_all | solution.py:17
  95.9 0.6 collective-permute-done.2.other_ref
  96.5 0.4 shard_map.60
  97.0 1.0 reshape.25
  98.0 10.7 %all-to-all-start.4 = ((bf16[64,4,1024]{2,1,0:T(4,128)(2,1)}), bf16[64,4,1024]{2,1,0:T(4,128)(2,1)S(1)}, u32[]{:S(2)}, u32[]{:S(2)}) async-start(bf16[64,4,1024]{2,1,0:T(4,128)(2,1)} %reshape.25), calls=%async_computation.4 | async-start | bytes 1048576 | tf_op jit(solution)/shard_map/all_to_all | solution.py:17
  108.6 3.3 %collective-permute-start = (bf16[4,4096]{1,0:T(4,128)(2,1)S(1)}, bf16[4,4096]{1,0:T(4,128)(2,1)S(1)}, u32[]{:S(2)}, u32[]{:S(2)}) collective-permute-start(bf16[4,4096]{1,0:T(4,128)(2,1)S(1)} %bitcast.23), channel_id=1, source_target_pairs={{0,64},{1,65},{2,66},{3,67},{4,68},{5,69},{6,70},{7,71},{8,72},{9,... | collective-permute-start | bytes 98312 | tf_op jit(solution)/shard_map/ppermute | solution.py:22
  112.0 11.3 %all-to-all-done.4 = bf16[64,4,1024]{2,1,0:T(4,128)(2,1)S(1)} async-done(((bf16[64,4,1024]{2,1,0:T(4,128)(2,1)}), bf16[64,4,1024]{2,1,0:T(4,128)(2,1)S(1)}, u32[]{:S(2)}, u32[]{:S(2)}) %all-to-all-start.4) | async-done | bytes 524320 | tf_op jit(solution)/shard_map/all_to_all | solution.py:17
  123.3 0.2 convert_reduce_fusion
  123.5 0.0 collective-permute-done
  123.5 11.4 %collective-permute-start.3 = (bf16[4,4096]{1,0:T(4,128)(2,1)S(1)}, bf16[4,4096]{1,0:T(4,128)(2,1)S(1)}, u32[]{:S(2)}, u32[]{:S(2)}) collective-permute-start(bf16[4,4096]{1,0:T(4,128)(2,1)S(1)} %add_convert_fusion), channel_id=1, source_target_pairs={{0,192},{1,193},{2,194},{3,195},{4,196},{5,197},{6,198},{7,199},{8... | collective-permute-start | bytes 98312 | tf_op jit(solution)/shard_map/ppermute | solution.py:32
  134.9 1.0 collective-permute-done.3
  135.9 0.6 copy.7
  (8 shorter events, 0.0 us)
Async XLA Ops:
  0.0 0.8 copy-start.4
  0.8 0.7 copy-start.6
  1.6 39.6 %copy-start = (bf16[1,1,1024,512]{3,2,1,0:T(8,128)(2,1)S(1)}, bf16[1,1,1024,512]{3,2,1,0:T(8,128)(2,1)}, u32[]{:S(2)}) copy-start(bf16[1,1,1024,512]{3,2,1,0:T(8,128)(2,1)} %param.7) | copy-start | bytes 3145732
  1.7 39.6 %copy-start.1 = (bf16[1,1,1024,512]{3,2,1,0:T(8,128)(2,1)S(1)}, bf16[1,1,1024,512]{3,2,1,0:T(8,128)(2,1)}, u32[]{:S(2)}) copy-start(bf16[1,1,1024,512]{3,2,1,0:T(8,128)(2,1)} %param.8) | copy-start | bytes 3145732
  42.0 0.8 copy-start.3
  42.8 15.4 %all-to-all-start.1 = ((bf16[4,64,1024]{2,1,0:T(8,128)(2,1)}), bf16[4,64,1024]{2,1,0:T(8,128)(2,1)S(1)}, u32[]{:S(2)}, u32[]{:S(2)}) async-start(bf16[4,64,1024]{2,1,0:T(8,128)(2,1)} %bitcast.20), calls=%async_computation.1 | async-start | bytes 1048576 | tf_op jit(solution)/shard_map/all_to_all | solution.py:17
  47.1 12.2 %collective-permute-start.1 = (bf16[256,1024]{1,0:T(8,128)(2,1)S(1)}, bf16[256,1024]{1,0:T(8,128)(2,1)}, u32[]{:S(2)}, u32[]{:S(2)}) collective-permute-start(bf16[256,1024]{1,0:T(8,128)(2,1)S(1)} %reshape.21.columns_ref), channel_id=1, source_target_pairs={{0,64},{1,65},{2,66},{3,67},{4,68},{5,69},{6,70},{7,71},{8,72},{9,... | collective-permute-start | bytes 1572872 | tf_op jit(solution)/shard_map/ppermute | solution.py:22
  61.1 22.5 %copy-start.2 = (bf16[1,1,512,1024]{3,2,1,0:T(8,128)(2,1)S(1)}, bf16[1,1,512,1024]{3,2,1,0:T(8,128)(2,1)}, u32[]{:S(2)}) copy-start(bf16[1,1,512,1024]{3,2,1,0:T(8,128)(2,1)} %param.9) | copy-start | bytes 3145732
  84.0 12.5 %collective-permute-start.2 = (bf16[256,1024]{1,0:T(8,128)(2,1)S(1)}, bf16[256,1024]{1,0:T(8,128)(2,1)S(1)}, u32[]{:S(2)}, u32[]{:S(2)}) collective-permute-start(bf16[256,1024]{1,0:T(8,128)(2,1)S(1)} %get-tuple-element.8), channel_id=1, source_target_pairs={{0,64},{1,65},{2,66},{3,67},{4,68},{5,69},{6,70},{7,71},{8,72},{9,... | collective-permute-start | bytes 1572872 | tf_op jit(solution)/shard_map/ppermute | solution.py:22
  98.0 10.7 %copy-start.5 = (bf16[1,4,4096]{2,1,0:T(4,128)(2,1)S(1)}, bf16[1,4,4096]{2,1,0:T(4,128)(2,1)}, u32[]{:S(2)}) copy-start(bf16[1,4,4096]{2,1,0:T(4,128)(2,1)} %param.5) | copy-start | bytes 98308
  98.0 25.3 %all-to-all-start.4 = ((bf16[64,4,1024]{2,1,0:T(4,128)(2,1)}), bf16[64,4,1024]{2,1,0:T(4,128)(2,1)S(1)}, u32[]{:S(2)}, u32[]{:S(2)}) async-start(bf16[64,4,1024]{2,1,0:T(4,128)(2,1)} %reshape.25), calls=%async_computation.4 | async-start | bytes 1048576 | tf_op jit(solution)/shard_map/all_to_all | solution.py:17
  108.6 14.9 %collective-permute-start = (bf16[4,4096]{1,0:T(4,128)(2,1)S(1)}, bf16[4,4096]{1,0:T(4,128)(2,1)S(1)}, u32[]{:S(2)}, u32[]{:S(2)}) collective-permute-start(bf16[4,4096]{1,0:T(4,128)(2,1)S(1)} %bitcast.23), channel_id=1, source_target_pairs={{0,64},{1,65},{2,66},{3,67},{4,68},{5,69},{6,70},{7,71},{8,72},{9,... | collective-permute-start | bytes 98312 | tf_op jit(solution)/shard_map/ppermute | solution.py:22
  123.5 12.4 %collective-permute-start.3 = (bf16[4,4096]{1,0:T(4,128)(2,1)S(1)}, bf16[4,4096]{1,0:T(4,128)(2,1)S(1)}, u32[]{:S(2)}, u32[]{:S(2)}) collective-permute-start(bf16[4,4096]{1,0:T(4,128)(2,1)S(1)} %add_convert_fusion), channel_id=1, source_target_pairs={{0,192},{1,193},{2,194},{3,195},{4,196},{5,197},{6,198},{7,199},{8... | collective-permute-start | bytes 98312 | tf_op jit(solution)/shard_map/ppermute | solution.py:32

commit v6 on v5

--- a/solution.py
+++ b/solution.py
@@ -13,8 +13,17 @@
     return [list(range(low, low + size)) for low in range(0, count, size)]
 
 
-def traded(blocks, size):
-    return lax.all_to_all(blocks, "tensor", 0, 0, axis_index_groups=runs(size), tiled=True)
+def every_other(run, size):
+    count = lax.axis_size("tensor")
+    return [
+        [low + place for place in range(run) if place // size % 2 == half]
+        for low in range(0, count, run)
+        for half in range(2)
+    ]
+
+
+def traded(blocks, groups):
+    return lax.all_to_all(blocks, "tensor", 0, 0, axis_index_groups=groups, tiled=True)
 
 
 def flipped(values, mask):
@@ -40,7 +49,7 @@
     spec = pl.BlockSpec(memory_space=pltpu.VMEM)
     return pl.pallas_call(
         body,
-        out_shape=[jax.ShapeDtypeStruct(shape, bf16) for shape in outs],
+        out_shape=[jax.ShapeDtypeStruct(shape, kind) for shape, kind in outs],
         in_specs=[spec] * len(operands),
         out_specs=[spec] * len(outs),
         compiler_params=pltpu.CompilerParams(vmem_limit_bytes=24 * 2**20),
@@ -48,10 +57,12 @@
     )(*operands)
 
 
-def norm_kernel(acts_ref, gain_ref, out_ref):
+def norm_kernel(acts_ref, gain_ref, out_ref, rows_ref):
     count, _, depth = out_ref.shape
     inputs = acts_ref[...].astype(f32)
     groups = inputs.shape[1] // depth
+    blocks = [inputs[:, low : low + depth] for low in range(0, groups * depth, depth)]
+    rows_ref[...] = jnp.concatenate(blocks, axis=0).astype(bf16)
     scale = lax.rsqrt(jnp.mean(inputs * inputs, axis=-1, keepdims=True) + 1e-05)
     normed = (inputs * scale * gain_ref[...]).astype(bf16)
     for block in range(count):
@@ -60,9 +71,26 @@
 
 
 def gate_up(columns_ref, gate_ref, up_ref, out_ref):
-    width = gate_ref.shape[1]
-    out_ref[:, :width] = dot(columns_ref[...], gate_ref[...]).astype(bf16)
-    out_ref[:, width : 2 * width] = dot(columns_ref[...], up_ref[...]).astype(bf16)
+    total, width = out_ref.shape[0], gate_ref.shape[1]
+    out_ref[:, :width] = dot(columns_ref[:total], gate_ref[...]).astype(bf16)
+    out_ref[:, width : 2 * width] = dot(columns_ref[:total], up_ref[...]).astype(bf16)
+
+
+def ordered_gate_up(got_ref, acts_ref, gate_ref, up_ref, columns_ref, out_ref):
+    count, tokens, _ = got_ref.shape
+    groups = acts_ref.shape[0] // tokens
+    places = [
+        low + member + half * groups
+        for low in range(0, count, 2 * groups)
+        for member in range(groups)
+        for half in range(2)
+    ]
+    for start in range(0, count, 4):
+        pieces = [got_ref[place].astype(f32) for place in places[start : start + 4]]
+        rows = slice(start * tokens, (start + 4) * tokens)
+        columns_ref[rows] = jnp.concatenate(pieces, axis=0).astype(bf16)
+    columns_ref[count * tokens :] = acts_ref[...]
+    gate_up(columns_ref, gate_ref, up_ref, out_ref)
 
 
 def gated(shares_ref, width):
@@ -99,31 +127,61 @@
     rows_ref[...] = (own + other_ref[...].astype(f32)).astype(bf16)
 
 
+def finish(parts_ref, far_ref, own_ref, other_ref):
+    tokens, features = own_ref.shape
+    depth = parts_ref.shape[2]
+    groups = features // depth
+    upper = lax.axis_index("tensor") // groups % 2
+    acts = far_ref[far_ref.shape[0] - tokens * groups :].astype(f32)
+    for block in range(groups):
+        total = parts_ref[block].astype(f32)
+        for part in range(block + groups, parts_ref.shape[0], groups):
+            total = total + parts_ref[part].astype(f32)
+        low, high = total[:tokens], total[tokens:]
+        columns = slice(block * depth, (block + 1) * depth)
+        residual = acts[block * tokens : (block + 1) * tokens]
+        own_ref[:, columns] = residual + jnp.where(upper == 0, low, high)
+        other_ref[:, columns] = jnp.where(upper == 0, high, low)
+
+
 def per_device(acts, norm_gain, gate_w, up_w, down_w):
     gate_local, up_local, down_local = gate_w[0, 0], up_w[0, 0], down_w[0, 0]
     tokens, features = acts.shape[1:]
     depth, width = gate_local.shape
     groups_a = features // depth
     near = lax.axis_size("tensor") // 2
-    groups_b = near // groups_a
     total = near * tokens
     piece = total // groups_a
     cost = 2 * total * depth * width
     weight = 2 * depth * width
-
-    mirror_acts = flipped(acts[0], near)
-    (sent,) = local(norm_kernel, [(near, tokens, depth)], 0, 2 * total * depth, acts[0], norm_gain)
-    near_columns = traded(sent, near).reshape(total, depth)
+    quads = runs(groups_a)
+
+    sent, acts_rows = local(
+        norm_kernel,
+        [((near, tokens, depth), bf16), ((groups_a * tokens, depth), bf16)],
+        0,
+        2 * total * depth,
+        acts[0],
+        norm_gain,
+    )
+    near_columns, sums = local(
+        ordered_gate_up,
+        [((total + groups_a * tokens, depth), bf16), ((total, 2 * width), bf16)],
+        2 * cost,
+        2 * weight,
+        traded(sent, runs(near)),
+        acts_rows,
+        gate_local,
+        up_local,
+    )
     far_columns = flipped(near_columns, near)
-
-    (sums,) = local(
-        gate_up, [(total, 2 * width)], 2 * cost, 2 * weight, near_columns, gate_local, up_local
-    )
-    shares = traded(sums.reshape(groups_a, piece, 2 * width), groups_a)
-    (near_share,) = local(near_share_kernel, [(piece, width)], 0, 2 * total * width, shares)
+    shares = traded(sums.reshape(groups_a, piece, 2 * width), quads)
+    (near_share,) = local(
+        near_share_kernel, [((piece, width), bf16)], 0, 2 * total * width, shares
+    )
     (sums,) = local(
         far_sums_near_share,
-        [(total, 3 * width)],
+        [((total, 3 * width), bf16)],
         2 * cost,
         2 * weight,
         far_columns,
@@ -131,10 +189,10 @@
         gate_local,
         up_local,
     )
-    got = traded(sums.reshape(groups_a, piece, 3 * width), groups_a)
+    got = traded(sums.reshape(groups_a, piece, 3 * width), quads)
     near_rows, spread = local(
         near_down_far_share,
-        [(total, depth), (groups_a, piece, width)],
+        [((total, depth), bf16), ((groups_a, piece, width), bf16)],
         cost,
         weight,
         got,
@@ -142,13 +200,17 @@
     )
 
     mirror_rows = flipped(near_rows, near)
-    hidden = traded(spread, groups_a).reshape(total, width)
-    (rows,) = local(far_down, [(total, depth)], cost, weight, hidden, down_local, mirror_rows)
-    parts = traded(rows.reshape(near, tokens, depth), near)
-    parts = parts.reshape(groups_b, groups_a, tokens, depth).astype(f32)
-    summed = jnp.transpose(jnp.sum(parts, axis=0), (1, 0, 2)).reshape(tokens, features)
-    block = (mirror_acts.astype(f32) + summed).astype(bf16)
-    return passed_along(block, near)[None]
+    hidden = traded(spread, quads).reshape(total, width)
+    (rows,) = local(
+        far_down, [((total, depth), bf16)], cost, weight, hidden, down_local, mirror_rows
+    )
+    rows = rows.reshape(near // 2, 2 * tokens, depth)
+    parts = traded(rows, every_other(near, groups_a))
+    own, other = local(
+        finish, [((tokens, features), f32)] * 2, 0, 2 * total * depth, parts, far_columns
+    )
+    block = passed_along(own, near) + passed_along(other, near ^ groups_a)
+    return block.astype(bf16)[None]
 
 
 def solution(mesh):

time: 137 us -> 146 us (1.066)
  blocking collectives: 70.4 us -> 94.5 us
  starting transfers between devices: 36.3 us -> 24.8 us
  waiting for transfers between devices: 21.7 us -> 17.9 us
    all_to_all x3 -> x4, blocking collectives: 70.4 us -> 94.5 us  [traded(): lax.all_to_all(blocks, 'tensor', 0, 0, axis_index_groups=groups, tiled=True)]
    all_to_all x2 -> x1, waiting for transfers between devices: 19 us -> 7.72 us  [traded(): lax.all_to_all(blocks, 'tensor', 0, 0, axis_index_groups=groups, tiled=True)]
    all_to_all x2 -> x1, starting transfers between devices: 15 us -> 4.46 us  [traded(): lax.all_to_all(blocks, 'tensor', 0, 0, axis_index_groups=groups, tiled=True)]
    ppermute x1 -> x2, waiting for transfers between devices: 1 us -> 7.7 us  [passed_along(): return lax.ppermute(value, ('section', 'tensor'), route)]
    ppermute x3 -> x2, starting transfers between devices: 9.95 us -> 6.62 us  [flipped(): return lax.ppermute(values, 'tensor', [(i, i ^ mask) for i in range(count)])]
    ppermute x1 -> x2, starting transfers between devices: 11.4 us -> 13.7 us  [passed_along(): return lax.ppermute(value, ('section', 'tensor'), route)]
    unnamed x15 -> x14, local copies, waits for them, and re-layouts: 2.89 us -> 3.61 us
    pallas_call x6 -> x7, Pallas kernels: 3.63 us -> 3.51 us  [local(): pl.pallas_call(body, out_shape=[jax.ShapeDtypeStruct(shape, kind) for sha...]
  transfers between devices with their start and end apart: 6 -> 5, of which waited for: 5 -> 4; matrix products, arithmetic and copies ran while one was open for 0% -> 0% of each run, Pallas kernels for 0% -> 0%
where the time goes in v6:
time: 146 us; the launch traced here: 145 us
  blocking collectives  94.5 us (65%)
  starting transfers between devices  24.8 us (17%)
  waiting for transfers between devices  17.9 us (12%)
  local copies, waits for them, and re-layouts  3.61 us (2%)
  Pallas kernels  3.51 us (2%)
    all_to_all x4, blocking collectives, traded(): lax.all_to_all(blocks, 'tensor', 0, 0, axis_index_groups=groups, tiled=True)  94.5 us
    ppermute x2, starting transfers between devices, passed_along(): return lax.ppermute(value, ('section', 'tensor'), route)  13.7 us
    all_to_all x1, waiting for transfers between devices, traded(): lax.all_to_all(blocks, 'tensor', 0, 0, axis_index_groups=groups, tiled=True)  7.72 us
    ppermute x2, waiting for transfers between devices, passed_along(): return lax.ppermute(value, ('section', 'tensor'), route)  7.7 us
    ppermute x2, starting transfers between devices, flipped(): return lax.ppermute(values, 'tensor', [(i, i ^ mask) for i in range(count)])  6.62 us
    all_to_all x1, starting transfers between devices, traded(): lax.all_to_all(blocks, 'tensor', 0, 0, axis_index_groups=groups, tiled=True)  4.46 us
    unnamed x14, local copies, waits for them, and re-layouts  3.61 us
    pallas_call x7, Pallas kernels, local(): pl.pallas_call(body, out_shape=[jax.ShapeDtypeStruct(shape, kind) for sha...  3.51 us
  transfers between devices with their start and end apart: 5, of which 4 were waited for; matrix products, arithmetic and copies ran while one was open for 0% of the time, Pallas kernels for 0%

profile of v6, /device:TPU:1, one launch (start us, length us, event | category | flops | bytes accessed | tf_op | source)
XLA Modules:
  0.0 145.1 jit_solution(3787313753977570962)
XLA Ops:
  0.0 0.0 copy-start.1
  0.0 0.0 copy-start.4
  0.0 0.8 copy-done.4
  0.9 0.7 copy-done.5
  1.6 0.2 shard_map.55
  1.7 39.3 %all_to_all.25.got_ref = bf16[64,4,1024]{2,1,0:T(4,128)(2,1)S(1)} all-to-all(bf16[64,4,1024]{2,1,0:T(4,128)(2,1)S(1)} %get-tuple-element.13), channel_id=1, replica_groups={{0,1,2,3,4,5,6,7,8,9,10,11,12,13,14,15,16,17,18,19,20,21,22,23,24,25,26..., dimensions={0} | all-to-all | bytes 1048576 | tf_op jit(solution)/shard_map/all_to_all | solution.py:26
  41.1 0.0 copy-done.1
  41.1 1.2 copy-done.2
  42.3 1.5 %shard_map.56 = (bf16[272,1024]{1,0:T(8,128)(2,1)S(1)}, bf16[256,1024]{1,0:T(8,128)(2,1)}) custom-call(bf16[64,4,1024]{2,1,0:T(4,128)(2,1)S(1)} %all_to_all.25.got_ref, bf16[16,1024]{1,0:T(8,128)(2,1)S(1)} %get-tuple-element.14.acts_ref, bf16[1024,512]{1,0:T(8,128)(2,1)S(1)} %bitcast.12, bf16[1024,512]{1,0:T(8,128)(2,1)S(1)} %bitcast.14), custom_call_target="tpu_custom_call" | custom-call | flops 536870912 | bytes 2097152 | tf_op jit(solution)/shard_map/pallas_call | solution.py:50
  43.8 0.8 copy-done.6
  44.6 4.5 %all-to-all-start.1 = ((bf16[4,64,1024]{2,1,0:T(8,128)(2,1)}), bf16[4,64,1024]{2,1,0:T(8,128)(2,1)S(1)}, u32[]{:S(2)}, u32[]{:S(2)}) async-start(bf16[4,64,1024]{2,1,0:T(8,128)(2,1)} %bitcast.3), calls=%async_computation.1 | async-start | bytes 1048576 | tf_op jit(solution)/shard_map/all_to_all | solution.py:26
  49.1 3.3 %collective-permute-start = (bf16[272,1024]{1,0:T(8,128)(2,1)}, bf16[272,1024]{1,0:T(8,128)(2,1)S(1)}, u32[]{:S(2)}, u32[]{:S(2)}) collective-permute-start(bf16[272,1024]{1,0:T(8,128)(2,1)} %copy-done.6), channel_id=1, source_target_pairs={{0,64},{1,65},{2,66},{3,67},{4,68},{5,69},{6,70},{7,71},{8,72},{9,... | collective-permute-start | bytes 1671176 | tf_op jit(solution)/shard_map/ppermute | solution.py:31
  52.4 7.7 %all-to-all-done.1.shares_ref = bf16[4,64,1024]{2,1,0:T(8,128)(2,1)S(1)} async-done(((bf16[4,64,1024]{2,1,0:T(8,128)(2,1)}), bf16[4,64,1024]{2,1,0:T(8,128)(2,1)S(1)}, u32[]{:S(2)}, u32[]{:S(2)}) %all-to-all-start.1) | async-done | bytes 524320 | tf_op jit(solution)/shard_map/all_to_all | solution.py:26
  60.1 0.1 shard_map.57.share_ref
  60.2 1.9 %collective-permute-done.columns_ref.far_ref = bf16[272,1024]{1,0:T(8,128)(2,1)S(1)} collective-permute-done((bf16[272,1024]{1,0:T(8,128)(2,1)}, bf16[272,1024]{1,0:T(8,128)(2,1)S(1)}, u32[]{:S(2)}, u32[]{:S(2)}) %collective-permute-start) | collective-permute-done | bytes 557088 | tf_op jit(solution)/shard_map/ppermute | solution.py:31
  62.1 0.0 copy-done.3
  62.1 0.7 shard_map.58
  62.8 0.0 copy-start
  62.8 22.4 %all_to_all.26.got_ref = bf16[4,64,1536]{2,1,0:T(8,128)(2,1)S(1)} all-to-all(bf16[4,64,1536]{2,1,0:T(8,128)(2,1)S(1)} %bitcast.16), channel_id=1, replica_groups={{0,1,2,3},{4,5,6,7},{8,9,10,11},{12,13,14,15},{16,17,18,19},{20,21,22,2..., dimensions={0} | all-to-all | bytes 1572864 | tf_op jit(solution)/shard_map/all_to_all | solution.py:26
  85.3 0.0 copy-done
  85.3 0.5 shard_map.59
  85.8 3.3 %collective-permute-start.1 = (bf16[256,1024]{1,0:T(8,128)(2,1)S(1)}, bf16[256,1024]{1,0:T(8,128)(2,1)S(1)}, u32[]{:S(2)}, u32[]{:S(2)}) collective-permute-start(bf16[256,1024]{1,0:T(8,128)(2,1)S(1)} %get-tuple-element.18), channel_id=1, source_target_pairs={{0,64},{1,65},{2,66},{3,67},{4,68},{5,69},{6,70},{7,71},{8,72},{9,... | collective-permute-start | bytes 1572872 | tf_op jit(solution)/shard_map/ppermute | solution.py:31
  89.1 8.5 %all_to_all.27 = bf16[4,64,512]{2,1,0:T(8,128)(2,1)S(1)} all-to-all(bf16[4,64,512]{2,1,0:T(8,128)(2,1)S(1)} %get-tuple-element.17), channel_id=1, replica_groups={{0,1,2,3},{4,5,6,7},{8,9,10,11},{12,13,14,15},{16,17,18,19},{20,21,22,2..., dimensions={0} | all-to-all | bytes 524288 | tf_op jit(solution)/shard_map/all_to_all | solution.py:26
  97.6 0.6 collective-permute-done.1.other_ref
  98.3 0.4 shard_map.60
  98.7 24.2 %all_to_all.28.parts_ref = bf16[32,8,1024]{2,1,0:T(8,128)(2,1)S(1)} all-to-all(bf16[32,8,1024]{2,1,0:T(8,128)(2,1)S(1)} %bitcast.17), channel_id=1, replica_groups={{0,1,2,3,8,9,10,11,16,17,18,19,24,25,26,27,32,33,34,35,40,41,42,43,48,4..., dimensions={0} | all-to-all | bytes 1048576 | tf_op jit(solution)/shard_map/all_to_all | solution.py:26
  123.0 0.1 shard_map.61
  123.0 10.5 %collective-permute-start.2 = (f32[4,4096]{1,0:T(4,128)S(1)}, f32[4,4096]{1,0:T(4,128)S(1)}, u32[]{:S(2)}, u32[]{:S(2)}) collective-permute-start(f32[4,4096]{1,0:T(4,128)S(1)} %get-tuple-element.19), channel_id=1, source_target_pairs={{0,192},{1,193},{2,194},{3,195},{4,196},{5,197},{6,198},{7,199},{8... | collective-permute-start | bytes 196616 | tf_op jit(solution)/shard_map/ppermute | solution.py:41
  133.6 3.2 %collective-permute-start.3 = (f32[4,4096]{1,0:T(4,128)S(1)}, f32[4,4096]{1,0:T(4,128)S(1)}, u32[]{:S(2)}, u32[]{:S(2)}) collective-permute-start(f32[4,4096]{1,0:T(4,128)S(1)} %get-tuple-element.20), channel_id=1, source_target_pairs={{0,196},{1,197},{2,198},{3,199},{4,192},{5,193},{6,194},{7,195},{8... | collective-permute-start | bytes 196616 | tf_op jit(solution)/shard_map/ppermute | solution.py:41
  136.8 0.0 collective-permute-done.2
  136.8 7.7 %collective-permute-done.3 = f32[4,4096]{1,0:T(4,128)S(1)} collective-permute-done((f32[4,4096]{1,0:T(4,128)S(1)}, f32[4,4096]{1,0:T(4,128)S(1)}, u32[]{:S(2)}, u32[]{:S(2)}) %collective-permute-start.3) | collective-permute-done | bytes 65568 | tf_op jit(solution)/shard_map/ppermute | solution.py:41
  144.5 0.6 fusion
  (4 shorter events, 0.0 us)
Async XLA Ops:
  0.0 41.1 %copy-start.1 = (bf16[1,1,1024,512]{3,2,1,0:T(8,128)(2,1)S(1)}, bf16[1,1,1024,512]{3,2,1,0:T(8,128)(2,1)}, u32[]{:S(2)}) copy-start(bf16[1,1,1024,512]{3,2,1,0:T(8,128)(2,1)} %param.7) | copy-start | bytes 3145732
  0.0 0.8 copy-start.4
  0.8 0.7 copy-start.5
  41.1 1.2 copy-start.2
  43.8 0.8 copy-start.6
  44.6 17.5 %copy-start.3 = (bf16[1,1,1024,512]{3,2,1,0:T(8,128)(2,1)S(1)}, bf16[1,1,1024,512]{3,2,1,0:T(8,128)(2,1)}, u32[]{:S(2)}) copy-start(bf16[1,1,1024,512]{3,2,1,0:T(8,128)(2,1)} %param.8) | copy-start | bytes 3145732
  44.6 15.5 %all-to-all-start.1 = ((bf16[4,64,1024]{2,1,0:T(8,128)(2,1)}), bf16[4,64,1024]{2,1,0:T(8,128)(2,1)S(1)}, u32[]{:S(2)}, u32[]{:S(2)}) async-start(bf16[4,64,1024]{2,1,0:T(8,128)(2,1)} %bitcast.3), calls=%async_computation.1 | async-start | bytes 1048576 | tf_op jit(solution)/shard_map/all_to_all | solution.py:26
  49.1 13.0 %collective-permute-start = (bf16[272,1024]{1,0:T(8,128)(2,1)}, bf16[272,1024]{1,0:T(8,128)(2,1)S(1)}, u32[]{:S(2)}, u32[]{:S(2)}) collective-permute-start(bf16[272,1024]{1,0:T(8,128)(2,1)} %copy-done.6), channel_id=1, source_target_pairs={{0,64},{1,65},{2,66},{3,67},{4,68},{5,69},{6,70},{7,71},{8,72},{9,... | collective-permute-start | bytes 1671176 | tf_op jit(solution)/shard_map/ppermute | solution.py:31
  62.8 22.5 %copy-start = (bf16[1,1,512,1024]{3,2,1,0:T(8,128)(2,1)S(1)}, bf16[1,1,512,1024]{3,2,1,0:T(8,128)(2,1)}, u32[]{:S(2)}) copy-start(bf16[1,1,512,1024]{3,2,1,0:T(8,128)(2,1)} %param.9) | copy-start | bytes 3145732
  85.8 12.5 %collective-permute-start.1 = (bf16[256,1024]{1,0:T(8,128)(2,1)S(1)}, bf16[256,1024]{1,0:T(8,128)(2,1)S(1)}, u32[]{:S(2)}, u32[]{:S(2)}) collective-permute-start(bf16[256,1024]{1,0:T(8,128)(2,1)S(1)} %get-tuple-element.18), channel_id=1, source_target_pairs={{0,64},{1,65},{2,66},{3,67},{4,68},{5,69},{6,70},{7,71},{8,72},{9,... | collective-permute-start | bytes 1572872 | tf_op jit(solution)/shard_map/ppermute | solution.py:31
  123.0 13.8 %collective-permute-start.2 = (f32[4,4096]{1,0:T(4,128)S(1)}, f32[4,4096]{1,0:T(4,128)S(1)}, u32[]{:S(2)}, u32[]{:S(2)}) collective-permute-start(f32[4,4096]{1,0:T(4,128)S(1)} %get-tuple-element.19), channel_id=1, source_target_pairs={{0,192},{1,193},{2,194},{3,195},{4,196},{5,197},{6,198},{7,199},{8... | collective-permute-start | bytes 196616 | tf_op jit(solution)/shard_map/ppermute | solution.py:41
  133.6 10.9 %collective-permute-start.3 = (f32[4,4096]{1,0:T(4,128)S(1)}, f32[4,4096]{1,0:T(4,128)S(1)}, u32[]{:S(2)}, u32[]{:S(2)}) collective-permute-start(f32[4,4096]{1,0:T(4,128)S(1)} %get-tuple-element.20), channel_id=1, source_target_pairs={{0,196},{1,197},{2,198},{3,199},{4,192},{5,193},{6,194},{7,195},{8... | collective-permute-start | bytes 196616 | tf_op jit(solution)/shard_map/ppermute | solution.py:41

commit v7 on v5

--- a/solution.py
+++ b/solution.py
@@ -36,21 +36,33 @@
     return jnp.dot(left, right, preferred_element_type=f32)
 
 
-def local(body, outs, flops, moved, *operands):
-    spec = pl.BlockSpec(memory_space=pltpu.VMEM)
+def local(body, outs, flops, moved, *operands, after=(), scratch=(), fetches=False):
+    spec = pl.BlockSpec(memory_space=pl.ANY if fetches else pltpu.VMEM)
+    limit = (56 if fetches else 24) * 2**20
+
+    def kernel(*refs):
+        body(*refs[len(after) :])
+
     return pl.pallas_call(
-        body,
+        kernel,
         out_shape=[jax.ShapeDtypeStruct(shape, bf16) for shape in outs],
-        in_specs=[spec] * len(operands),
-        out_specs=[spec] * len(outs),
-        compiler_params=pltpu.CompilerParams(vmem_limit_bytes=24 * 2**20),
+        in_specs=[pl.BlockSpec(memory_space=pl.ANY)] * len(after) + [spec] * len(operands),
+        out_specs=[pl.BlockSpec(memory_space=pltpu.VMEM)] * len(outs),
+        scratch_shapes=scratch,
+        compiler_params=pltpu.CompilerParams(vmem_limit_bytes=limit),
         cost_estimate=pl.CostEstimate(flops=flops, bytes_accessed=moved, transcendentals=0),
-    )(*operands)
+    )(*after, *operands)
 
 
-def norm_kernel(acts_ref, gain_ref, out_ref):
+def norm_kernel(acts_hbm, gain_hbm, out_ref, acts_ref, gain_ref, acts_sem, gain_sem):
+    acts_copy = pltpu.make_async_copy(acts_hbm, acts_ref, acts_sem)
+    gain_copy = pltpu.make_async_copy(gain_hbm, gain_ref, gain_sem)
+    acts_copy.start()
+    gain_copy.start()
     count, _, depth = out_ref.shape
-    inputs = acts_ref[...].astype(f32)
+    acts_copy.wait()
+    gain_copy.wait()
+    inputs = acts_ref[0].astype(f32)
     groups = inputs.shape[1] // depth
     scale = lax.rsqrt(jnp.mean(inputs * inputs, axis=-1, keepdims=True) + 1e-05)
     normed = (inputs * scale * gain_ref[...]).astype(bf16)
@@ -112,12 +124,33 @@
     weight = 2 * depth * width
 
     mirror_acts = flipped(acts[0], near)
-    (sent,) = local(norm_kernel, [(near, tokens, depth)], 0, 2 * total * depth, acts[0], norm_gain)
+    (sent,) = local(
+        norm_kernel,
+        [(near, tokens, depth)],
+        0,
+        2 * total * depth,
+        acts,
+        norm_gain,
+        scratch=[
+            pltpu.VMEM(acts.shape, bf16),
+            pltpu.VMEM(norm_gain.shape, f32),
+            pltpu.SemaphoreType.DMA,
+            pltpu.SemaphoreType.DMA,
+        ],
+        fetches=True,
+    )
     near_columns = traded(sent, near).reshape(total, depth)
     far_columns = flipped(near_columns, near)
 
     (sums,) = local(
-        gate_up, [(total, 2 * width)], 2 * cost, 2 * weight, near_columns, gate_local, up_local
+        gate_up,
+        [(total, 2 * width)],
+        2 * cost,
+        2 * weight,
+        near_columns,
+        gate_local,
+        up_local,
+        after=(mirror_acts,),
     )
     shares = traded(sums.reshape(groups_a, piece, 2 * width), groups_a)
     (near_share,) = local(near_share_kernel, [(piece, width)], 0, 2 * total * width, shares)
@@ -148,7 +181,7 @@
     parts = parts.reshape(groups_b, groups_a, tokens, depth).astype(f32)
     summed = jnp.transpose(jnp.sum(parts, axis=0), (1, 0, 2)).reshape(tokens, features)
     block = (mirror_acts.astype(f32) + summed).astype(bf16)
-    return passed_along(block, near)[None]
+    return passed_along(block[None], near)
 
 
 def solution(mesh):

time: 137 us -> 137 us (level)
  blocking collectives: 70.4 us -> 56 us
  starting transfers between devices: 36.3 us -> 48.9 us
  local copies, waits for them, and re-layouts: 4.01 us -> 0.95 us
  Pallas kernels: 3.63 us -> 6.07 us
  waiting for transfers between devices: 21.7 us -> 23.4 us
    all_to_all x3, blocking collectives: 70.4 us -> 56 us  [traded(): lax.all_to_all(blocks, 'tensor', 0, 0, axis_index_groups=runs(size), tile...]
    all_to_all x2, starting transfers between devices: 15 us -> 27.6 us  [traded(): lax.all_to_all(blocks, 'tensor', 0, 0, axis_index_groups=runs(size), tile...]
    pallas_call x6, Pallas kernels: 3.63 us -> 6.07 us  [local(): pl.pallas_call(kernel, out_shape=[jax.ShapeDtypeStruct(shape, bf16) for s...]
    unnamed x15 -> x9, local copies, waits for them, and re-layouts: 2.89 us -> 0.64 us
    all_to_all x2, waiting for transfers between devices: 19 us -> 20.7 us  [traded(): lax.all_to_all(blocks, 'tensor', 0, 0, axis_index_groups=runs(size), tile...]
where the time goes in v7:
time: 137 us; the launch traced here: 136 us
  blocking collectives  56 us (41%)
  starting transfers between devices  48.9 us (36%)
  waiting for transfers between devices  23.4 us (17%)
  Pallas kernels  6.07 us (4%)
    all_to_all x3, blocking collectives, traded(): lax.all_to_all(blocks, 'tensor', 0, 0, axis_index_groups=runs(size), tile...  56 us
    all_to_all x2, starting transfers between devices, traded(): lax.all_to_all(blocks, 'tensor', 0, 0, axis_index_groups=runs(size), tile...  27.6 us
    all_to_all x2, waiting for transfers between devices, traded(): lax.all_to_all(blocks, 'tensor', 0, 0, axis_index_groups=runs(size), tile...  20.7 us
    ppermute x1, starting transfers between devices, passed_along(): return lax.ppermute(value, ('section', 'tensor'), route)  11.4 us
    ppermute x3, starting transfers between devices, flipped(): return lax.ppermute(values, 'tensor', [(i, i ^ mask) for i in range(count)])  9.94 us
    pallas_call x6, Pallas kernels, local(): pl.pallas_call(kernel, out_shape=[jax.ShapeDtypeStruct(shape, bf16) for s...  6.07 us
  transfers between devices with their start and end apart: 6, of which 5 were waited for; matrix products, arithmetic and copies ran while one was open for 0% of the time, Pallas kernels for 0%

profile of v7, /device:TPU:1, one launch (start us, length us, event | category | flops | bytes accessed | tf_op | source)
XLA Modules:
  0.0 135.8 jit_solution(16054554256610614345)
XLA Ops:
  0.0 1.8 %shard_map.55 = bf16[64,4,1024]{2,1,0:T(4,128)(2,1)} custom-call(bf16[1,4,4096]{2,1,0:T(4,128)(2,1)} %refs_0_.1, f32[1,4096]{1,0:T(1,128)} %refs_1_.1), custom_call_target="tpu_custom_call" | custom-call | bytes 524288 | tf_op jit(solution)/shard_map/pallas_call | solution.py:46
  1.8 0.0 copy-start
  1.8 0.0 copy-start.1
  1.8 23.3 %all-to-all-start = ((bf16[64,4,1024]{2,1,0:T(4,128)(2,1)}), bf16[64,4,1024]{2,1,0:T(4,128)(2,1)S(1)}, u32[]{:S(2)}, u32[]{:S(2)}) async-start(bf16[64,4,1024]{2,1,0:T(4,128)(2,1)} %shard_map.55), calls=%async_computation | async-start | bytes 1048576 | tf_op jit(solution)/shard_map/all_to_all | solution.py:17
  25.2 0.0 copy-done.3
  25.2 3.3 %collective-permute-start = (bf16[4,4096]{1,0:T(4,128)(2,1)S(1)}, bf16[4,4096]{1,0:T(4,128)(2,1)S(1)}, u32[]{:S(2)}, u32[]{:S(2)}) collective-permute-start(bf16[4,4096]{1,0:T(4,128)(2,1)S(1)} %bitcast.24), channel_id=1, source_target_pairs={{0,64},{1,65},{2,66},{3,67},{4,68},{5,69},{6,70},{7,71},{8,72},{9,... | collective-permute-start | bytes 98312 | tf_op jit(solution)/shard_map/ppermute | solution.py:22
  28.5 13.0 %all-to-all-done = bf16[64,4,1024]{2,1,0:T(4,128)(2,1)S(1)} async-done(((bf16[64,4,1024]{2,1,0:T(4,128)(2,1)}), bf16[64,4,1024]{2,1,0:T(4,128)(2,1)S(1)}, u32[]{:S(2)}, u32[]{:S(2)}) %all-to-all-start) | async-done | bytes 524320 | tf_op jit(solution)/shard_map/all_to_all | solution.py:17
  41.5 0.1 reshape.21.refs_1_
  41.6 0.0 collective-permute-done.refs_0_
  41.6 0.0 copy-done
  41.7 0.0 copy-done.1
  41.7 1.5 %shard_map.56 = bf16[256,1024]{1,0:T(8,128)(2,1)} custom-call(bf16[4,4096]{1,0:T(4,128)(2,1)S(1)} %collective-permute-done.refs_0_, bf16[256,1024]{1,0:T(8,128)(2,1)S(1)} %reshape.21.refs_1_, bf16[1024,512]{1,0:T(8,128)(2,1)S(1)} %bitcast.14, bf16[1024,512]{1,0:T(8,128)(2,1)S(1)} %bitcast.16), custom_call_target="tpu_custom_call" | custom-call | flops 536870912 | bytes 2097152 | tf_op jit(solution)/shard_map/pallas_call | solution.py:46
  43.2 4.3 %all-to-all-start.1 = ((bf16[4,64,1024]{2,1,0:T(8,128)(2,1)}), bf16[4,64,1024]{2,1,0:T(8,128)(2,1)S(1)}, u32[]{:S(2)}, u32[]{:S(2)}) async-start(bf16[4,64,1024]{2,1,0:T(8,128)(2,1)} %bitcast.3), calls=%async_computation.1 | async-start | bytes 1048576 | tf_op jit(solution)/shard_map/all_to_all | solution.py:17
  47.5 3.3 %collective-permute-start.1 = (bf16[256,1024]{1,0:T(8,128)(2,1)S(1)}, bf16[256,1024]{1,0:T(8,128)(2,1)}, u32[]{:S(2)}, u32[]{:S(2)}) collective-permute-start(bf16[256,1024]{1,0:T(8,128)(2,1)S(1)} %reshape.21.refs_1_), channel_id=1, source_target_pairs={{0,64},{1,65},{2,66},{3,67},{4,68},{5,69},{6,70},{7,71},{8,72},{9,... | collective-permute-start | bytes 1572872 | tf_op jit(solution)/shard_map/ppermute | solution.py:22
  50.8 7.7 %all-to-all-done.1.refs_0_ = bf16[4,64,1024]{2,1,0:T(8,128)(2,1)S(1)} async-done(((bf16[4,64,1024]{2,1,0:T(8,128)(2,1)}), bf16[4,64,1024]{2,1,0:T(8,128)(2,1)S(1)}, u32[]{:S(2)}, u32[]{:S(2)}) %all-to-all-start.1) | async-done | bytes 524320 | tf_op jit(solution)/shard_map/all_to_all | solution.py:17
  58.5 0.1 shard_map.57.refs_1_
  58.6 1.1 collective-permute-done.1.refs_0_
  59.7 1.8 %shard_map.58 = bf16[256,1536]{1,0:T(8,128)(2,1)S(1)} custom-call(bf16[256,1024]{1,0:T(8,128)(2,1)} %collective-permute-done.1.refs_0_, bf16[64,512]{1,0:T(8,128)(2,1)S(1)} %shard_map.57.refs_1_, bf16[1024,512]{1,0:T(8,128)(2,1)S(1)} %bitcast.15, bf16[1024,512]{1,0:T(8,128)(2,1)S(1)} %bitcast.17), custom_call_target="tpu_custom_call" | custom-call | flops 536870912 | bytes 2097152 | tf_op jit(solution)/shard_map/pallas_call | solution.py:46
  61.5 0.0 copy-start.2
  61.5 22.4 %all_to_all.25.refs_0_ = bf16[4,64,1536]{2,1,0:T(8,128)(2,1)S(1)} all-to-all(bf16[4,64,1536]{2,1,0:T(8,128)(2,1)S(1)} %bitcast.20), channel_id=1, replica_groups={{0,1,2,3},{4,5,6,7},{8,9,10,11},{12,13,14,15},{16,17,18,19},{20,21,22,2..., dimensions={0} | all-to-all | bytes 1572864 | tf_op jit(solution)/shard_map/all_to_all | solution.py:17
  83.9 0.0 copy-done.2
  83.9 0.5 shard_map.59
  84.4 3.3 %collective-permute-start.2 = (bf16[256,1024]{1,0:T(8,128)(2,1)S(1)}, bf16[256,1024]{1,0:T(8,128)(2,1)S(1)}, u32[]{:S(2)}, u32[]{:S(2)}) collective-permute-start(bf16[256,1024]{1,0:T(8,128)(2,1)S(1)} %get-tuple-element.8), channel_id=1, source_target_pairs={{0,64},{1,65},{2,66},{3,67},{4,68},{5,69},{6,70},{7,71},{8,72},{9,... | collective-permute-start | bytes 1572872 | tf_op jit(solution)/shard_map/ppermute | solution.py:22
  87.7 8.5 %all_to_all.26 = bf16[4,64,512]{2,1,0:T(8,128)(2,1)S(1)} all-to-all(bf16[4,64,512]{2,1,0:T(8,128)(2,1)S(1)} %get-tuple-element.7), channel_id=1, replica_groups={{0,1,2,3},{4,5,6,7},{8,9,10,11},{12,13,14,15},{16,17,18,19},{20,21,22,2..., dimensions={0} | all-to-all | bytes 524288 | tf_op jit(solution)/shard_map/all_to_all | solution.py:17
  96.3 0.6 collective-permute-done.2.refs_2_
  96.9 0.4 shard_map.60
  97.4 0.2 reshape.25
  97.6 25.0 %all_to_all.27 = bf16[64,4,1024]{2,1,0:T(4,128)(2,1)S(1)} all-to-all(bf16[64,4,1024]{2,1,0:T(4,128)(2,1)S(1)} %reshape.25), channel_id=1, replica_groups={{0,1,2,3,4,5,6,7,8,9,10,11,12,13,14,15,16,17,18,19,20,21,22,23,24,25,26..., dimensions={0} | all-to-all | bytes 1048576 | tf_op jit(solution)/shard_map/all_to_all | solution.py:17
  122.5 0.2 convert_reduce_fusion
  122.8 11.4 %collective-permute-start.3 = (bf16[1,4,4096]{2,1,0:T(4,128)(2,1)S(1)}, bf16[1,4,4096]{2,1,0:T(4,128)(2,1)S(1)}, u32[]{:S(2)}, u32[]{:S(2)}) collective-permute-start(bf16[1,4,4096]{2,1,0:T(4,128)(2,1)S(1)} %fusion), channel_id=1, source_target_pairs={{0,192},{1,193},{2,194},{3,195},{4,196},{5,197},{6,198},{7,199},{8... | collective-permute-start | bytes 98312 | tf_op jit(solution)/shard_map/ppermute | solution.py:32
  134.2 1.0 collective-permute-done.3
  135.2 0.6 copy.7
  (2 shorter events, 0.0 us)
Async XLA Ops:
  0.0 25.2 %copy-start.3 = (bf16[1,4,4096]{2,1,0:T(4,128)(2,1)S(1)}, bf16[1,4,4096]{2,1,0:T(4,128)(2,1)}, u32[]{:S(2)}) copy-start(bf16[1,4,4096]{2,1,0:T(4,128)(2,1)} %refs_0_.1) | copy-start | bytes 98308
  1.8 39.8 %copy-start = (bf16[1,1,1024,512]{3,2,1,0:T(8,128)(2,1)S(1)}, bf16[1,1,1024,512]{3,2,1,0:T(8,128)(2,1)}, u32[]{:S(2)}) copy-start(bf16[1,1,1024,512]{3,2,1,0:T(8,128)(2,1)} %param.7) | copy-start | bytes 3145732
  1.8 39.8 %copy-start.1 = (bf16[1,1,1024,512]{3,2,1,0:T(8,128)(2,1)S(1)}, bf16[1,1,1024,512]{3,2,1,0:T(8,128)(2,1)}, u32[]{:S(2)}) copy-start(bf16[1,1,1024,512]{3,2,1,0:T(8,128)(2,1)} %param.8) | copy-start | bytes 3145732
  1.8 39.7 %all-to-all-start = ((bf16[64,4,1024]{2,1,0:T(4,128)(2,1)}), bf16[64,4,1024]{2,1,0:T(4,128)(2,1)S(1)}, u32[]{:S(2)}, u32[]{:S(2)}) async-start(bf16[64,4,1024]{2,1,0:T(4,128)(2,1)} %shard_map.55), calls=%async_computation | async-start | bytes 1048576 | tf_op jit(solution)/shard_map/all_to_all | solution.py:17
  25.2 16.5 %collective-permute-start = (bf16[4,4096]{1,0:T(4,128)(2,1)S(1)}, bf16[4,4096]{1,0:T(4,128)(2,1)S(1)}, u32[]{:S(2)}, u32[]{:S(2)}) collective-permute-start(bf16[4,4096]{1,0:T(4,128)(2,1)S(1)} %bitcast.24), channel_id=1, source_target_pairs={{0,64},{1,65},{2,66},{3,67},{4,68},{5,69},{6,70},{7,71},{8,72},{9,... | collective-permute-start | bytes 98312 | tf_op jit(solution)/shard_map/ppermute | solution.py:22
  43.2 15.4 %all-to-all-start.1 = ((bf16[4,64,1024]{2,1,0:T(8,128)(2,1)}), bf16[4,64,1024]{2,1,0:T(8,128)(2,1)S(1)}, u32[]{:S(2)}, u32[]{:S(2)}) async-start(bf16[4,64,1024]{2,1,0:T(8,128)(2,1)} %bitcast.3), calls=%async_computation.1 | async-start | bytes 1048576 | tf_op jit(solution)/shard_map/all_to_all | solution.py:17
  47.5 12.2 %collective-permute-start.1 = (bf16[256,1024]{1,0:T(8,128)(2,1)S(1)}, bf16[256,1024]{1,0:T(8,128)(2,1)}, u32[]{:S(2)}, u32[]{:S(2)}) collective-permute-start(bf16[256,1024]{1,0:T(8,128)(2,1)S(1)} %reshape.21.refs_1_), channel_id=1, source_target_pairs={{0,64},{1,65},{2,66},{3,67},{4,68},{5,69},{6,70},{7,71},{8,72},{9,... | collective-permute-start | bytes 1572872 | tf_op jit(solution)/shard_map/ppermute | solution.py:22
  61.5 22.5 %copy-start.2 = (bf16[1,1,512,1024]{3,2,1,0:T(8,128)(2,1)S(1)}, bf16[1,1,512,1024]{3,2,1,0:T(8,128)(2,1)}, u32[]{:S(2)}) copy-start(bf16[1,1,512,1024]{3,2,1,0:T(8,128)(2,1)} %param.9) | copy-start | bytes 3145732
  84.4 12.5 %collective-permute-start.2 = (bf16[256,1024]{1,0:T(8,128)(2,1)S(1)}, bf16[256,1024]{1,0:T(8,128)(2,1)S(1)}, u32[]{:S(2)}, u32[]{:S(2)}) collective-permute-start(bf16[256,1024]{1,0:T(8,128)(2,1)S(1)} %get-tuple-element.8), channel_id=1, source_target_pairs={{0,64},{1,65},{2,66},{3,67},{4,68},{5,69},{6,70},{7,71},{8,72},{9,... | collective-permute-start | bytes 1572872 | tf_op jit(solution)/shard_map/ppermute | solution.py:22
  122.8 12.4 %collective-permute-start.3 = (bf16[1,4,4096]{2,1,0:T(4,128)(2,1)S(1)}, bf16[1,4,4096]{2,1,0:T(4,128)(2,1)S(1)}, u32[]{:S(2)}, u32[]{:S(2)}) collective-permute-start(bf16[1,4,4096]{2,1,0:T(4,128)(2,1)S(1)} %fusion), channel_id=1, source_target_pairs={{0,192},{1,193},{2,194},{3,195},{4,196},{5,197},{6,198},{7,199},{8... | collective-permute-start | bytes 98312 | tf_op jit(solution)/shard_map/ppermute | solution.py:32

commit v8 on v7

--- a/solution.py
+++ b/solution.py
@@ -13,8 +13,14 @@
     return [list(range(low, low + size)) for low in range(0, count, size)]
 
 
-def traded(blocks, size):
-    return lax.all_to_all(blocks, "tensor", 0, 0, axis_index_groups=runs(size), tiled=True)
+def scattered(run, size):
+    count = run // size
+    places = [(3 * k + 5 * a) % count * size + a for k in range(count) for a in range(size)]
+    return [[low + place for place in places] for low in range(0, lax.axis_size("tensor"), run)]
+
+
+def traded(blocks, groups):
+    return lax.all_to_all(blocks, "tensor", 0, 0, axis_index_groups=groups, tiled=True)
 
 
 def flipped(values, mask):
@@ -122,6 +128,7 @@
     piece = total // groups_a
     cost = 2 * total * depth * width
     weight = 2 * depth * width
+    quads, half = runs(groups_a), scattered(near, groups_a)
 
     mirror_acts = flipped(acts[0], near)
     (sent,) = local(
@@ -139,7 +146,7 @@
         ],
         fetches=True,
     )
-    near_columns = traded(sent, near).reshape(total, depth)
+    near_columns = traded(sent, half).reshape(total, depth)
     far_columns = flipped(near_columns, near)
 
     (sums,) = local(
@@ -152,7 +159,7 @@
         up_local,
         after=(mirror_acts,),
     )
-    shares = traded(sums.reshape(groups_a, piece, 2 * width), groups_a)
+    shares = traded(sums.reshape(groups_a, piece, 2 * width), quads)
     (near_share,) = local(near_share_kernel, [(piece, width)], 0, 2 * total * width, shares)
     (sums,) = local(
         far_sums_near_share,
@@ -164,7 +171,7 @@
         gate_local,
         up_local,
     )
-    got = traded(sums.reshape(groups_a, piece, 3 * width), groups_a)
+    got = traded(sums.reshape(groups_a, piece, 3 * width), quads)
     near_rows, spread = local(
         near_down_far_share,
         [(total, depth), (groups_a, piece, width)],
@@ -175,9 +182,9 @@
     )
 
     mirror_rows = flipped(near_rows, near)
-    hidden = traded(spread, groups_a).reshape(total, width)
+    hidden = traded(spread, quads).reshape(total, width)
     (rows,) = local(far_down, [(total, depth)], cost, weight, hidden, down_local, mirror_rows)
-    parts = traded(rows.reshape(near, tokens, depth), near)
+    parts = traded(rows.reshape(near, tokens, depth), half)
     parts = parts.reshape(groups_b, groups_a, tokens, depth).astype(f32)
     summed = jnp.transpose(jnp.sum(parts, axis=0), (1, 0, 2)).reshape(tokens, features)
     block = (mirror_acts.astype(f32) + summed).astype(bf16)

time: 137 us -> 135 us (0.985)
  starting transfers between devices: 48.9 us -> 46.9 us
where the time goes in v8:
time: 135 us
  blocking collectives  56.8 us (42%)
  starting transfers between devices  46.9 us (35%)
  waiting for transfers between devices  23.4 us (17%)
  Pallas kernels  6.07 us (4%)
    all_to_all x3, blocking collectives, traded(): lax.all_to_all(blocks, 'tensor', 0, 0, axis_index_groups=groups, tiled=True)  56.8 us
    all_to_all x2, starting transfers between devices, traded(): lax.all_to_all(blocks, 'tensor', 0, 0, axis_index_groups=groups, tiled=True)  26.8 us
    all_to_all x2, waiting for transfers between devices, traded(): lax.all_to_all(blocks, 'tensor', 0, 0, axis_index_groups=groups, tiled=True)  20.6 us
    ppermute x1, starting transfers between devices, passed_along(): return lax.ppermute(value, ('section', 'tensor'), route)  10.2 us
    ppermute x3, starting transfers between devices, flipped(): return lax.ppermute(values, 'tensor', [(i, i ^ mask) for i in range(count)])  9.95 us
    pallas_call x6, Pallas kernels, local(): pl.pallas_call(kernel, out_shape=[jax.ShapeDtypeStruct(shape, bf16) for s...  6.07 us
  transfers between devices with their start and end apart: 6, of which 5 were waited for; matrix products, arithmetic and copies ran while one was open for 0% of the time, Pallas kernels for 0%

profile of v8, /device:TPU:1, one launch (start us, length us, event | category | flops | bytes accessed | tf_op | source)
XLA Modules:
  0.0 134.6 jit_solution(15635313876282586937)
XLA Ops:
  0.0 1.8 %shard_map.55 = bf16[64,4,1024]{2,1,0:T(4,128)(2,1)} custom-call(bf16[1,4,4096]{2,1,0:T(4,128)(2,1)} %refs_0_.1, f32[1,4096]{1,0:T(1,128)} %refs_1_.1), custom_call_target="tpu_custom_call" | custom-call | bytes 524288 | tf_op jit(solution)/shard_map/pallas_call | solution.py:52
  1.8 0.0 copy-start
  1.8 0.0 copy-start.1
  1.8 23.3 %all-to-all-start = ((bf16[64,4,1024]{2,1,0:T(4,128)(2,1)}), bf16[64,4,1024]{2,1,0:T(4,128)(2,1)S(1)}, u32[]{:S(2)}, u32[]{:S(2)}) async-start(bf16[64,4,1024]{2,1,0:T(4,128)(2,1)} %shard_map.55), calls=%async_computation | async-start | bytes 1048576 | tf_op jit(solution)/shard_map/all_to_all | solution.py:23
  25.2 0.0 copy-done.3
  25.2 3.3 %collective-permute-start = (bf16[4,4096]{1,0:T(4,128)(2,1)S(1)}, bf16[4,4096]{1,0:T(4,128)(2,1)S(1)}, u32[]{:S(2)}, u32[]{:S(2)}) collective-permute-start(bf16[4,4096]{1,0:T(4,128)(2,1)S(1)} %bitcast.24), channel_id=1, source_target_pairs={{0,64},{1,65},{2,66},{3,67},{4,68},{5,69},{6,70},{7,71},{8,72},{9,... | collective-permute-start | bytes 98312 | tf_op jit(solution)/shard_map/ppermute | solution.py:28
  28.5 12.8 %all-to-all-done = bf16[64,4,1024]{2,1,0:T(4,128)(2,1)S(1)} async-done(((bf16[64,4,1024]{2,1,0:T(4,128)(2,1)}), bf16[64,4,1024]{2,1,0:T(4,128)(2,1)S(1)}, u32[]{:S(2)}, u32[]{:S(2)}) %all-to-all-start) | async-done | bytes 524320 | tf_op jit(solution)/shard_map/all_to_all | solution.py:23
  41.3 0.1 reshape.21.refs_1_
  41.5 0.0 collective-permute-done.refs_0_
  41.5 0.0 copy-done
  41.5 0.0 copy-done.1
  41.5 1.5 %shard_map.56 = bf16[256,1024]{1,0:T(8,128)(2,1)} custom-call(bf16[4,4096]{1,0:T(4,128)(2,1)S(1)} %collective-permute-done.refs_0_, bf16[256,1024]{1,0:T(8,128)(2,1)S(1)} %reshape.21.refs_1_, bf16[1024,512]{1,0:T(8,128)(2,1)S(1)} %bitcast.14, bf16[1024,512]{1,0:T(8,128)(2,1)S(1)} %bitcast.16), custom_call_target="tpu_custom_call" | custom-call | flops 536870912 | bytes 2097152 | tf_op jit(solution)/shard_map/pallas_call | solution.py:52
  43.0 3.5 %all-to-all-start.1 = ((bf16[4,64,1024]{2,1,0:T(8,128)(2,1)}), bf16[4,64,1024]{2,1,0:T(8,128)(2,1)S(1)}, u32[]{:S(2)}, u32[]{:S(2)}) async-start(bf16[4,64,1024]{2,1,0:T(8,128)(2,1)} %bitcast.3), calls=%async_computation.1 | async-start | bytes 1048576 | tf_op jit(solution)/shard_map/all_to_all | solution.py:23
  46.4 3.3 %collective-permute-start.1 = (bf16[256,1024]{1,0:T(8,128)(2,1)S(1)}, bf16[256,1024]{1,0:T(8,128)(2,1)}, u32[]{:S(2)}, u32[]{:S(2)}) collective-permute-start(bf16[256,1024]{1,0:T(8,128)(2,1)S(1)} %reshape.21.refs_1_), channel_id=1, source_target_pairs={{0,64},{1,65},{2,66},{3,67},{4,68},{5,69},{6,70},{7,71},{8,72},{9,... | collective-permute-start | bytes 1572872 | tf_op jit(solution)/shard_map/ppermute | solution.py:28
  49.8 7.8 %all-to-all-done.1.refs_0_ = bf16[4,64,1024]{2,1,0:T(8,128)(2,1)S(1)} async-done(((bf16[4,64,1024]{2,1,0:T(8,128)(2,1)}), bf16[4,64,1024]{2,1,0:T(8,128)(2,1)S(1)}, u32[]{:S(2)}, u32[]{:S(2)}) %all-to-all-start.1) | async-done | bytes 524320 | tf_op jit(solution)/shard_map/all_to_all | solution.py:23
  57.6 0.1 shard_map.57.refs_1_
  57.7 1.1 collective-permute-done.1.refs_0_
  58.8 1.8 %shard_map.58 = bf16[256,1536]{1,0:T(8,128)(2,1)S(1)} custom-call(bf16[256,1024]{1,0:T(8,128)(2,1)} %collective-permute-done.1.refs_0_, bf16[64,512]{1,0:T(8,128)(2,1)S(1)} %shard_map.57.refs_1_, bf16[1024,512]{1,0:T(8,128)(2,1)S(1)} %bitcast.15, bf16[1024,512]{1,0:T(8,128)(2,1)S(1)} %bitcast.17), custom_call_target="tpu_custom_call" | custom-call | flops 536870912 | bytes 2097152 | tf_op jit(solution)/shard_map/pallas_call | solution.py:52
  60.5 0.0 copy-start.2
  60.6 22.4 %all_to_all.25.refs_0_ = bf16[4,64,1536]{2,1,0:T(8,128)(2,1)S(1)} all-to-all(bf16[4,64,1536]{2,1,0:T(8,128)(2,1)S(1)} %bitcast.20), channel_id=1, replica_groups={{0,1,2,3},{4,5,6,7},{8,9,10,11},{12,13,14,15},{16,17,18,19},{20,21,22,2..., dimensions={0} | all-to-all | bytes 1572864 | tf_op jit(solution)/shard_map/all_to_all | solution.py:23
  83.0 0.0 copy-done.2
  83.0 0.5 shard_map.59
  83.5 3.3 %collective-permute-start.2 = (bf16[256,1024]{1,0:T(8,128)(2,1)S(1)}, bf16[256,1024]{1,0:T(8,128)(2,1)S(1)}, u32[]{:S(2)}, u32[]{:S(2)}) collective-permute-start(bf16[256,1024]{1,0:T(8,128)(2,1)S(1)} %get-tuple-element.8), channel_id=1, source_target_pairs={{0,64},{1,65},{2,66},{3,67},{4,68},{5,69},{6,70},{7,71},{8,72},{9,... | collective-permute-start | bytes 1572872 | tf_op jit(solution)/shard_map/ppermute | solution.py:28
  86.8 8.5 %all_to_all.26 = bf16[4,64,512]{2,1,0:T(8,128)(2,1)S(1)} all-to-all(bf16[4,64,512]{2,1,0:T(8,128)(2,1)S(1)} %get-tuple-element.7), channel_id=1, replica_groups={{0,1,2,3},{4,5,6,7},{8,9,10,11},{12,13,14,15},{16,17,18,19},{20,21,22,2..., dimensions={0} | all-to-all | bytes 524288 | tf_op jit(solution)/shard_map/all_to_all | solution.py:23
  95.3 0.7 collective-permute-done.2.refs_2_
  96.0 0.4 shard_map.60
  96.4 0.2 reshape.25
  96.6 25.9 %all_to_all.27 = bf16[64,4,1024]{2,1,0:T(4,128)(2,1)S(1)} all-to-all(bf16[64,4,1024]{2,1,0:T(4,128)(2,1)S(1)} %reshape.25), channel_id=1, replica_groups={{0,21,42,63,12,33,54,11,24,45,2,23,36,57,14,35,48,5,26,47,60,17,38,59,8..., dimensions={0} | all-to-all | bytes 1048576 | tf_op jit(solution)/shard_map/all_to_all | solution.py:23
  122.5 0.2 convert_reduce_fusion
  122.8 10.2 %collective-permute-start.3 = (bf16[1,4,4096]{2,1,0:T(4,128)(2,1)S(1)}, bf16[1,4,4096]{2,1,0:T(4,128)(2,1)S(1)}, u32[]{:S(2)}, u32[]{:S(2)}) collective-permute-start(bf16[1,4,4096]{2,1,0:T(4,128)(2,1)S(1)} %fusion), channel_id=1, source_target_pairs={{0,192},{1,193},{2,194},{3,195},{4,196},{5,197},{6,198},{7,199},{8... | collective-permute-start | bytes 98312 | tf_op jit(solution)/shard_map/ppermute | solution.py:38
  133.0 1.0 collective-permute-done.3
  134.0 0.6 copy.7
  (2 shorter events, 0.0 us)
Async XLA Ops:
  0.0 25.2 %copy-start.3 = (bf16[1,4,4096]{2,1,0:T(4,128)(2,1)S(1)}, bf16[1,4,4096]{2,1,0:T(4,128)(2,1)}, u32[]{:S(2)}) copy-start(bf16[1,4,4096]{2,1,0:T(4,128)(2,1)} %refs_0_.1) | copy-start | bytes 98308
  1.8 39.6 %copy-start = (bf16[1,1,1024,512]{3,2,1,0:T(8,128)(2,1)S(1)}, bf16[1,1,1024,512]{3,2,1,0:T(8,128)(2,1)}, u32[]{:S(2)}) copy-start(bf16[1,1,1024,512]{3,2,1,0:T(8,128)(2,1)} %param.7) | copy-start | bytes 3145732
  1.8 39.6 %copy-start.1 = (bf16[1,1,1024,512]{3,2,1,0:T(8,128)(2,1)S(1)}, bf16[1,1,1024,512]{3,2,1,0:T(8,128)(2,1)}, u32[]{:S(2)}) copy-start(bf16[1,1,1024,512]{3,2,1,0:T(8,128)(2,1)} %param.8) | copy-start | bytes 3145732
  1.8 39.5 %all-to-all-start = ((bf16[64,4,1024]{2,1,0:T(4,128)(2,1)}), bf16[64,4,1024]{2,1,0:T(4,128)(2,1)S(1)}, u32[]{:S(2)}, u32[]{:S(2)}) async-start(bf16[64,4,1024]{2,1,0:T(4,128)(2,1)} %shard_map.55), calls=%async_computation | async-start | bytes 1048576 | tf_op jit(solution)/shard_map/all_to_all | solution.py:23
  25.2 16.3 %collective-permute-start = (bf16[4,4096]{1,0:T(4,128)(2,1)S(1)}, bf16[4,4096]{1,0:T(4,128)(2,1)S(1)}, u32[]{:S(2)}, u32[]{:S(2)}) collective-permute-start(bf16[4,4096]{1,0:T(4,128)(2,1)S(1)} %bitcast.24), channel_id=1, source_target_pairs={{0,64},{1,65},{2,66},{3,67},{4,68},{5,69},{6,70},{7,71},{8,72},{9,... | collective-permute-start | bytes 98312 | tf_op jit(solution)/shard_map/ppermute | solution.py:28
  43.0 14.6 %all-to-all-start.1 = ((bf16[4,64,1024]{2,1,0:T(8,128)(2,1)}), bf16[4,64,1024]{2,1,0:T(8,128)(2,1)S(1)}, u32[]{:S(2)}, u32[]{:S(2)}) async-start(bf16[4,64,1024]{2,1,0:T(8,128)(2,1)} %bitcast.3), calls=%async_computation.1 | async-start | bytes 1048576 | tf_op jit(solution)/shard_map/all_to_all | solution.py:23
  46.4 12.3 %collective-permute-start.1 = (bf16[256,1024]{1,0:T(8,128)(2,1)S(1)}, bf16[256,1024]{1,0:T(8,128)(2,1)}, u32[]{:S(2)}, u32[]{:S(2)}) collective-permute-start(bf16[256,1024]{1,0:T(8,128)(2,1)S(1)} %reshape.21.refs_1_), channel_id=1, source_target_pairs={{0,64},{1,65},{2,66},{3,67},{4,68},{5,69},{6,70},{7,71},{8,72},{9,... | collective-permute-start | bytes 1572872 | tf_op jit(solution)/shard_map/ppermute | solution.py:28
  60.5 22.4 %copy-start.2 = (bf16[1,1,512,1024]{3,2,1,0:T(8,128)(2,1)S(1)}, bf16[1,1,512,1024]{3,2,1,0:T(8,128)(2,1)}, u32[]{:S(2)}) copy-start(bf16[1,1,512,1024]{3,2,1,0:T(8,128)(2,1)} %param.9) | copy-start | bytes 3145732
  83.5 12.5 %collective-permute-start.2 = (bf16[256,1024]{1,0:T(8,128)(2,1)S(1)}, bf16[256,1024]{1,0:T(8,128)(2,1)S(1)}, u32[]{:S(2)}, u32[]{:S(2)}) collective-permute-start(bf16[256,1024]{1,0:T(8,128)(2,1)S(1)} %get-tuple-element.8), channel_id=1, source_target_pairs={{0,64},{1,65},{2,66},{3,67},{4,68},{5,69},{6,70},{7,71},{8,72},{9,... | collective-permute-start | bytes 1572872 | tf_op jit(solution)/shard_map/ppermute | solution.py:28
  122.8 11.2 %collective-permute-start.3 = (bf16[1,4,4096]{2,1,0:T(4,128)(2,1)S(1)}, bf16[1,4,4096]{2,1,0:T(4,128)(2,1)S(1)}, u32[]{:S(2)}, u32[]{:S(2)}) collective-permute-start(bf16[1,4,4096]{2,1,0:T(4,128)(2,1)S(1)} %fusion), channel_id=1, source_target_pairs={{0,192},{1,193},{2,194},{3,195},{4,196},{5,197},{6,198},{7,199},{8... | collective-permute-start | bytes 98312 | tf_op jit(solution)/shard_map/ppermute | solution.py:38

commit v9 on v8

--- a/solution.py
+++ b/solution.py
@@ -42,9 +42,10 @@
     return jnp.dot(left, right, preferred_element_type=f32)
 
 
-def local(body, outs, flops, moved, *operands, after=(), scratch=(), fetches=False):
-    spec = pl.BlockSpec(memory_space=pl.ANY if fetches else pltpu.VMEM)
-    limit = (56 if fetches else 24) * 2**20
+def local(body, outs, flops, moved, *operands, after=(), scratch=(), fetches=0):
+    spec, placed = pl.BlockSpec(memory_space=pltpu.VMEM), pl.BlockSpec(memory_space=pl.ANY)
+    limit = (56 if fetches == len(operands) else 24) * 2**20
+    left = len(operands) - fetches
 
     def kernel(*refs):
         body(*refs[len(after) :])
@@ -52,8 +53,8 @@
     return pl.pallas_call(
         kernel,
         out_shape=[jax.ShapeDtypeStruct(shape, bf16) for shape in outs],
-        in_specs=[pl.BlockSpec(memory_space=pl.ANY)] * len(after) + [spec] * len(operands),
-        out_specs=[pl.BlockSpec(memory_space=pltpu.VMEM)] * len(outs),
+        in_specs=[placed] * (len(after) + fetches) + [spec] * left,
+        out_specs=[spec] * len(outs),
         scratch_shapes=scratch,
         compiler_params=pltpu.CompilerParams(vmem_limit_bytes=limit),
         cost_estimate=pl.CostEstimate(flops=flops, bytes_accessed=moved, transcendentals=0),
@@ -95,11 +96,21 @@
     share_ref[...] = gated(shares_ref, share_ref.shape[1])
 
 
-def far_sums_near_share(columns_ref, share_ref, gate_ref, up_ref, out_ref):
+def far_sums_near_share(far_ref, share_ref, gate_ref, up_ref, out_ref, columns_ref, arrived):
     piece, width = share_ref.shape
-    gate_up(columns_ref, gate_ref, up_ref, out_ref)
-    for low in range(0, out_ref.shape[0], piece):
+    total = out_ref.shape[0]
+    halves = [pl.ds(0, total // 2), pl.ds(total // 2, total // 2)]
+    fetched = [
+        pltpu.make_async_copy(far_ref.at[rows], columns_ref.at[rows], arrived.at[half])
+        for half, rows in enumerate(halves)
+    ]
+    for copy in fetched:
+        copy.start()
+    for low in range(0, total, piece):
         out_ref[low : low + piece, 2 * width :] = share_ref[...]
+    for copy, rows in zip(fetched, halves, strict=True):
+        copy.wait()
+        gate_up(columns_ref.at[rows], gate_ref, up_ref, out_ref.at[rows])
 
 
 def near_down_far_share(got_ref, down_ref, rows_ref, spread_ref):
@@ -144,7 +155,7 @@
             pltpu.SemaphoreType.DMA,
             pltpu.SemaphoreType.DMA,
         ],
-        fetches=True,
+        fetches=2,
     )
     near_columns = traded(sent, half).reshape(total, depth)
     far_columns = flipped(near_columns, near)
@@ -170,6 +181,8 @@
         near_share,
         gate_local,
         up_local,
+        fetches=1,
+        scratch=[pltpu.VMEM((total, depth), bf16), pltpu.SemaphoreType.DMA((2,))],
     )
     got = traded(sums.reshape(groups_a, piece, 3 * width), quads)
     near_rows, spread = local(

time: 135 us -> 136 us (level)
  no operation moved by 1% of the time
where the time goes in v9:
time: 136 us; the launch traced here: 135 us
  blocking collectives  56.8 us (42%)
  starting transfers between devices  47.2 us (35%)
  waiting for transfers between devices  23.4 us (17%)
  Pallas kernels  6.19 us (5%)
    all_to_all x3, blocking collectives, traded(): lax.all_to_all(blocks, 'tensor', 0, 0, axis_index_groups=groups, tiled=True)  56.8 us
    all_to_all x2, starting transfers between devices, traded(): lax.all_to_all(blocks, 'tensor', 0, 0, axis_index_groups=groups, tiled=True)  26.8 us
    all_to_all x2, waiting for transfers between devices, traded(): lax.all_to_all(blocks, 'tensor', 0, 0, axis_index_groups=groups, tiled=True)  20.6 us
    ppermute x1, starting transfers between devices, passed_along(): return lax.ppermute(value, ('section', 'tensor'), route)  10.5 us
    ppermute x3, starting transfers between devices, flipped(): return lax.ppermute(values, 'tensor', [(i, i ^ mask) for i in range(count)])  9.95 us
    pallas_call x6, Pallas kernels, local(): pl.pallas_call(kernel, out_shape=[jax.ShapeDtypeStruct(shape, bf16) for s...  6.19 us
  transfers between devices with their start and end apart: 6, of which 5 were waited for; matrix products, arithmetic and copies ran while one was open for 0% of the time, Pallas kernels for 0%

profile of v9, /device:TPU:1, one launch (start us, length us, event | category | flops | bytes accessed | tf_op | source)
XLA Modules:
  0.0 135.0 jit_solution(14873268027707671111)
XLA Ops:
  0.0 1.8 %shard_map.55 = bf16[64,4,1024]{2,1,0:T(4,128)(2,1)} custom-call(bf16[1,4,4096]{2,1,0:T(4,128)(2,1)} %refs_0_.1, f32[1,4096]{1,0:T(1,128)} %refs_1_.1), custom_call_target="tpu_custom_call" | custom-call | bytes 524288 | tf_op jit(solution)/shard_map/pallas_call | solution.py:53
  1.8 0.0 copy-start
  1.8 0.0 copy-start.1
  1.8 23.3 %all-to-all-start = ((bf16[64,4,1024]{2,1,0:T(4,128)(2,1)}), bf16[64,4,1024]{2,1,0:T(4,128)(2,1)S(1)}, u32[]{:S(2)}, u32[]{:S(2)}) async-start(bf16[64,4,1024]{2,1,0:T(4,128)(2,1)} %shard_map.55), calls=%async_computation | async-start | bytes 1048576 | tf_op jit(solution)/shard_map/all_to_all | solution.py:23
  25.2 0.0 copy-done.3
  25.2 3.3 %collective-permute-start = (bf16[4,4096]{1,0:T(4,128)(2,1)S(1)}, bf16[4,4096]{1,0:T(4,128)(2,1)S(1)}, u32[]{:S(2)}, u32[]{:S(2)}) collective-permute-start(bf16[4,4096]{1,0:T(4,128)(2,1)S(1)} %bitcast.24), channel_id=1, source_target_pairs={{0,64},{1,65},{2,66},{3,67},{4,68},{5,69},{6,70},{7,71},{8,72},{9,... | collective-permute-start | bytes 98312 | tf_op jit(solution)/shard_map/ppermute | solution.py:28
  28.5 12.8 %all-to-all-done = bf16[64,4,1024]{2,1,0:T(4,128)(2,1)S(1)} async-done(((bf16[64,4,1024]{2,1,0:T(4,128)(2,1)}), bf16[64,4,1024]{2,1,0:T(4,128)(2,1)S(1)}, u32[]{:S(2)}, u32[]{:S(2)}) %all-to-all-start) | async-done | bytes 524320 | tf_op jit(solution)/shard_map/all_to_all | solution.py:23
  41.3 0.1 reshape.21.refs_1_
  41.5 0.0 collective-permute-done.refs_0_
  41.5 0.0 copy-done
  41.5 0.0 copy-done.1
  41.5 1.5 %shard_map.56 = bf16[256,1024]{1,0:T(8,128)(2,1)} custom-call(bf16[4,4096]{1,0:T(4,128)(2,1)S(1)} %collective-permute-done.refs_0_, bf16[256,1024]{1,0:T(8,128)(2,1)S(1)} %reshape.21.refs_1_, bf16[1024,512]{1,0:T(8,128)(2,1)S(1)} %bitcast.14, bf16[1024,512]{1,0:T(8,128)(2,1)S(1)} %bitcast.16), custom_call_target="tpu_custom_call" | custom-call | flops 536870912 | bytes 2097152 | tf_op jit(solution)/shard_map/pallas_call | solution.py:53
  43.0 3.5 %all-to-all-start.1 = ((bf16[4,64,1024]{2,1,0:T(8,128)(2,1)}), bf16[4,64,1024]{2,1,0:T(8,128)(2,1)S(1)}, u32[]{:S(2)}, u32[]{:S(2)}) async-start(bf16[4,64,1024]{2,1,0:T(8,128)(2,1)} %bitcast.3), calls=%async_computation.1 | async-start | bytes 1048576 | tf_op jit(solution)/shard_map/all_to_all | solution.py:23
  46.4 3.3 %collective-permute-start.1 = (bf16[256,1024]{1,0:T(8,128)(2,1)S(1)}, bf16[256,1024]{1,0:T(8,128)(2,1)}, u32[]{:S(2)}, u32[]{:S(2)}) collective-permute-start(bf16[256,1024]{1,0:T(8,128)(2,1)S(1)} %reshape.21.refs_1_), channel_id=1, source_target_pairs={{0,64},{1,65},{2,66},{3,67},{4,68},{5,69},{6,70},{7,71},{8,72},{9,... | collective-permute-start | bytes 1572872 | tf_op jit(solution)/shard_map/ppermute | solution.py:28
  49.8 7.8 %all-to-all-done.1.refs_0_ = bf16[4,64,1024]{2,1,0:T(8,128)(2,1)S(1)} async-done(((bf16[4,64,1024]{2,1,0:T(8,128)(2,1)}), bf16[4,64,1024]{2,1,0:T(8,128)(2,1)S(1)}, u32[]{:S(2)}, u32[]{:S(2)}) %all-to-all-start.1) | async-done | bytes 524320 | tf_op jit(solution)/shard_map/all_to_all | solution.py:23
  57.6 0.1 shard_map.57.refs_1_
  57.7 1.1 collective-permute-done.1.refs_0_
  58.8 1.9 %shard_map.58 = bf16[256,1536]{1,0:T(8,128)(2,1)S(1)} custom-call(bf16[256,1024]{1,0:T(8,128)(2,1)} %collective-permute-done.1.refs_0_, bf16[64,512]{1,0:T(8,128)(2,1)S(1)} %shard_map.57.refs_1_, bf16[1024,512]{1,0:T(8,128)(2,1)S(1)} %bitcast.15, bf16[1024,512]{1,0:T(8,128)(2,1)S(1)} %bitcast.17), custom_call_target="tpu_custom_call" | custom-call | flops 536870912 | bytes 2097152 | tf_op jit(solution)/shard_map/pallas_call | solution.py:53
  60.7 0.0 copy-start.2
  60.7 22.4 %all_to_all.25.refs_0_ = bf16[4,64,1536]{2,1,0:T(8,128)(2,1)S(1)} all-to-all(bf16[4,64,1536]{2,1,0:T(8,128)(2,1)S(1)} %bitcast.20), channel_id=1, replica_groups={{0,1,2,3},{4,5,6,7},{8,9,10,11},{12,13,14,15},{16,17,18,19},{20,21,22,2..., dimensions={0} | all-to-all | bytes 1572864 | tf_op jit(solution)/shard_map/all_to_all | solution.py:23
  83.1 0.0 copy-done.2
  83.1 0.5 shard_map.59
  83.6 3.3 %collective-permute-start.2 = (bf16[256,1024]{1,0:T(8,128)(2,1)S(1)}, bf16[256,1024]{1,0:T(8,128)(2,1)S(1)}, u32[]{:S(2)}, u32[]{:S(2)}) collective-permute-start(bf16[256,1024]{1,0:T(8,128)(2,1)S(1)} %get-tuple-element.8), channel_id=1, source_target_pairs={{0,64},{1,65},{2,66},{3,67},{4,68},{5,69},{6,70},{7,71},{8,72},{9,... | collective-permute-start | bytes 1572872 | tf_op jit(solution)/shard_map/ppermute | solution.py:28
  86.9 8.5 %all_to_all.26 = bf16[4,64,512]{2,1,0:T(8,128)(2,1)S(1)} all-to-all(bf16[4,64,512]{2,1,0:T(8,128)(2,1)S(1)} %get-tuple-element.7), channel_id=1, replica_groups={{0,1,2,3},{4,5,6,7},{8,9,10,11},{12,13,14,15},{16,17,18,19},{20,21,22,2..., dimensions={0} | all-to-all | bytes 524288 | tf_op jit(solution)/shard_map/all_to_all | solution.py:23
  95.4 0.7 collective-permute-done.2.refs_2_
  96.1 0.4 shard_map.60
  96.6 0.2 reshape.25
  96.8 25.9 %all_to_all.27 = bf16[64,4,1024]{2,1,0:T(4,128)(2,1)S(1)} all-to-all(bf16[64,4,1024]{2,1,0:T(4,128)(2,1)S(1)} %reshape.25), channel_id=1, replica_groups={{0,21,42,63,12,33,54,11,24,45,2,23,36,57,14,35,48,5,26,47,60,17,38,59,8..., dimensions={0} | all-to-all | bytes 1048576 | tf_op jit(solution)/shard_map/all_to_all | solution.py:23
  122.6 0.2 convert_reduce_fusion
  122.9 10.5 %collective-permute-start.3 = (bf16[1,4,4096]{2,1,0:T(4,128)(2,1)S(1)}, bf16[1,4,4096]{2,1,0:T(4,128)(2,1)S(1)}, u32[]{:S(2)}, u32[]{:S(2)}) collective-permute-start(bf16[1,4,4096]{2,1,0:T(4,128)(2,1)S(1)} %fusion), channel_id=1, source_target_pairs={{0,192},{1,193},{2,194},{3,195},{4,196},{5,197},{6,198},{7,199},{8... | collective-permute-start | bytes 98312 | tf_op jit(solution)/shard_map/ppermute | solution.py:38
  133.4 1.0 collective-permute-done.3
  134.4 0.6 copy.7
  (2 shorter events, 0.0 us)
Async XLA Ops:
  0.0 25.2 %copy-start.3 = (bf16[1,4,4096]{2,1,0:T(4,128)(2,1)S(1)}, bf16[1,4,4096]{2,1,0:T(4,128)(2,1)}, u32[]{:S(2)}) copy-start(bf16[1,4,4096]{2,1,0:T(4,128)(2,1)} %refs_0_.1) | copy-start | bytes 98308
  1.8 39.6 %copy-start = (bf16[1,1,1024,512]{3,2,1,0:T(8,128)(2,1)S(1)}, bf16[1,1,1024,512]{3,2,1,0:T(8,128)(2,1)}, u32[]{:S(2)}) copy-start(bf16[1,1,1024,512]{3,2,1,0:T(8,128)(2,1)} %param.7) | copy-start | bytes 3145732
  1.8 39.6 %copy-start.1 = (bf16[1,1,1024,512]{3,2,1,0:T(8,128)(2,1)S(1)}, bf16[1,1,1024,512]{3,2,1,0:T(8,128)(2,1)}, u32[]{:S(2)}) copy-start(bf16[1,1,1024,512]{3,2,1,0:T(8,128)(2,1)} %param.8) | copy-start | bytes 3145732
  1.8 39.5 %all-to-all-start = ((bf16[64,4,1024]{2,1,0:T(4,128)(2,1)}), bf16[64,4,1024]{2,1,0:T(4,128)(2,1)S(1)}, u32[]{:S(2)}, u32[]{:S(2)}) async-start(bf16[64,4,1024]{2,1,0:T(4,128)(2,1)} %shard_map.55), calls=%async_computation | async-start | bytes 1048576 | tf_op jit(solution)/shard_map/all_to_all | solution.py:23
  25.2 16.3 %collective-permute-start = (bf16[4,4096]{1,0:T(4,128)(2,1)S(1)}, bf16[4,4096]{1,0:T(4,128)(2,1)S(1)}, u32[]{:S(2)}, u32[]{:S(2)}) collective-permute-start(bf16[4,4096]{1,0:T(4,128)(2,1)S(1)} %bitcast.24), channel_id=1, source_target_pairs={{0,64},{1,65},{2,66},{3,67},{4,68},{5,69},{6,70},{7,71},{8,72},{9,... | collective-permute-start | bytes 98312 | tf_op jit(solution)/shard_map/ppermute | solution.py:28
  43.0 14.6 %all-to-all-start.1 = ((bf16[4,64,1024]{2,1,0:T(8,128)(2,1)}), bf16[4,64,1024]{2,1,0:T(8,128)(2,1)S(1)}, u32[]{:S(2)}, u32[]{:S(2)}) async-start(bf16[4,64,1024]{2,1,0:T(8,128)(2,1)} %bitcast.3), calls=%async_computation.1 | async-start | bytes 1048576 | tf_op jit(solution)/shard_map/all_to_all | solution.py:23
  46.4 12.3 %collective-permute-start.1 = (bf16[256,1024]{1,0:T(8,128)(2,1)S(1)}, bf16[256,1024]{1,0:T(8,128)(2,1)}, u32[]{:S(2)}, u32[]{:S(2)}) collective-permute-start(bf16[256,1024]{1,0:T(8,128)(2,1)S(1)} %reshape.21.refs_1_), channel_id=1, source_target_pairs={{0,64},{1,65},{2,66},{3,67},{4,68},{5,69},{6,70},{7,71},{8,72},{9,... | collective-permute-start | bytes 1572872 | tf_op jit(solution)/shard_map/ppermute | solution.py:28
  60.7 22.4 %copy-start.2 = (bf16[1,1,512,1024]{3,2,1,0:T(8,128)(2,1)S(1)}, bf16[1,1,512,1024]{3,2,1,0:T(8,128)(2,1)}, u32[]{:S(2)}) copy-start(bf16[1,1,512,1024]{3,2,1,0:T(8,128)(2,1)} %param.9) | copy-start | bytes 3145732
  83.6 12.5 %collective-permute-start.2 = (bf16[256,1024]{1,0:T(8,128)(2,1)S(1)}, bf16[256,1024]{1,0:T(8,128)(2,1)S(1)}, u32[]{:S(2)}, u32[]{:S(2)}) collective-permute-start(bf16[256,1024]{1,0:T(8,128)(2,1)S(1)} %get-tuple-element.8), channel_id=1, source_target_pairs={{0,64},{1,65},{2,66},{3,67},{4,68},{5,69},{6,70},{7,71},{8,72},{9,... | collective-permute-start | bytes 1572872 | tf_op jit(solution)/shard_map/ppermute | solution.py:28
  122.9 11.5 %collective-permute-start.3 = (bf16[1,4,4096]{2,1,0:T(4,128)(2,1)S(1)}, bf16[1,4,4096]{2,1,0:T(4,128)(2,1)S(1)}, u32[]{:S(2)}, u32[]{:S(2)}) collective-permute-start(bf16[1,4,4096]{2,1,0:T(4,128)(2,1)S(1)} %fusion), channel_id=1, source_target_pairs={{0,192},{1,193},{2,194},{3,195},{4,196},{5,197},{6,198},{7,199},{8... | collective-permute-start | bytes 98312 | tf_op jit(solution)/shard_map/ppermute | solution.py:38

commit v10 on v8

--- a/solution.py
+++ b/solution.py
@@ -13,10 +13,13 @@
     return [list(range(low, low + size)) for low in range(0, count, size)]
 
 
-def scattered(run, size):
-    count = run // size
-    places = [(3 * k + 5 * a) % count * size + a for k in range(count) for a in range(size)]
-    return [[low + place for place in places] for low in range(0, lax.axis_size("tensor"), run)]
+def strided(run, size):
+    count = lax.axis_size("tensor")
+    return [
+        list(range(low + place, low + run, size))
+        for low in range(0, count, run)
+        for place in range(size)
+    ]
 
 
 def traded(blocks, groups):
@@ -123,12 +126,11 @@
     depth, width = gate_local.shape
     groups_a = features // depth
     near = lax.axis_size("tensor") // 2
-    groups_b = near // groups_a
     total = near * tokens
     piece = total // groups_a
     cost = 2 * total * depth * width
     weight = 2 * depth * width
-    quads, half = runs(groups_a), scattered(near, groups_a)
+    quads, line = runs(groups_a), 2 * groups_a
 
     mirror_acts = flipped(acts[0], near)
     (sent,) = local(
@@ -146,7 +148,7 @@
         ],
         fetches=True,
     )
-    near_columns = traded(sent, half).reshape(total, depth)
+    near_columns = traded(sent, runs(near)).reshape(total, depth)
     far_columns = flipped(near_columns, near)
 
     (sums,) = local(
@@ -184,8 +186,9 @@
     mirror_rows = flipped(near_rows, near)
     hidden = traded(spread, quads).reshape(total, width)
     (rows,) = local(far_down, [(total, depth)], cost, weight, hidden, down_local, mirror_rows)
-    parts = traded(rows.reshape(near, tokens, depth), half)
-    parts = parts.reshape(groups_b, groups_a, tokens, depth).astype(f32)
+    parts = traded(rows.reshape(near // line, line * tokens, depth), strided(near, line))
+    rows = jnp.sum(parts.astype(f32), axis=0).astype(bf16).reshape(line, tokens, depth)
+    parts = traded(rows, runs(line)).reshape(2, groups_a, tokens, depth).astype(f32)
     summed = jnp.transpose(jnp.sum(parts, axis=0), (1, 0, 2)).reshape(tokens, features)
     block = (mirror_acts.astype(f32) + summed).astype(bf16)
     return passed_along(block[None], near)

time: 135 us -> 143 us (1.059)
  blocking collectives: 56.8 us -> 62.7 us
  starting transfers between devices: 46.9 us -> 49.2 us
    all_to_all x3 -> x4, blocking collectives: 56.8 us -> 62.7 us  [traded(): lax.all_to_all(blocks, 'tensor', 0, 0, axis_index_groups=groups, tiled=True)]
where the time goes in v10:
time: 143 us; the launch traced here: 142 us
  blocking collectives  62.7 us (44%)
  starting transfers between devices  49.2 us (34%)
  waiting for transfers between devices  23.4 us (16%)
  Pallas kernels  6.08 us (4%)
    all_to_all x4, blocking collectives, traded(): lax.all_to_all(blocks, 'tensor', 0, 0, axis_index_groups=groups, tiled=True)  62.7 us
    all_to_all x2, starting transfers between devices, traded(): lax.all_to_all(blocks, 'tensor', 0, 0, axis_index_groups=groups, tiled=True)  27.6 us
    all_to_all x2, waiting for transfers between devices, traded(): lax.all_to_all(blocks, 'tensor', 0, 0, axis_index_groups=groups, tiled=True)  20.7 us
    ppermute x1, starting transfers between devices, passed_along(): return lax.ppermute(value, ('section', 'tensor'), route)  11.6 us
    ppermute x3, starting transfers between devices, flipped(): return lax.ppermute(values, 'tensor', [(i, i ^ mask) for i in range(count)])  9.94 us
    pallas_call x6, Pallas kernels, local(): pl.pallas_call(kernel, out_shape=[jax.ShapeDtypeStruct(shape, bf16) for s...  6.08 us
  transfers between devices with their start and end apart: 6, of which 5 were waited for; matrix products, arithmetic and copies ran while one was open for 0% of the time, Pallas kernels for 0%

profile of v10, /device:TPU:1, one launch (start us, length us, event | category | flops | bytes accessed | tf_op | source)
XLA Modules:
  0.0 142.4 jit_solution(3877826393569993890)
XLA Ops:
  0.0 1.8 %shard_map.55 = bf16[64,4,1024]{2,1,0:T(4,128)(2,1)} custom-call(bf16[1,4,4096]{2,1,0:T(4,128)(2,1)} %refs_0_.1, f32[1,4096]{1,0:T(1,128)} %refs_1_.1), custom_call_target="tpu_custom_call" | custom-call | bytes 524288 | tf_op jit(solution)/shard_map/pallas_call | solution.py:55
  1.8 0.0 copy-start
  1.8 0.0 copy-start.1
  1.8 23.3 %all-to-all-start = ((bf16[64,4,1024]{2,1,0:T(4,128)(2,1)}), bf16[64,4,1024]{2,1,0:T(4,128)(2,1)S(1)}, u32[]{:S(2)}, u32[]{:S(2)}) async-start(bf16[64,4,1024]{2,1,0:T(4,128)(2,1)} %shard_map.55), calls=%async_computation | async-start | bytes 1048576 | tf_op jit(solution)/shard_map/all_to_all | solution.py:26
  25.2 0.0 copy-done.3
  25.2 3.3 %collective-permute-start = (bf16[4,4096]{1,0:T(4,128)(2,1)S(1)}, bf16[4,4096]{1,0:T(4,128)(2,1)S(1)}, u32[]{:S(2)}, u32[]{:S(2)}) collective-permute-start(bf16[4,4096]{1,0:T(4,128)(2,1)S(1)} %bitcast.26), channel_id=1, source_target_pairs={{0,64},{1,65},{2,66},{3,67},{4,68},{5,69},{6,70},{7,71},{8,72},{9,... | collective-permute-start | bytes 98312 | tf_op jit(solution)/shard_map/ppermute | solution.py:31
  28.5 13.0 %all-to-all-done = bf16[64,4,1024]{2,1,0:T(4,128)(2,1)S(1)} async-done(((bf16[64,4,1024]{2,1,0:T(4,128)(2,1)}), bf16[64,4,1024]{2,1,0:T(4,128)(2,1)S(1)}, u32[]{:S(2)}, u32[]{:S(2)}) %all-to-all-start) | async-done | bytes 524320 | tf_op jit(solution)/shard_map/all_to_all | solution.py:26
  41.5 0.1 reshape.24.refs_1_
  41.6 0.0 collective-permute-done.refs_0_
  41.6 0.0 copy-done
  41.7 0.0 copy-done.1
  41.7 1.5 %shard_map.56 = bf16[256,1024]{1,0:T(8,128)(2,1)} custom-call(bf16[4,4096]{1,0:T(4,128)(2,1)S(1)} %collective-permute-done.refs_0_, bf16[256,1024]{1,0:T(8,128)(2,1)S(1)} %reshape.24.refs_1_, bf16[1024,512]{1,0:T(8,128)(2,1)S(1)} %bitcast.15, bf16[1024,512]{1,0:T(8,128)(2,1)S(1)} %bitcast.17), custom_call_target="tpu_custom_call" | custom-call | flops 536870912 | bytes 2097152 | tf_op jit(solution)/shard_map/pallas_call | solution.py:55
  43.2 4.3 %all-to-all-start.1 = ((bf16[4,64,1024]{2,1,0:T(8,128)(2,1)}), bf16[4,64,1024]{2,1,0:T(8,128)(2,1)S(1)}, u32[]{:S(2)}, u32[]{:S(2)}) async-start(bf16[4,64,1024]{2,1,0:T(8,128)(2,1)} %bitcast.3), calls=%async_computation.1 | async-start | bytes 1048576 | tf_op jit(solution)/shard_map/all_to_all | solution.py:26
  47.5 3.3 %collective-permute-start.1 = (bf16[256,1024]{1,0:T(8,128)(2,1)S(1)}, bf16[256,1024]{1,0:T(8,128)(2,1)}, u32[]{:S(2)}, u32[]{:S(2)}) collective-permute-start(bf16[256,1024]{1,0:T(8,128)(2,1)S(1)} %reshape.24.refs_1_), channel_id=1, source_target_pairs={{0,64},{1,65},{2,66},{3,67},{4,68},{5,69},{6,70},{7,71},{8,72},{9,... | collective-permute-start | bytes 1572872 | tf_op jit(solution)/shard_map/ppermute | solution.py:31
  50.8 7.7 %all-to-all-done.1.refs_0_ = bf16[4,64,1024]{2,1,0:T(8,128)(2,1)S(1)} async-done(((bf16[4,64,1024]{2,1,0:T(8,128)(2,1)}), bf16[4,64,1024]{2,1,0:T(8,128)(2,1)S(1)}, u32[]{:S(2)}, u32[]{:S(2)}) %all-to-all-start.1) | async-done | bytes 524320 | tf_op jit(solution)/shard_map/all_to_all | solution.py:26
  58.5 0.1 shard_map.57.refs_1_
  58.6 1.1 collective-permute-done.1.refs_0_
  59.7 1.8 %shard_map.58 = bf16[256,1536]{1,0:T(8,128)(2,1)S(1)} custom-call(bf16[256,1024]{1,0:T(8,128)(2,1)} %collective-permute-done.1.refs_0_, bf16[64,512]{1,0:T(8,128)(2,1)S(1)} %shard_map.57.refs_1_, bf16[1024,512]{1,0:T(8,128)(2,1)S(1)} %bitcast.16, bf16[1024,512]{1,0:T(8,128)(2,1)S(1)} %bitcast.18), custom_call_target="tpu_custom_call" | custom-call | flops 536870912 | bytes 2097152 | tf_op jit(solution)/shard_map/pallas_call | solution.py:55
  61.5 0.0 copy-start.2
  61.5 22.4 %all_to_all.30.refs_0_ = bf16[4,64,1536]{2,1,0:T(8,128)(2,1)S(1)} all-to-all(bf16[4,64,1536]{2,1,0:T(8,128)(2,1)S(1)} %bitcast.21), channel_id=1, replica_groups={{0,1,2,3},{4,5,6,7},{8,9,10,11},{12,13,14,15},{16,17,18,19},{20,21,22,2..., dimensions={0} | all-to-all | bytes 1572864 | tf_op jit(solution)/shard_map/all_to_all | solution.py:26
  83.9 0.0 copy-done.2
  83.9 0.5 shard_map.59
  84.4 3.3 %collective-permute-start.2 = (bf16[256,1024]{1,0:T(8,128)(2,1)S(1)}, bf16[256,1024]{1,0:T(8,128)(2,1)S(1)}, u32[]{:S(2)}, u32[]{:S(2)}) collective-permute-start(bf16[256,1024]{1,0:T(8,128)(2,1)S(1)} %get-tuple-element.8), channel_id=1, source_target_pairs={{0,64},{1,65},{2,66},{3,67},{4,68},{5,69},{6,70},{7,71},{8,72},{9,... | collective-permute-start | bytes 1572872 | tf_op jit(solution)/shard_map/ppermute | solution.py:31
  87.7 8.5 %all_to_all.31 = bf16[4,64,512]{2,1,0:T(8,128)(2,1)S(1)} all-to-all(bf16[4,64,512]{2,1,0:T(8,128)(2,1)S(1)} %get-tuple-element.7), channel_id=1, replica_groups={{0,1,2,3},{4,5,6,7},{8,9,10,11},{12,13,14,15},{16,17,18,19},{20,21,22,2..., dimensions={0} | all-to-all | bytes 524288 | tf_op jit(solution)/shard_map/all_to_all | solution.py:26
  96.3 0.6 collective-permute-done.2.refs_2_
  96.9 0.4 shard_map.60
  97.4 21.1 %all_to_all.32 = bf16[8,32,1024]{2,1,0:T(8,128)(2,1)S(1)} all-to-all(bf16[8,32,1024]{2,1,0:T(8,128)(2,1)S(1)} %bitcast.22), channel_id=1, replica_groups={{0,8,16,24,32,40,48,56},{1,9,17,25,33,41,49,57},{2,10,18,26,34,42,50,58..., dimensions={0} | all-to-all | bytes 1048576 | tf_op jit(solution)/shard_map/all_to_all | solution.py:26
  118.4 0.1 reduce_sum.21
  118.6 10.6 %all_to_all.33 = bf16[8,4,1024]{2,1,0:T(4,128)(2,1)S(1)} all-to-all(bf16[8,4,1024]{2,1,0:T(4,128)(2,1)S(1)} %reshape.29), channel_id=1, replica_groups={{0,1,2,3,4,5,6,7},{8,9,10,11,12,13,14,15},{16,17,18,19,20,21,22,23},{24..., dimensions={0} | all-to-all | bytes 131072 | tf_op jit(solution)/shard_map/all_to_all | solution.py:26
  129.2 11.6 %collective-permute-start.3 = (bf16[1,4,4096]{2,1,0:T(4,128)(2,1)S(1)}, bf16[1,4,4096]{2,1,0:T(4,128)(2,1)S(1)}, u32[]{:S(2)}, u32[]{:S(2)}) collective-permute-start(bf16[1,4,4096]{2,1,0:T(4,128)(2,1)S(1)} %fusion), channel_id=1, source_target_pairs={{0,192},{1,193},{2,194},{3,195},{4,196},{5,197},{6,198},{7,199},{8... | collective-permute-start | bytes 98312 | tf_op jit(solution)/shard_map/ppermute | solution.py:41
  140.8 1.0 collective-permute-done.3
  141.8 0.6 copy.7
  (4 shorter events, 0.1 us)
Async XLA Ops:
  0.0 25.2 %copy-start.3 = (bf16[1,4,4096]{2,1,0:T(4,128)(2,1)S(1)}, bf16[1,4,4096]{2,1,0:T(4,128)(2,1)}, u32[]{:S(2)}) copy-start(bf16[1,4,4096]{2,1,0:T(4,128)(2,1)} %refs_0_.1) | copy-start | bytes 98308
  1.8 39.8 %copy-start = (bf16[1,1,1024,512]{3,2,1,0:T(8,128)(2,1)S(1)}, bf16[1,1,1024,512]{3,2,1,0:T(8,128)(2,1)}, u32[]{:S(2)}) copy-start(bf16[1,1,1024,512]{3,2,1,0:T(8,128)(2,1)} %param.7) | copy-start | bytes 3145732
  1.8 39.8 %copy-start.1 = (bf16[1,1,1024,512]{3,2,1,0:T(8,128)(2,1)S(1)}, bf16[1,1,1024,512]{3,2,1,0:T(8,128)(2,1)}, u32[]{:S(2)}) copy-start(bf16[1,1,1024,512]{3,2,1,0:T(8,128)(2,1)} %param.8) | copy-start | bytes 3145732
  1.8 39.7 %all-to-all-start = ((bf16[64,4,1024]{2,1,0:T(4,128)(2,1)}), bf16[64,4,1024]{2,1,0:T(4,128)(2,1)S(1)}, u32[]{:S(2)}, u32[]{:S(2)}) async-start(bf16[64,4,1024]{2,1,0:T(4,128)(2,1)} %shard_map.55), calls=%async_computation | async-start | bytes 1048576 | tf_op jit(solution)/shard_map/all_to_all | solution.py:26
  25.2 16.5 %collective-permute-start = (bf16[4,4096]{1,0:T(4,128)(2,1)S(1)}, bf16[4,4096]{1,0:T(4,128)(2,1)S(1)}, u32[]{:S(2)}, u32[]{:S(2)}) collective-permute-start(bf16[4,4096]{1,0:T(4,128)(2,1)S(1)} %bitcast.26), channel_id=1, source_target_pairs={{0,64},{1,65},{2,66},{3,67},{4,68},{5,69},{6,70},{7,71},{8,72},{9,... | collective-permute-start | bytes 98312 | tf_op jit(solution)/shard_map/ppermute | solution.py:31
  43.2 15.4 %all-to-all-start.1 = ((bf16[4,64,1024]{2,1,0:T(8,128)(2,1)}), bf16[4,64,1024]{2,1,0:T(8,128)(2,1)S(1)}, u32[]{:S(2)}, u32[]{:S(2)}) async-start(bf16[4,64,1024]{2,1,0:T(8,128)(2,1)} %bitcast.3), calls=%async_computation.1 | async-start | bytes 1048576 | tf_op jit(solution)/shard_map/all_to_all | solution.py:26
  47.5 12.2 %collective-permute-start.1 = (bf16[256,1024]{1,0:T(8,128)(2,1)S(1)}, bf16[256,1024]{1,0:T(8,128)(2,1)}, u32[]{:S(2)}, u32[]{:S(2)}) collective-permute-start(bf16[256,1024]{1,0:T(8,128)(2,1)S(1)} %reshape.24.refs_1_), channel_id=1, source_target_pairs={{0,64},{1,65},{2,66},{3,67},{4,68},{5,69},{6,70},{7,71},{8,72},{9,... | collective-permute-start | bytes 1572872 | tf_op jit(solution)/shard_map/ppermute | solution.py:31
  61.5 22.5 %copy-start.2 = (bf16[1,1,512,1024]{3,2,1,0:T(8,128)(2,1)S(1)}, bf16[1,1,512,1024]{3,2,1,0:T(8,128)(2,1)}, u32[]{:S(2)}) copy-start(bf16[1,1,512,1024]{3,2,1,0:T(8,128)(2,1)} %param.9) | copy-start | bytes 3145732
  84.4 12.5 %collective-permute-start.2 = (bf16[256,1024]{1,0:T(8,128)(2,1)S(1)}, bf16[256,1024]{1,0:T(8,128)(2,1)S(1)}, u32[]{:S(2)}, u32[]{:S(2)}) collective-permute-start(bf16[256,1024]{1,0:T(8,128)(2,1)S(1)} %get-tuple-element.8), channel_id=1, source_target_pairs={{0,64},{1,65},{2,66},{3,67},{4,68},{5,69},{6,70},{7,71},{8,72},{9,... | collective-permute-start | bytes 1572872 | tf_op jit(solution)/shard_map/ppermute | solution.py:31
  129.2 12.6 %collective-permute-start.3 = (bf16[1,4,4096]{2,1,0:T(4,128)(2,1)S(1)}, bf16[1,4,4096]{2,1,0:T(4,128)(2,1)S(1)}, u32[]{:S(2)}, u32[]{:S(2)}) collective-permute-start(bf16[1,4,4096]{2,1,0:T(4,128)(2,1)S(1)} %fusion), channel_id=1, source_target_pairs={{0,192},{1,193},{2,194},{3,195},{4,196},{5,197},{6,198},{7,199},{8... | collective-permute-start | bytes 98312 | tf_op jit(solution)/shard_map/ppermute | solution.py:41
